TPU v7x, 32 devices: a whole 2x2x4 slice. The times are simulated.
32 devices in a mesh: dp: 8 (over y, x, core), tensor: 4 (over z).
Axes of the slice: x: 2, y: 2, z: 4, core: 2. Of those that a mesh axis runs over, the one named last changes fastest.
Arguments:
- layer_input: bfloat16 [16384, 1024], P(('dp', 'tensor')), may hold values from -6 to 6
- segments: int32 [16384], P('dp'), may hold values from 0 to 4, as said below
- norm_gain: float32 [1024], replicated, may hold values from 0.1 to 1.9
- w_query: bfloat16 [1024, 1024], P('dp', 'tensor'), may hold values from -0.1875 to 0.1875
- w_key: bfloat16 [1024, 1024], P('dp', 'tensor'), may hold values from -0.1875 to 0.1875
- w_value: bfloat16 [1024, 2048], P('dp', 'tensor'), may hold values from -0.1875 to 0.1875
- w_outgate: bfloat16 [1024, 2048], P('dp', 'tensor'), may hold values from -0.1875 to 0.1875
- w_beta: bfloat16 [1024, 8], P('dp', 'tensor'), may hold values from -0.1875 to 0.1875
- w_decay: bfloat16 [1024, 8], P('dp', 'tensor'), may hold values from -0.1875 to 0.1875
- conv_query: float32 [4, 1024], replicated, may hold values from -3 to 3
- conv_key: float32 [4, 1024], replicated, may hold values from -3 to 3
- conv_value: float32 [4, 2048], replicated, may hold values from -3 to 3
- decay_log: float32 [8], replicated, may hold values from -7 to 0
- decay_bias: float32 [8], replicated, may hold values from -3 to 3
- out_gain: float32 [256], replicated, may hold values from 0.1 to 1.9
- w_out: bfloat16 [2048, 1024], P('tensor', 'dp'), may hold values from -0.125 to 0.125
- ffn_gain: float32 [1024], replicated, may hold values from 0.1 to 1.9
- w_gate: bfloat16 [1024, 2816], P('dp', 'tensor'), may hold values from -0.1875 to 0.1875
- w_up: bfloat16 [1024, 2816], P('dp', 'tensor'), may hold values from -0.1875 to 0.1875
- w_down: bfloat16 [2816, 1024], P('tensor', 'dp'), may hold values from -0.109375 to 0.109375
- cotangent: bfloat16 [16384, 1024], P(('dp', 'tensor')), may hold values from -6 to 6
Outputs:
- layer_output: bfloat16 [16384, 1024], P(('dp', 'tensor'))
- grad_input: float32 [16384, 1024], P(('dp', 'tensor'))
- grad_norm_gain: float32 [1024], replicated
- grad_w_query: float32 [1024, 1024], P('dp', 'tensor')
- grad_w_key: float32 [1024, 1024], P('dp', 'tensor')
- grad_w_value: float32 [1024, 2048], P('dp', 'tensor')
- grad_w_outgate: float32 [1024, 2048], P('dp', 'tensor')
- grad_w_beta: float32 [1024, 8], P('dp', 'tensor')
- grad_w_decay: float32 [1024, 8], P('dp', 'tensor')
- grad_conv_query: float32 [4, 1024], replicated
- grad_conv_key: float32 [4, 1024], replicated
- grad_conv_value: float32 [4, 2048], replicated
- grad_decay_log: float32 [8], replicated
- grad_decay_bias: float32 [8], replicated
- grad_out_gain: float32 [256], replicated
- grad_w_out: float32 [2048, 1024], P('tensor', 'dp')
- grad_ffn_gain: float32 [1024], replicated
- grad_w_gate: float32 [1024, 2816], P('dp', 'tensor')
- grad_w_up: float32 [1024, 2816], P('dp', 'tensor')
- grad_w_down: float32 [2816, 1024], P('tensor', 'dp')
Inputs may be any that keep to these rules, and one draw needn't show every extreme that they name: `segments`: within each group of 2048 consecutive tokens the segment numbers never fall; tokens with equal numbers form one packed sequence.
All inputs are finite; a program needn't handle non-finite values.
Results may differ from a plain program's by a relative error of at most 0.014.
The roundings to bfloat16 on the way count: a program that leaves them out, or rounds other values in their place, can miss the bound.
Values may be sent and summed in bfloat16 or wider, within the bound.
No kernel may reach another device: no remote copies, remote signals or barrier semaphores. Data moves between devices by JAX's collectives and lax.ppermute only.
A program may use at most 256 MiB of HBM per device.

v0:
```python
from functools import partial

import jax
import jax.numpy as jnp
from jax import lax
from jax.sharding import PartitionSpec as P

SPAN = 128


highest_precision = lax.Precision.HIGHEST


def exact_einsum(form, left, right):
    return jnp.einsum(
        form, left, right, precision=highest_precision, preferred_element_type=jnp.float32
    )


def rms_norm(values, gain):
    return values * lax.rsqrt(jnp.mean(values * values, axis=-1, keepdims=True) + 1e-06) * gain


def unit_rows(values):
    return values * lax.rsqrt(jnp.sum(values * values, axis=-1, keepdims=True) + 1e-06)


def shift_masks(segment_ids, width):
    masks_list = []
    for lag_count in range(1, width):
        earlier = jnp.concatenate([jnp.full((lag_count,), -1, jnp.int32), segment_ids[:-lag_count]])
        masks_list.append((segment_ids == earlier).astype(jnp.float32))
    return masks_list


def short_conv(values, weight, same_masks):
    total = values * weight[0]
    for lag_count in range(1, weight.shape[0]):
        shifted = jnp.pad(values, ((lag_count, 0), (0, 0)))[: values.shape[0]]
        total = total + shifted * same_masks[lag_count - 1][:, None] * weight[lag_count]
    return total


def mixer_inputs(
    proj_query,
    proj_key,
    proj_value,
    proj_beta,
    proj_decay,
    conv_query,
    conv_key,
    conv_value,
    decay_log,
    decay_bias,
    same_masks,
):
    length = proj_query.shape[0]
    heads_here = proj_beta.shape[1]
    query_rows = jax.nn.silu(short_conv(proj_query, conv_query, same_masks)).reshape(
        length, heads_here, -1
    )
    key_rows = jax.nn.silu(short_conv(proj_key, conv_key, same_masks)).reshape(
        length, heads_here, -1
    )
    value_rows = jax.nn.silu(short_conv(proj_value, conv_value, same_masks)).reshape(
        length, heads_here, -1
    )
    query_rows = unit_rows(query_rows) * query_rows.shape[-1] ** (-0.5)
    key_rows = unit_rows(key_rows)
    beta_rows = jax.nn.sigmoid(proj_beta)
    decay_rows = -jnp.exp(decay_log) * jax.nn.softplus(proj_decay + decay_bias)
    return (query_rows, key_rows, value_rows, beta_rows, decay_rows)


def gated_norm(outputs, proj_gate, gain):
    length, heads_here, width_value = outputs.shape
    normed = outputs * lax.rsqrt(jnp.mean(outputs * outputs, axis=-1, keepdims=True) + 1e-06) * gain
    return (normed * jax.nn.silu(proj_gate.reshape(length, heads_here, width_value))).reshape(
        length, -1
    )


def span_delta(query_rows, key_rows, value_rows, beta_rows, decay_rows, segment_ids, block_rows):
    length, heads_here, width_key = key_rows.shape
    width_value = value_rows.shape[-1]
    blocks = length // block_rows
    query_blocks = query_rows.reshape(blocks, block_rows, heads_here, width_key).transpose(
        0, 2, 1, 3
    )
    key_blocks = key_rows.reshape(blocks, block_rows, heads_here, width_key).transpose(0, 2, 1, 3)
    value_blocks = value_rows.reshape(blocks, block_rows, heads_here, width_value).transpose(
        0, 2, 1, 3
    )
    beta_blocks = beta_rows.reshape(blocks, block_rows, heads_here).transpose(0, 2, 1)
    decay_blocks = decay_rows.reshape(blocks, block_rows, heads_here).transpose(0, 2, 1)
    segment_blocks = segment_ids.reshape(blocks, block_rows)
    before = jnp.concatenate([jnp.full((1,), -1, jnp.int32), segment_ids[:-1]]).reshape(
        blocks, block_rows
    )[:, 0]
    continuing = (segment_blocks == before[:, None]).astype(jnp.float32)
    places = jnp.arange(block_rows)
    same_segment = segment_blocks[:, :, None] == segment_blocks[:, None, :]
    lower_mask = ((places[:, None] >= places[None, :])[None] & same_segment)[:, None]
    strict_mask = (places[:, None] > places[None, :]).astype(jnp.float32)
    cumulative = jnp.cumsum(decay_blocks, axis=-1)
    gaps = cumulative[..., :, None] - cumulative[..., None, :]
    decay_matrix = jnp.where(lower_mask, jnp.exp(jnp.where(lower_mask, gaps, 0.0)), 0.0)
    key_products = exact_einsum("nhtd,nhjd->nhtj", key_blocks, key_blocks)
    system = (
        jnp.eye(block_rows, dtype=jnp.float32)
        + beta_blocks[..., :, None] * decay_matrix * key_products * strict_mask
    )
    growth = jnp.exp(cumulative) * continuing[:, None, :]
    right_sides = jnp.concatenate(
        [beta_blocks[..., None] * value_blocks, (beta_blocks * growth)[..., None] * key_blocks],
        axis=-1,
    )
    solved = jax.scipy.linalg.solve_triangular(system, right_sides, lower=True, unit_diagonal=True)
    value_solved = solved[..., :width_value]
    key_solved = solved[..., width_value:]
    scores = exact_einsum("nhtd,nhjd->nhtj", query_blocks, key_blocks) * decay_matrix
    query_grown = growth[..., None] * query_blocks
    same_last = (segment_blocks == segment_blocks[:, -1:]).astype(jnp.float32)
    tail_decay = jnp.exp(cumulative[..., -1:] - cumulative) * same_last[:, None, :]
    carry_scale = jnp.exp(cumulative[..., -1]) * continuing[:, -1][:, None]

    def block_step(carried, sliced):
        value_part, key_part, score_part, query_part, key_now, tail_part, scale_part = sliced
        fresh = value_part - exact_einsum("htd,hvd->htv", key_part, carried)
        emitted = exact_einsum("htd,hvd->htv", query_part, carried) + exact_einsum(
            "htj,hjv->htv", score_part, fresh
        )
        carried = scale_part[:, None, None] * carried + exact_einsum(
            "hjv,hjd->hvd", tail_part[..., None] * fresh, key_now
        )
        return (carried, emitted)

    initial = jnp.zeros((heads_here, width_value, width_key), jnp.float32)
    last_state, outputs = lax.scan(
        block_step,
        initial,
        (value_solved, key_solved, scores, query_grown, key_blocks, tail_decay, carry_scale),
    )
    return outputs.transpose(0, 2, 1, 3).reshape(length, heads_here, width_value)


def mixer_core(
    proj_query,
    proj_key,
    proj_value,
    proj_gate,
    proj_beta,
    proj_decay,
    conv_query,
    conv_key,
    conv_value,
    decay_log,
    decay_bias,
    out_gain,
    same_masks,
    segment_ids,
):
    query_rows, key_rows, value_rows, beta_rows, decay_rows = mixer_inputs(
        proj_query,
        proj_key,
        proj_value,
        proj_beta,
        proj_decay,
        conv_query,
        conv_key,
        conv_value,
        decay_log,
        decay_bias,
        same_masks,
    )
    outputs = span_delta(query_rows, key_rows, value_rows, beta_rows, decay_rows, segment_ids, SPAN)
    return gated_norm(outputs, proj_gate, out_gain)


def shards(
    layer_input,
    segments,
    norm_gain,
    w_query,
    w_key,
    w_value,
    w_outgate,
    w_beta,
    w_decay,
    conv_query,
    conv_key,
    conv_value,
    decay_log,
    decay_bias,
    out_gain,
    w_out,
    ffn_gain,
    w_gate,
    w_up,
    w_down,
    cotangent,
):
    tensor_rank = lax.axis_index("tensor")
    key_cols = w_query.shape[1]
    value_cols = w_value.shape[1]
    local_heads = w_beta.shape[1]
    gathered = (
        lax.all_gather(w_query, "dp", axis=0, tiled=True),
        lax.all_gather(w_key, "dp", axis=0, tiled=True),
        lax.all_gather(w_value, "dp", axis=0, tiled=True),
        lax.all_gather(w_outgate, "dp", axis=0, tiled=True),
        lax.all_gather(w_beta, "dp", axis=0, tiled=True),
        lax.all_gather(w_decay, "dp", axis=0, tiled=True),
        lax.all_gather(w_out, "dp", axis=1, tiled=True),
        lax.all_gather(w_gate, "dp", axis=0, tiled=True),
        lax.all_gather(w_up, "dp", axis=0, tiled=True),
        lax.all_gather(w_down, "dp", axis=1, tiled=True),
    )
    residual = layer_input.astype(jnp.float32)
    normed, first_back = jax.vjp(rms_norm, residual, norm_gain)
    mixer_rows = lax.all_gather(normed.astype(jnp.bfloat16), "tensor", axis=0, tiled=True)
    joined = jnp.concatenate(gathered[:6], axis=1)
    projected = jnp.dot(mixer_rows, joined, preferred_element_type=jnp.float32)
    offsets = [
        key_cols,
        2 * key_cols,
        2 * key_cols + value_cols,
        2 * key_cols + 2 * value_cols,
        2 * key_cols + 2 * value_cols + local_heads,
    ]
    pieces = jnp.split(projected, offsets, axis=1)
    local_small = (
        lax.dynamic_slice_in_dim(conv_query, tensor_rank * key_cols, key_cols, 1),
        lax.dynamic_slice_in_dim(conv_key, tensor_rank * key_cols, key_cols, 1),
        lax.dynamic_slice_in_dim(conv_value, tensor_rank * value_cols, value_cols, 1),
        lax.dynamic_slice_in_dim(decay_log, tensor_rank * local_heads, local_heads, 0),
        lax.dynamic_slice_in_dim(decay_bias, tensor_rank * local_heads, local_heads, 0),
        out_gain,
    )
    same_masks = shift_masks(segments, conv_query.shape[0])
    local_mixer = partial(mixer_core, same_masks=same_masks, segment_ids=segments)
    gated, mixer_back = jax.vjp(local_mixer, *pieces, *local_small)
    gated_low = gated.astype(jnp.bfloat16)
    attended = lax.psum_scatter(
        jnp.dot(gated_low, gathered[6], preferred_element_type=jnp.float32),
        "tensor",
        scatter_dimension=0,
        tiled=True,
    )
    middle = residual + attended
    second, second_back = jax.vjp(rms_norm, middle, ffn_gain)
    ffn_inputs = lax.all_gather(second.astype(jnp.bfloat16), "tensor", axis=0, tiled=True)
    gate_rows = jnp.dot(ffn_inputs, gathered[7], preferred_element_type=jnp.float32)
    up_rows = jnp.dot(ffn_inputs, gathered[8], preferred_element_type=jnp.float32)
    hidden = (jax.nn.silu(gate_rows) * up_rows).astype(jnp.bfloat16)
    ffn_rows = lax.psum_scatter(
        jnp.dot(hidden, gathered[9], preferred_element_type=jnp.float32).astype(jnp.bfloat16),
        "tensor",
        scatter_dimension=0,
        tiled=True,
    ).astype(jnp.float32)
    layer_output = (middle + ffn_rows).astype(jnp.bfloat16)
    cot_rows = lax.all_gather(cotangent, "tensor", axis=0, tiled=True)
    grad_down = jnp.einsum("lf,ld->fd", hidden, cot_rows, preferred_element_type=jnp.float32)
    grad_hidden = jnp.einsum("ld,fd->lf", cot_rows, gathered[9], preferred_element_type=jnp.float32)
    sigmoid_gate = jax.nn.sigmoid(gate_rows)
    grad_gate_rows = (
        grad_hidden * up_rows * sigmoid_gate * (1.0 + gate_rows * (1.0 - sigmoid_gate))
    ).astype(jnp.bfloat16)
    grad_up_rows = (grad_hidden * gate_rows * sigmoid_gate).astype(jnp.bfloat16)
    grad_gate = jnp.einsum(
        "ld,lf->df", ffn_inputs, grad_gate_rows, preferred_element_type=jnp.float32
    )
    grad_up = jnp.einsum("ld,lf->df", ffn_inputs, grad_up_rows, preferred_element_type=jnp.float32)
    back_second = jnp.einsum(
        "lf,df->ld", grad_gate_rows, gathered[7], preferred_element_type=jnp.float32
    ) + jnp.einsum("lf,df->ld", grad_up_rows, gathered[8], preferred_element_type=jnp.float32)
    grad_second = lax.psum_scatter(back_second, "tensor", scatter_dimension=0, tiled=True)
    grad_middle_norm, grad_ffn_gain = second_back(grad_second)
    grad_middle = cotangent.astype(jnp.float32) + grad_middle_norm
    attn_rows = lax.all_gather(grad_middle.astype(jnp.bfloat16), "tensor", axis=0, tiled=True)
    grad_out = jnp.einsum("lv,ld->vd", gated_low, attn_rows, preferred_element_type=jnp.float32)
    grad_gated = jnp.einsum("ld,vd->lv", attn_rows, gathered[6], preferred_element_type=jnp.float32)
    mixer_grads_local = mixer_back(grad_gated)
    grad_proj = jnp.concatenate(
        [grad_part.astype(jnp.bfloat16) for grad_part in mixer_grads_local[:6]], axis=1
    )
    grad_joined = jnp.einsum("ld,lc->dc", mixer_rows, grad_proj, preferred_element_type=jnp.float32)
    back_first = jnp.einsum("lc,dc->ld", grad_proj, joined, preferred_element_type=jnp.float32)
    grad_first = lax.psum_scatter(
        back_first.astype(jnp.bfloat16), "tensor", scatter_dimension=0, tiled=True
    ).astype(jnp.float32)
    grad_residual_norm, grad_norm_gain = first_back(grad_first)
    grad_input = grad_middle + grad_residual_norm
    grad_columns = jnp.split(grad_joined, offsets, axis=1)
    summed = (
        lax.psum_scatter(grad_columns[0], "dp", scatter_dimension=0, tiled=True),
        lax.psum_scatter(grad_columns[1], "dp", scatter_dimension=0, tiled=True),
        lax.psum_scatter(grad_columns[2], "dp", scatter_dimension=0, tiled=True),
        lax.psum_scatter(grad_columns[3], "dp", scatter_dimension=0, tiled=True),
        lax.psum_scatter(grad_columns[4], "dp", scatter_dimension=0, tiled=True),
        lax.psum_scatter(grad_columns[5], "dp", scatter_dimension=0, tiled=True),
        lax.psum_scatter(grad_out, "dp", scatter_dimension=1, tiled=True),
        lax.psum_scatter(grad_gate, "dp", scatter_dimension=0, tiled=True),
        lax.psum_scatter(grad_up, "dp", scatter_dimension=0, tiled=True),
        lax.psum_scatter(grad_down, "dp", scatter_dimension=1, tiled=True),
    )
    (
        grad_conv_query_part,
        grad_conv_key_part,
        grad_conv_value_part,
        grad_decay_log_part,
        grad_decay_bias_part,
        grad_out_gain_part,
    ) = mixer_grads_local[6:]
    full_conv_query = lax.dynamic_update_slice_in_dim(
        jnp.zeros_like(conv_query), grad_conv_query_part, tensor_rank * key_cols, 1
    )
    full_conv_key = lax.dynamic_update_slice_in_dim(
        jnp.zeros_like(conv_key), grad_conv_key_part, tensor_rank * key_cols, 1
    )
    full_conv_value = lax.dynamic_update_slice_in_dim(
        jnp.zeros_like(conv_value), grad_conv_value_part, tensor_rank * value_cols, 1
    )
    full_decay_log = lax.dynamic_update_slice_in_dim(
        jnp.zeros_like(decay_log), grad_decay_log_part, tensor_rank * local_heads, 0
    )
    full_decay_bias = lax.dynamic_update_slice_in_dim(
        jnp.zeros_like(decay_bias), grad_decay_bias_part, tensor_rank * local_heads, 0
    )
    small = lax.psum(
        (
            grad_norm_gain,
            grad_ffn_gain,
            grad_out_gain_part,
            full_conv_query,
            full_conv_key,
            full_conv_value,
            full_decay_log,
            full_decay_bias,
        ),
        ("dp", "tensor"),
    )
    return (
        layer_output,
        grad_input,
        small[0],
        summed[0],
        summed[1],
        summed[2],
        summed[3],
        summed[4],
        summed[5],
        small[3],
        small[4],
        small[5],
        small[6],
        small[7],
        small[2],
        summed[6],
        small[1],
        summed[7],
        summed[8],
        summed[9],
    )


def solution(mesh):
    in_specs = (
        P(("dp", "tensor"), None),
        P("dp"),
        P(),
        P("dp", "tensor"),
        P("dp", "tensor"),
        P("dp", "tensor"),
        P("dp", "tensor"),
        P("dp", "tensor"),
        P("dp", "tensor"),
        P(),
        P(),
        P(),
        P(),
        P(),
        P(),
        P("tensor", "dp"),
        P(),
        P("dp", "tensor"),
        P("dp", "tensor"),
        P("tensor", "dp"),
        P(("dp", "tensor"), None),
    )
    out_specs = (
        P(("dp", "tensor"), None),
        P(("dp", "tensor"), None),
        P(),
        P("dp", "tensor"),
        P("dp", "tensor"),
        P("dp", "tensor"),
        P("dp", "tensor"),
        P("dp", "tensor"),
        P("dp", "tensor"),
        P(),
        P(),
        P(),
        P(),
        P(),
        P(),
        P("tensor", "dp"),
        P(),
        P("dp", "tensor"),
        P("dp", "tensor"),
        P("tensor", "dp"),
    )
    return jax.shard_map(shards, mesh=mesh, in_specs=in_specs, out_specs=out_specs, check_vma=False)
```

profile of v0, /device:TPU:0, one launch (start us, length us, event | category | flops | bytes accessed | tf_op | source)
XLA Modules:
  0.0 2569.4 jit_solution(6259069316459720499)
XLA Ops:
  14.2 11.8 all_gather.43
  26.0 10.7 all_gather.44
  36.7 8.4 all_gather.47
  45.3 8.6 all_gather.48
  70.3 76.6 %all-gather.11.cloned.1.call-done = bf16[2048,1024]{1,0:T(8,128)(2,1)} async-done(((bf16[512,1024]{1,0:T(8,128)(2,1)}), bf16[2048,1024]{1,0:T(8,128)(2,1)}) %all-gather.11.cloned.1.call-update) | async-done | bytes 4194320 | tf_op jit(solution)/shard_map/all_gather | solution.py:221
  146.8 9.6 fusion.220
  199.8 315.8 %custom-call.10 = f32[16,2,1,128,128]{3,4,2,1,0:T(8,128)} custom-call(f32[16,2,1,128,128]{4,3,2,1,0:T(8,128)} %get-tuple-element.974), custom_call_target="InvertDiagBlocksLowerTriangular" | custom-call | tf_op jit(solution)/shard_map/jvp(jit(_solve_triangular))/vmap(vmap())/triangular_solve | solution.py:118
  515.6 11.9 multiply_bitcast_fusion.1
  539.2 6.9 fusion.77
  562.1 128.2 %while.52 = (s32[]{:T(128)}, f32[2,256,128]{2,1,0:T(8,128)S(1)}, f32[16,2,128,256]{3,2,1,0:T(8,128)}, f32[16,2,256,128]{3,2,1,0:T(8,128)}, f32[16,2,128,256]{3,2...) while((s32[]{:T(128)}, f32[2,256,128]{2,1,0:T(8,128)S(1)}, ...), condition=%wide.region_5.6_spmd.clone, body=%wide.region_4.5_spmd.clone.sunk | while | flops 403308544 | bytes 4467918 | solution.py:139
  704.9 6.5 slice_bitcast_fusion
  711.4 7.5 fusion.222
  719.7 142.6 %reduce-scatter.19.cloned.1.call-done = f32[512,1024]{1,0:T(8,128)} async-done(((f32[2048,1024]{1,0:T(8,128)}), f32[512,1024]{1,0:T(8,128)}) %reduce-scatter.19.cloned.1.call-update) | async-done | bytes 2097168 | tf_op jit(solution)/shard_map/reduce_scatter | solution.py:244
  869.0 21.1 all-gather.21.cloned.1.call-done
  890.0 82.9 %all-gather.19.cloned.1.call-done = bf16[2048,1024]{1,0:T(8,128)(2,1)} async-done(((bf16[512,1024]{1,0:T(8,128)(2,1)}), bf16[2048,1024]{1,0:T(8,128)(2,1)}) %all-gather.19.cloned.1.call-update) | async-done | bytes 4194320 | tf_op jit(solution)/shard_map/all_gather | solution.py:252
  973.0 8.4 fusion.223
  981.4 17.4 all-gather.23.cloned.1.call-done
  998.7 8.3 fusion.224
  1007.0 19.0 all-gather.25.cloned.1.call-done
  1025.9 82.2 %all-gather.27.cloned.1.call-done = bf16[2048,1024]{1,0:T(8,128)(2,1)} async-done(((bf16[512,1024]{1,0:T(8,128)(2,1)}), bf16[2048,1024]{1,0:T(8,128)(2,1)}) %all-gather.27.cloned.1.call-update) | async-done | bytes 4194320 | tf_op jit(solution)/shard_map/all_gather | solution.py:263
  1108.1 12.0 multiply_convert_fusion
  1129.6 143.1 %reduce-scatter.23.cloned.1.call-done = f32[512,1024]{1,0:T(8,128)} async-done(((f32[2048,1024]{1,0:T(8,128)}), f32[512,1024]{1,0:T(8,128)}) %reduce-scatter.23.cloned.1.call-update) | async-done | bytes 2097168 | tf_op jit(solution)/shard_map/reduce_scatter | solution.py:278
  1289.3 70.3 %all-gather.29.cloned.1.call-done = bf16[2048,1024]{1,0:T(8,128)(2,1)} async-done(((bf16[512,1024]{1,0:T(8,128)(2,1)}), bf16[2048,1024]{1,0:T(8,128)(2,1)}) %all-gather.29.cloned.1.call-update) | async-done | bytes 4194320 | tf_op jit(solution)/shard_map/all_gather | solution.py:281
  1386.5 280.6 %while.53 = (s32[]{:T(128)}, f32[2,256,128]{2,1,0:T(8,128)S(1)}, f32[16,2,128,256]{3,2,1,0:T(8,128)}, f32[16,2,128,128]{3,2,1,0:T(8,128)}, f32[16,2,128,128]{3,2...) while((s32[]{:T(128)}, f32[2,256,128]{2,1,0:T(8,128)S(1)}, ...), condition=%wide.region_16.17_spmd.clone, body=%wide.region_13.16_spmd.clone.sunk | while | flops 806289152 | bytes 7094563 | solution.py:139
  1667.1 8.9 fusion.82
  1683.2 8.0 fusion.81
  1697.5 7.0 multiply_select_fusion
  1712.4 6.6 add_bitcast_fusion
  1731.0 17.7 multiply_reduce_fusion.3
  1766.5 12.0 multiply_reduce_fusion.5
  1794.9 23.5 concatenate.24
  1818.4 10.1 fusion.227
  1844.0 11.3 convolution_convert_fusion
  1856.7 7.1 convolution_convert_fusion.1
  1865.7 6.9 fusion.231
  1874.4 6.9 fusion.230
  1883.2 6.9 fusion.229
  1904.0 37.6 %reduce-scatter.27.cloned.1.call-done = f32[128,256]{0,1:T(8,128)} async-done(((f32[1024,256]{0,1:T(8,128)}), f32[128,256]{0,1:T(8,128)}) %reduce-scatter.27.cloned.1.call-update) | async-done | bytes 131088 | tf_op jit(solution)/shard_map/reduce_scatter | solution.py:297
  1943.2 38.0 %reduce-scatter.29.cloned.1.call-done = f32[128,256]{0,1:T(8,128)} async-done(((f32[1024,256]{0,1:T(8,128)}), f32[128,256]{0,1:T(8,128)}) %reduce-scatter.29.cloned.1.call-update) | async-done | bytes 131088 | tf_op jit(solution)/shard_map/reduce_scatter | solution.py:298
  1982.8 42.7 %reduce-scatter.31.cloned.1.call-done = f32[128,512]{0,1:T(8,128)} async-done(((f32[1024,512]{0,1:T(8,128)}), f32[128,512]{0,1:T(8,128)}) %reduce-scatter.31.cloned.1.call-update) | async-done | bytes 262160 | tf_op jit(solution)/shard_map/reduce_scatter | solution.py:299
  2027.3 43.5 %reduce-scatter.33.cloned.1.call-done = f32[128,512]{0,1:T(8,128)} async-done(((f32[1024,512]{0,1:T(8,128)}), f32[128,512]{0,1:T(8,128)}) %reduce-scatter.33.cloned.1.call-update) | async-done | bytes 262160 | tf_op jit(solution)/shard_map/reduce_scatter | solution.py:300
  2072.7 77.3 %reduce-scatter.25.cloned.1.call-done = bf16[512,1024]{1,0:T(8,128)(2,1)} async-done(((bf16[2048,1024]{1,0:T(8,128)(2,1)}), bf16[512,1024]{1,0:T(8,128)(2,1)}) %reduce-scatter.25.cloned.1.call-update) | async-done | bytes 1048592 | tf_op jit(solution)/shard_map/reduce_scatter | solution.py:290
  2152.8 76.7 %reduce-scatter.21.cloned.1.call-done = bf16[512,1024]{1,0:T(8,128)(2,1)} async-done(((bf16[2048,1024]{1,0:T(8,128)(2,1)}), bf16[512,1024]{1,0:T(8,128)(2,1)}) %reduce-scatter.21.cloned.1.call-update) | async-done | bytes 1048592 | tf_op jit(solution)/shard_map/reduce_scatter | solution.py:256
  2233.8 45.2 %reduce-scatter.39.cloned.1.call-done = f32[128,704]{0,1:T(8,128)} async-done(((f32[1024,704]{0,1:T(8,128)}), f32[128,704]{0,1:T(8,128)}) %reduce-scatter.39.cloned.1.call-update) | async-done | bytes 360464 | tf_op jit(solution)/shard_map/reduce_scatter | solution.py:305
  2278.9 49.2 %reduce-scatter.37.cloned.1.call-done = f32[128,704]{0,1:T(8,128)} async-done(((f32[1024,704]{0,1:T(8,128)}), f32[128,704]{0,1:T(8,128)}) %reduce-scatter.37.cloned.1.call-update) | async-done | bytes 360464 | tf_op jit(solution)/shard_map/reduce_scatter | solution.py:304
  2328.2 48.9 %reduce-scatter.41.cloned.1.call-done = f32[704,128]{1,0:T(8,128)} async-done(((f32[704,1024]{1,0:T(8,128)}), f32[704,128]{1,0:T(8,128)}) %reduce-scatter.41.cloned.1.call-update) | async-done | bytes 360464 | tf_op jit(solution)/shard_map/reduce_scatter | solution.py:306
  2377.1 45.3 %reduce-scatter.35.cloned.1.call-done = f32[512,128]{1,0:T(8,128)} async-done(((f32[512,1024]{1,0:T(8,128)}), f32[512,128]{1,0:T(8,128)}) %reduce-scatter.35.cloned.1.call-update) | async-done | bytes 262160 | tf_op jit(solution)/shard_map/reduce_scatter | solution.py:303
  2422.4 130.3 %all-reduce.39.cloned.1.call-done = (f32[1024]{0:T(1024)}, f32[4,1024]{1,0:T(4,128)}, f32[4,1024]{1,0:T(4,128)}, f32[4,2048]{1,0:T(4,128)}, f32[8]{0:T(128)}, /*index=5*/f32[8]{0:T(128)}, f32[256]{0:T(256)}, f32[1024]{0:T(1024)}) async-done(((f32[1024]{0:T(1024)}, f32[4,1024]{1,0:T(4,128)}, f32[4,1024]{1,0:T(4,128)}, f32[4,2048]{1,0:T(4,128)}, f32[8]{0:T(128)}, /*index=5*/f32[8]{0:T(128)}, f32[256]{0:T(256)}, ...) | async-done | bytes 74832 | tf_op jit(solution)/shard_map/psum | solution.py:331
  (853 shorter events, 703.6 us)
Async XLA Ops:
  7.2 53.5 %all-gather.13.cloned.1.call-start = ((), (), s32[]{:S(2)}) async-start(), calls=%async_computation.15 | async-start | bytes 1179648 | tf_op jit(solution)/shard_map/all_gather | solution.py:210
  7.9 56.0 %all-gather.15.cloned.1.call-start = ((), (), s32[]{:S(2)}) async-start(), calls=%async_computation.16 | async-start | bytes 1179648 | tf_op jit(solution)/shard_map/all_gather | solution.py:211
  8.7 138.1 %all-gather.11.cloned.1.call-start = ((), (), s32[]{:S(2)}) async-start(), calls=%async_computation.14 | async-start | bytes 5242880 | tf_op jit(solution)/shard_map/all_gather | solution.py:221
  12.9 698.6 %all-gather.17.cloned.1.call-start = ((), (), s32[]{:S(2)}) async-start(), calls=%async_computation.17 | async-start | bytes 1179648 | tf_op jit(solution)/shard_map/all_gather | solution.py:214
  13.5 848.8 %reduce-scatter.19.cloned.1.call-start = ((), (), s32[]{:S(2)}) async-start(), calls=%async_computation.18 | async-start | bytes 10485760 | tf_op jit(solution)/shard_map/reduce_scatter | solution.py:244
  14.2 182.8 %copy-start.50 = (f32[128,128]{1,0:T(8,128)}, f32[128,128]{1,0:T(8,128)S(1)}, u32[]{:S(2)}) copy-start(f32[128,128]{1,0:T(8,128)S(1)} %get-tuple-element.1018) | copy-start | bytes 196612
  58.1 457.5 %copy-start.56 = (f32[2048]{0:T(1024)}, f32[2048]{0:T(1024)S(1)}, u32[]{:S(2)}) copy-start(f32[2048]{0:T(1024)S(1)} %get-tuple-element.1002) | copy-start | bytes 24580
  58.1 457.5 %copy-start.58 = (f32[2048]{0:T(1024)}, f32[2048]{0:T(1024)S(1)}, u32[]{:S(2)}) copy-start(f32[2048]{0:T(1024)S(1)} %get-tuple-element.1003) | copy-start | bytes 24580
  58.1 457.5 %copy-start.60 = (f32[2048]{0:T(1024)}, f32[2048]{0:T(1024)S(1)}, u32[]{:S(2)}) copy-start(f32[2048]{0:T(1024)S(1)} %get-tuple-element.1004) | copy-start | bytes 24580
  59.6 455.9 %copy-start.92 = (f32[1,512]{1,0:T(1,128)}, f32[1,512]{1,0:T(1,128)S(1)}, u32[]{:S(2)}) copy-start(f32[1,512]{1,0:T(1,128)S(1)} %get-tuple-element.976) | copy-start | bytes 6148
  179.6 371.8 %copy-start.70 = (f32[16,2,128]{2,0,1:T(8,128)}, f32[16,2,128]{2,0,1:T(8,128)S(1)}, u32[]{:S(2)}) copy-start(f32[16,2,128]{2,0,1:T(8,128)S(1)} %get-tuple-element.933) | copy-start | bytes 49156
  197.0 318.6 %copy-start.99 = (f32[1,512]{1,0:T(1,128)S(1)}, f32[1,512]{1,0:T(1,128)}, u32[]{:S(2)}) copy-start(f32[1,512]{1,0:T(1,128)} %get-tuple-element.977) | copy-start | bytes 6148
  197.0 318.6 %copy-start.101 = (f32[1,512]{1,0:T(1,128)S(1)}, f32[1,512]{1,0:T(1,128)}, u32[]{:S(2)}) copy-start(f32[1,512]{1,0:T(1,128)} %get-tuple-element.978) | copy-start | bytes 6148
  197.1 318.6 %copy-start.103 = (f32[1,512]{1,0:T(1,128)S(1)}, f32[1,512]{1,0:T(1,128)}, u32[]{:S(2)}) copy-start(f32[1,512]{1,0:T(1,128)} %get-tuple-element.979) | copy-start | bytes 6148
  719.0 171.0 %all-gather.21.cloned.1.call-start = ((), (), s32[]{:S(2)}) async-start(), calls=%async_computation.20 | async-start | bytes 1622016 | tf_op jit(solution)/shard_map/all_gather | solution.py:215
  719.6 253.4 %all-gather.19.cloned.1.call-start = ((), (), s32[]{:S(2)}) async-start(), calls=%async_computation.19 | async-start | bytes 5242880 | tf_op jit(solution)/shard_map/all_gather | solution.py:252
  864.2 412.0 %copy-start.87 = (f32[512]{0:T(512)}, f32[512]{0:T(512)S(1)}, u32[]{:S(2)}) copy-start(f32[512]{0:T(512)S(1)} %fusion.193) | copy-start | bytes 6148
  866.8 131.9 %all-gather.23.cloned.1.call-start = ((), (), s32[]{:S(2)}) async-start(), calls=%async_computation.21 | async-start | bytes 1622016 | tf_op jit(solution)/shard_map/all_gather | solution.py:216
  867.6 158.3 %all-gather.25.cloned.1.call-start = ((), (), s32[]{:S(2)}) async-start(), calls=%async_computation.22 | async-start | bytes 1622016 | tf_op jit(solution)/shard_map/all_gather | solution.py:217
  868.3 239.8 %all-gather.27.cloned.1.call-start = ((), (), s32[]{:S(2)}) async-start(), calls=%async_computation.24 | async-start | bytes 5242880 | tf_op jit(solution)/shard_map/all_gather | solution.py:263
  868.9 403.8 %reduce-scatter.23.cloned.1.call-start = ((), (), s32[]{:S(2)}) async-start(), calls=%async_computation.25 | async-start | bytes 10485760 | tf_op jit(solution)/shard_map/reduce_scatter | solution.py:278
  1129.6 230.0 %all-gather.29.cloned.1.call-start = ((), (), s32[]{:S(2)}) async-start(), calls=%async_computation.26 | async-start | bytes 5242880 | tf_op jit(solution)/shard_map/all_gather | solution.py:281
  1277.9 620.7 %reduce-scatter.43.cloned.1.call-start = ((), (), s32[]{:S(2)}) async-start(), calls=%async_computation.36 | async-start | bytes 589824
  1832.3 70.2 %reduce-scatter.45.cloned.1.call-start = ((), (), s32[]{:S(2)}) async-start(), calls=%async_computation.37 | async-start | bytes 589824
  1833.4 108.2 %reduce-scatter.27.cloned.1.call-start = ((), (), s32[]{:S(2)}) async-start(), calls=%async_computation.28 | async-start | bytes 1179648 | tf_op jit(solution)/shard_map/reduce_scatter | solution.py:297
  1836.6 144.6 %reduce-scatter.29.cloned.1.call-start = ((), (), s32[]{:S(2)}) async-start(), calls=%async_computation.29 | async-start | bytes 1179648 | tf_op jit(solution)/shard_map/reduce_scatter | solution.py:298
  1837.1 188.4 %reduce-scatter.31.cloned.1.call-start = ((), (), s32[]{:S(2)}) async-start(), calls=%async_computation.30 | async-start | bytes 2359296 | tf_op jit(solution)/shard_map/reduce_scatter | solution.py:299
  1842.1 228.8 %reduce-scatter.33.cloned.1.call-start = ((), (), s32[]{:S(2)}) async-start(), calls=%async_computation.31 | async-start | bytes 2359296 | tf_op jit(solution)/shard_map/reduce_scatter | solution.py:300
  1842.7 307.3 %reduce-scatter.25.cloned.1.call-start = ((), (), s32[]{:S(2)}) async-start(), calls=%async_computation.27 | async-start | bytes 5242880 | tf_op jit(solution)/shard_map/reduce_scatter | solution.py:290
  1855.4 374.1 %reduce-scatter.21.cloned.1.call-start = ((), (), s32[]{:S(2)}) async-start(), calls=%async_computation.23 | async-start | bytes 5242880 | tf_op jit(solution)/shard_map/reduce_scatter | solution.py:256
  1863.9 415.1 %reduce-scatter.39.cloned.1.call-start = ((), (), s32[]{:S(2)}) async-start(), calls=%async_computation.34 | async-start | bytes 3244032 | tf_op jit(solution)/shard_map/reduce_scatter | solution.py:305
  1872.6 455.6 %reduce-scatter.37.cloned.1.call-start = ((), (), s32[]{:S(2)}) async-start(), calls=%async_computation.33 | async-start | bytes 3244032 | tf_op jit(solution)/shard_map/reduce_scatter | solution.py:304
  1881.4 495.7 %reduce-scatter.41.cloned.1.call-start = ((), (), s32[]{:S(2)}) async-start(), calls=%async_computation.35 | async-start | bytes 3244032 | tf_op jit(solution)/shard_map/reduce_scatter | solution.py:306
  1890.1 532.3 %reduce-scatter.35.cloned.1.call-start = ((), (), s32[]{:S(2)}) async-start(), calls=%async_computation.32 | async-start | bytes 2359296 | tf_op jit(solution)/shard_map/reduce_scatter | solution.py:303
  1897.6 252.4 %copy-start.20 = (bf16[512,1024]{1,0:T(8,128)(2,1)S(1)}, bf16[512,1024]{1,0:T(8,128)(2,1)}, u32[]{:S(2)}) copy-start(bf16[512,1024]{1,0:T(8,128)(2,1)} %param.25) | copy-start | bytes 3145732
  1897.6 252.4 %copy-start.89 = (f32[1024]{0:T(1024)S(1)}, f32[1024]{0:T(1024)}, u32[]{:S(2)}) copy-start(f32[1024]{0:T(1024)} %param.27) | copy-start | bytes 12292
  1897.6 252.4 %copy-start.91 = (f32[512]{0:T(512)S(1)}, f32[512]{0:T(512)}, u32[]{:S(2)}) copy-start(f32[512]{0:T(512)} %copy-done.90) | copy-start | bytes 6148
  1897.6 255.1 %copy-start.96 = (f32[512]{0:T(512)S(1)}, f32[512]{0:T(512)}, u32[]{:S(2)}) copy-start(f32[512]{0:T(512)} %copy-done.95) | copy-start | bytes 6148
  1897.6 331.9 %copy-start.4 = (f32[512,1024]{1,0:T(8,128)S(1)}, f32[512,1024]{1,0:T(8,128)}, u32[]{:S(2)}) copy-start(f32[512,1024]{1,0:T(8,128)} %copy-done.2) | copy-start | bytes 6291460
  1897.6 331.9 %copy-start.80 = (f32[1024]{0:T(1024)S(1)}, f32[1024]{0:T(1024)}, u32[]{:S(2)}) copy-start(f32[1024]{0:T(1024)} %param.41) | copy-start | bytes 12292
  1897.6 331.9 %copy-start.88 = (f32[512]{0:T(512)S(1)}, f32[512]{0:T(512)}, u32[]{:S(2)}) copy-start(f32[512]{0:T(512)} %copy-done.87) | copy-start | bytes 6148
  1897.6 331.9 %copy-start.98 = (f32[512]{0:T(512)S(1)}, f32[512]{0:T(512)}, u32[]{:S(2)}) copy-start(f32[512]{0:T(512)} %copy-done.97) | copy-start | bytes 6148
  1897.6 655.0 %all-reduce.39.cloned.1.call-start = ((), (), s32[]{:S(2)}) async-start(), calls=%async_computation.38 | async-start | bytes 151552 | tf_op jit(solution)/shard_map/psum | solution.py:331
  1897.9 254.8 %copy-start.129 = (f32[8]{0:T(128)}, f32[8]{0:T(128)S(1)}, u32[]{:S(2)}) copy-start(f32[8]{0:T(128)S(1)} %dynamic_update_slice.107) | copy-start | bytes 100
  1898.0 254.8 %copy-start.85 = (f32[4,1024]{1,0:T(4,128)}, f32[4,1024]{1,0:T(4,128)S(1)}, u32[]{:S(2)}) copy-start(f32[4,1024]{1,0:T(4,128)S(1)} %add_dynamic-update-slice_fusion.1) | copy-start | bytes 49156
  1898.0 254.7 %copy-start.84 = (f32[4,1024]{1,0:T(4,128)}, f32[4,1024]{1,0:T(4,128)S(1)}, u32[]{:S(2)}) copy-start(f32[4,1024]{1,0:T(4,128)S(1)} %add_dynamic-update-slice_fusion.2) | copy-start | bytes 49156
  1898.1 254.7 %copy-start.78 = (f32[4,2048]{1,0:T(4,128)}, f32[4,2048]{1,0:T(4,128)S(1)}, u32[]{:S(2)}) copy-start(f32[4,2048]{1,0:T(4,128)S(1)} %add_dynamic-update-slice_fusion) | copy-start | bytes 98308
  1898.6 254.2 %copy-start.128 = (f32[8]{0:T(128)}, f32[8]{0:T(128)S(1)}, u32[]{:S(2)}) copy-start(f32[8]{0:T(128)S(1)} %multiply_dynamic-update-slice_fusion) | copy-start | bytes 100
  (122 other events, 2288.8 us)
Sparse Core Ops, SparseCore 0:
  9.9 28.2 all-gather.12
  40.1 23.7 all-gather.14
  66.0 80.7 all-gather.10
  148.5 22.1 all-gather.16
  719.1 143.0 reduce-scatter.18
  864.0 26.0 all-gather.20
  892.2 80.7 all-gather.18
  974.8 23.8 all-gather.22
  1000.6 25.2 all-gather.24
  1027.3 80.7 all-gather.26
  1129.7 142.9 reduce-scatter.22
  1278.0 81.4 all-gather.28
  1832.4 32.6 reduce-scatter.42
  1868.3 34.1 reduce-scatter.44
  1905.5 35.9 reduce-scatter.26
  1945.1 35.9 reduce-scatter.28
  1984.3 41.2 reduce-scatter.30
  2029.6 41.2 reduce-scatter.32
  2073.2 76.7 reduce-scatter.24
  2152.2 77.2 reduce-scatter.20
  2233.5 45.4 reduce-scatter.38
  2283.3 44.8 reduce-scatter.36
  2332.1 44.9 reduce-scatter.40
  2381.2 41.1 reduce-scatter.34
  2430.5 122.0 all-reduce.38
where the time goes:
time: 2580 us; the launch traced here: 2570 us
  waiting for transfers between devices  1300 us (50%)
  matrix products  513 us (20%)
  other arithmetic  481 us (19%)
  local copies, waits for them, and re-layouts  217 us (8%)
  blocking collectives  39.5 us (2%)
    dot_general x198, matrix products, exact_einsum(): jnp.einsum(form, left, right, precision=highest_precision, preferred_elem...  367 us
    another operation x3, other arithmetic, span_delta(): jax.scipy.linalg.solve_triangular(system, right_sides, lower=True, unit_d...  317 us
    reduce_scatter x1, waiting for transfers between devices, shards(): lax.psum_scatter(back_second, 'tensor', scatter_dimension=0, tiled=True)  143 us
    reduce_scatter x1, waiting for transfers between devices, shards(): lax.psum_scatter(jnp.dot(gated_low, gathered[6], preferred_element_type=j...  143 us
    psum x1, waiting for transfers between devices, shards(): lax.psum((grad_norm_gain, grad_ffn_gain, grad_out_gain_part, full_conv_qu...  130 us
    all_gather x1, waiting for transfers between devices, shards(): lax.all_gather(second.astype(jnp.bfloat16), 'tensor', axis=0, tiled=True)  82.9 us
    all_gather x1, waiting for transfers between devices, shards(): cot_rows = lax.all_gather(cotangent, 'tensor', axis=0, tiled=True)  82.2 us
    reduce_scatter x1, waiting for transfers between devices, shards(): lax.psum_scatter(back_first.astype(jnp.bfloat16), 'tensor', scatter_dimen...  77.3 us
  transfers between devices with their start and end apart: 25, of which 22 were waited for; matrix products, arithmetic and copies ran while one was open for 26% of the time, Pallas kernels for 0%

commit v1 on v0

v1 whole, which is shorter than its diff:
```python
from functools import partial

import jax
import jax.numpy as jnp
from jax import lax
from jax.experimental import pallas as pl
from jax.experimental.pallas import tpu as pltpu
from jax.sharding import PartitionSpec as P

CHUNK = 128
TINY = 1e-06
LANES = 128


def split_high(values):
    high = values.astype(jnp.bfloat16)
    return high, (values - high.astype(jnp.float32)).astype(jnp.bfloat16)


def contract(left, right, dims):
    return lax.dot_general(
        left, right, ((dims[:1], dims[1:]), ((), ())), preferred_element_type=jnp.float32
    )


def dot_one(left, right, dims=(1, 0)):
    return contract(left.astype(jnp.bfloat16), right.astype(jnp.bfloat16), dims)


def dot_three(left, right, dims=(1, 0)):
    left_high, left_low = split_high(left)
    right_high, right_low = split_high(right)
    return (
        contract(left_high, right_high, dims)
        + contract(left_high, right_low, dims)
        + contract(left_low, right_high, dims)
    )


def square_three(left, right):
    left_high, left_low = split_high(left)
    right_high, right_low = split_high(right)
    wide_left = jnp.concatenate([left_high, left_low], axis=1)
    row = jnp.concatenate([right_high, right_low], axis=1)
    product = contract(wide_left, jnp.concatenate([row, row], axis=0), (1, 0))
    width = right.shape[1]
    return product[:, :width] + product[:, width:]


def iota2(shape, axis):
    return lax.broadcasted_iota(jnp.int32, shape, axis)


def sigmoid(values):
    return 1.0 / (1.0 + jnp.exp(-values))


def softplus(values):
    return jnp.maximum(values, 0.0) + jnp.log1p(jnp.exp(-jnp.abs(values)))


def unit_inverses(lowers):
    rows = iota2((CHUNK, CHUNK), 0)
    cols = iota2((CHUNK, CHUNK), 1)
    differ = jnp.bitwise_xor(rows, cols)
    identity = jnp.where(rows == cols, 1.0, 0.0)
    block = 1
    results = None
    while block < CHUNK:
        pick = jnp.logical_and(differ >= block, differ < 2 * block)
        parts = [jnp.where(pick, lower, 0.0) for lower in lowers]
        if block == 1:
            results = [identity - part for part in parts]
        else:
            inner = [square_three(part, result) for part, result in zip(parts, results)]
            outer = [square_three(result, mid) for mid, result in zip(inner, results)]
            results = [result - out for result, out in zip(results, outer)]
        block *= 2
    return results


def head_scalars(small, head_ref):
    decay_scale = -jnp.exp(head_ref[0:1, :])
    shifted = small + head_ref[1:2, :]
    return sigmoid(small), decay_scale * softplus(shifted), decay_scale * sigmoid(shifted)


def running_sum(values, reverse=False):
    rows = iota2((CHUNK, CHUNK), 0)
    cols = iota2((CHUNK, CHUNK), 1)
    keep = (cols >= rows) if reverse else (rows >= cols)
    ones = jnp.where(keep, 1.0, 0.0).astype(jnp.bfloat16)
    high, low = split_high(values)
    lowest = (values - high.astype(jnp.float32) - low.astype(jnp.float32)).astype(jnp.bfloat16)
    return (
        contract(ones, high, (1, 0)) + contract(ones, low, (1, 0)) + contract(ones, lowest, (1, 0))
    )


def conv_rows(window_ref, aux, taps_ref, count, lo, hi):
    total = window_ref[8 : 8 + count, lo:hi] * taps_ref[0:1, lo:hi]
    for lag in range(1, taps_ref.shape[0]):
        shifted = window_ref[8 - lag : 8 - lag + count, lo:hi] * aux[:, lag - 1 : lag]
        total = total + shifted * taps_ref[lag : lag + 1, lo:hi]
    return total


def decay_parts(cumulative, cumulative_rows, aux, segment_row, lane):
    cum_col = cumulative[:, lane : lane + 1]
    cum_row = cumulative_rows[lane : lane + 1, :]
    rows = iota2((CHUNK, CHUNK), 0)
    cols = iota2((CHUNK, CHUNK), 1)
    keep = jnp.logical_and(rows >= cols, aux[:, 5:6] == segment_row)
    matrix = jnp.where(keep, jnp.exp(jnp.minimum(cum_col - cum_row, 0.0)), 0.0)
    last = cum_col[CHUNK - 1 : CHUNK, :]
    growth = jnp.exp(cum_col) * aux[:, 3:4]
    tail = jnp.exp(last - cum_col) * aux[:, 4:5]
    carry = jnp.exp(last) * aux[CHUNK - 1 : CHUNK, 3:4]
    return matrix, growth, tail, carry


def forward_body(
    sizes,
    rank_ref,
    proj_ref,
    aux_ref,
    segment_ref,
    taps_ref,
    head_ref,
    gain_ref,
    gated_ref,
    out_ref,
    fresh_ref,
    state_ref,
    inverse_ref,
    window_ref,
    carried_ref,
):
    heads, dk, dv, chunks = sizes
    count = chunks * CHUNK
    keys, conv_cols = heads * dk, heads * (2 * dk + dv)
    gate_at, small_at = conv_cols, conv_cols + heads * dv

    @pl.when(pl.program_id(0) == 0)
    def start():
        window_ref[0:8, :] = jnp.zeros((8, conv_cols), jnp.float32)
        carried_ref[...] = jnp.zeros(carried_ref.shape, jnp.float32)

    aux = aux_ref[...]
    window_ref[8 : 8 + count, :] = proj_ref[:, :conv_cols]
    beta_all, decay_all, _ = head_scalars(proj_ref[:, small_at : small_at + LANES], head_ref)

    queries, key_rows, values = [], [], []
    for head in range(heads):
        mixed = conv_rows(window_ref, aux, taps_ref, count, head * dk, (head + 1) * dk)
        mixed = mixed * sigmoid(mixed)
        queries.append(
            mixed * (lax.rsqrt(jnp.sum(mixed * mixed, axis=1, keepdims=True) + TINY) * dk**-0.5)
        )
        mixed = conv_rows(window_ref, aux, taps_ref, count, keys + head * dk, keys + (head + 1) * dk)
        mixed = mixed * sigmoid(mixed)
        key_rows.append(mixed * lax.rsqrt(jnp.sum(mixed * mixed, axis=1, keepdims=True) + TINY))
        at = 2 * keys + head * dv
        mixed = conv_rows(window_ref, aux, taps_ref, count, at, at + dv)
        values.append(mixed * sigmoid(mixed))

    strict = iota2((CHUNK, CHUNK), 0) > iota2((CHUNK, CHUNK), 1)
    items = []
    lowers = []
    for chunk in range(chunks):
        span = slice(chunk * CHUNK, (chunk + 1) * CHUNK)
        cumulative = running_sum(decay_all[span])
        cumulative_rows = jnp.transpose(cumulative)
        for head in range(heads):
            matrix, growth, tail, carry = decay_parts(
                cumulative, cumulative_rows, aux[span], segment_ref[chunk], heads + head
            )
            beta = beta_all[span, head : head + 1]
            query, key = queries[head][span], key_rows[head][span]
            lowers.append(
                jnp.where(strict, beta * matrix * dot_three(key, key, (1, 1)), 0.0)
            )
            scores = dot_three(query, key, (1, 1)) * matrix
            items.append((span, chunk, head, beta, query, key, scores, growth, tail, carry))
    inverses = unit_inverses(lowers)
    for (span, chunk, head, beta, query, key, scores, growth, tail, carry), inverse in zip(
        items, inverses
    ):
        wide = slice(head * dv, (head + 1) * dv)
        inverse_ref[span, head * CHUNK : (head + 1) * CHUNK] = inverse
        state = carried_ref[head]
        state_ref[chunk, :, wide] = state
        right = beta * (values[head][span] - growth * dot_three(key, state))
        fresh = dot_three(inverse, right)
        fresh_ref[span, wide] = fresh
        carried_ref[head] = carry * state + dot_three(tail * key, fresh, (0, 0))
        emitted = growth * dot_three(query, state) + dot_three(scores, fresh)
        out_ref[span, wide] = emitted
        gate = proj_ref[span, gate_at + head * dv : gate_at + (head + 1) * dv]
        scale = lax.rsqrt(jnp.mean(emitted * emitted, axis=1, keepdims=True) + TINY)
        gated_ref[span, wide] = (
            emitted * scale * gain_ref[...] * (gate * sigmoid(gate))
        ).astype(jnp.bfloat16)
    window_ref[0:8, :] = proj_ref[count - 8 : count, :conv_cols]


def backward_body(
    sizes,
    rank_ref,
    proj_ref,
    before_ref,
    aux_ref,
    segment_ref,
    taps_ref,
    head_ref,
    gain_ref,
    out_ref,
    fresh_ref,
    state_ref,
    inverse_ref,
    grad_ref,
    dproj_ref,
    dtaps_ref,
    dgain_ref,
    dhead_ref,
    window_ref,
    later_ref,
    carried_ref,
):
    heads, dk, dv, chunks = sizes
    count = chunks * CHUNK
    keys, conv_cols = heads * dk, heads * (2 * dk + dv)
    gate_at, small_at = conv_cols, conv_cols + heads * dv
    lags = taps_ref.shape[0]

    @pl.when(pl.program_id(0) == 0)
    def start():
        later_ref[count : count + 8, :] = jnp.zeros((8, conv_cols), jnp.float32)
        carried_ref[...] = jnp.zeros(carried_ref.shape, jnp.float32)
        dtaps_ref[...] = jnp.zeros(dtaps_ref.shape, jnp.float32)
        dgain_ref[...] = jnp.zeros(dgain_ref.shape, jnp.float32)
        dhead_ref[...] = jnp.zeros(dhead_ref.shape, jnp.float32)

    aux = aux_ref[...]
    first = pl.program_id(0) == pl.num_programs(0) - 1
    window_ref[0:8, :] = jnp.where(first, 0.0, before_ref[:, :conv_cols])
    window_ref[8 : 8 + count, :] = proj_ref[:, :conv_cols]
    beta_all, decay_all, slope_all = head_scalars(
        proj_ref[:, small_at : small_at + LANES], head_ref
    )
    lane = iota2((CHUNK, LANES), 1)
    row_at = iota2((LANES, CHUNK), 0)
    strict = iota2((CHUNK, CHUNK), 0) > iota2((CHUNK, CHUNK), 1)

    def activated(lo, width):
        mixed = conv_rows(window_ref, aux, taps_ref, count, lo, lo + width)
        gate = sigmoid(mixed)
        return mixed * gate, gate * (1.0 + mixed * (1.0 - gate))

    for head in range(heads):
        wide = slice(head * dv, (head + 1) * dv)
        emitted = out_ref[:, wide]
        scale = lax.rsqrt(jnp.mean(emitted * emitted, axis=1, keepdims=True) + TINY)
        normed = emitted * scale
        at = gate_at + head * dv
        gate = proj_ref[:, at : at + dv]
        sig = sigmoid(gate)
        upper = grad_ref[:, wide].astype(jnp.float32)
        with_gate = upper * (gate * sig)
        dgain_ref[...] += jnp.sum((with_gate * normed).reshape(count // 8, 8, dv), axis=0)
        dproj_ref[:, at : at + dv] = (
            upper * normed * gain_ref[...] * (sig * (1.0 + gate * (1.0 - sig)))
        ).astype(jnp.bfloat16)
        dnormed = with_gate * gain_ref[...]
        dout_all = scale * (
            dnormed - normed * jnp.mean(dnormed * normed, axis=1, keepdims=True)
        )

        query_raw, query_slope = activated(head * dk, dk)
        query_scale = lax.rsqrt(jnp.sum(query_raw * query_raw, axis=1, keepdims=True) + TINY)
        query_unit = query_raw * query_scale
        key_raw, key_slope = activated(keys + head * dk, dk)
        key_scale = lax.rsqrt(jnp.sum(key_raw * key_raw, axis=1, keepdims=True) + TINY)
        key_all = key_raw * key_scale
        value_all, value_slope = activated(2 * keys + head * dv, dv)
        query_all = query_unit * dk**-0.5

        for chunk in reversed(range(chunks)):
            span = slice(chunk * CHUNK, (chunk + 1) * CHUNK)
            cumulative = running_sum(decay_all[span])
            matrix, growth, tail, carry = decay_parts(
                cumulative, jnp.transpose(cumulative), aux[span], segment_ref[chunk], heads + head
            )
            beta = beta_all[span, head : head + 1]
            query, key, value = query_all[span], key_all[span], value_all[span]
            inverse = inverse_ref[span, head * CHUNK : (head + 1) * CHUNK]
            state = state_ref[chunk, :, wide]
            fresh = fresh_ref[span, wide]
            dout = dout_all[span]
            key_products = dot_three(key, key, (1, 1)) * matrix
            scores = dot_three(query, key, (1, 1)) * matrix

            dstate = carried_ref[head]
            dfresh = dot_three(scores, dout, (0, 0)) + dot_three(tail * key, dstate)
            dright = dot_three(inverse, dfresh, (0, 0))
            carried_ref[head] = (
                carry * dstate
                + dot_three(growth * query, dout, (0, 0))
                - dot_three((growth * beta) * key, dright, (0, 0))
            )
            dscores = dot_three(dout, fresh, (1, 1))
            dlower = jnp.where(strict, -dot_three(dright, fresh, (1, 1)), 0.0)
            out_state = dot_three(dout, state, (1, 1))
            right_state = dot_three(dright, state, (1, 1))
            fresh_state = dot_three(fresh, dstate, (1, 1))
            dscores_key = dscores * matrix
            dlower_key = dlower * matrix * beta
            dquery = growth * out_state + dot_three(dscores_key, key)
            dkey = (
                tail * fresh_state
                + dot_three(dscores_key, query, (0, 0))
                - (growth * beta) * right_state
                + dot_three(dlower_key, key)
                + dot_three(dlower_key, key, (0, 0))
            )
            dvalue = beta * dright
            right_key = jnp.sum(right_state * key, axis=1, keepdims=True)
            dbeta = (
                jnp.sum(dright * value, axis=1, keepdims=True)
                - growth * right_key
                + jnp.sum(dlower * key_products, axis=1, keepdims=True)
            )
            dgrowth = jnp.sum(out_state * query, axis=1, keepdims=True) - beta * right_key
            dtail = jnp.sum(fresh_state * key, axis=1, keepdims=True)
            dcarry = jnp.sum(jnp.sum(dstate * state, axis=1, keepdims=True), axis=0, keepdims=True)
            dgap = dscores * scores + dlower * beta * key_products
            tail_term = dtail * tail
            last_term = jnp.sum(tail_term, axis=0, keepdims=True) + dcarry * carry
            is_last = iota2((CHUNK, 1), 0) == CHUNK - 1
            dcum = (
                jnp.sum(dgap, axis=1, keepdims=True)
                + dgrowth * growth
                - tail_term
                + jnp.where(is_last, last_term, 0.0)
            )
            down = jnp.sum(dgap, axis=0, keepdims=True)
            columns = jnp.transpose(jnp.where(row_at == heads + head, down, 0.0))
            ddecay = running_sum(jnp.where(lane == heads + head, dcum, 0.0) - columns, True)
            dbeta_lane = jnp.where(lane == head, dbeta, 0.0)
            dshift = ddecay * slope_all[span]
            dhead_ref[0:8, :] += jnp.sum(
                (ddecay * decay_all[span]).reshape(CHUNK // 8, 8, LANES), axis=0
            )
            dhead_ref[8:16, :] += jnp.sum(dshift.reshape(CHUNK // 8, 8, LANES), axis=0)
            sig_beta = beta_all[span]
            dsmall = dbeta_lane * (sig_beta * (1.0 - sig_beta)) + dshift
            if head == 0:
                small_parts = {} if chunk == chunks - 1 else small_parts
                small_parts[chunk] = dsmall
            else:
                small_parts[chunk] = small_parts[chunk] + dsmall

            def unit_back(grad, unit, scale_col):
                return scale_col * (grad - unit * jnp.sum(grad * unit, axis=1, keepdims=True))

            rows_at = slice(chunk * CHUNK, (chunk + 1) * CHUNK)
            later_ref[rows_at, head * dk : (head + 1) * dk] = (
                unit_back(dquery * dk**-0.5, query_unit[span], query_scale[span])
                * query_slope[span]
            )
            later_ref[rows_at, keys + head * dk : keys + (head + 1) * dk] = (
                unit_back(dkey, key, key_scale[span]) * key_slope[span]
            )
            at = 2 * keys + head * dv
            later_ref[rows_at, at : at + dv] = dvalue * value_slope[span]

    for chunk in range(chunks):
        span = slice(chunk * CHUNK, (chunk + 1) * CHUNK)
        dproj_ref[span, small_at : small_at + LANES] = small_parts[chunk].astype(jnp.bfloat16)

    block = 256
    for lo in range(0, conv_cols, block):
        hi = lo + block
        here = later_ref[0:count, lo:hi]
        total = here * taps_ref[0:1, lo:hi]
        dtaps_ref[0:8, lo:hi] += jnp.sum(
            (here * window_ref[8 : 8 + count, lo:hi]).reshape(count // 8, 8, block), axis=0
        )
        for lag in range(1, lags):
            ahead = later_ref[lag : lag + count, lo:hi] * aux[:, 5 + lag : 6 + lag]
            total = total + ahead * taps_ref[lag : lag + 1, lo:hi]
            shifted = window_ref[8 - lag : 8 - lag + count, lo:hi] * aux[:, lag - 1 : lag]
            dtaps_ref[8 * lag : 8 * lag + 8, lo:hi] += jnp.sum(
                (here * shifted).reshape(count // 8, 8, block), axis=0
            )
        dproj_ref[:, lo:hi] = total.astype(jnp.bfloat16)
    later_ref[count : count + 8, :] = later_ref[0:8, :]


FORWARD_CHUNKS = 2
BACKWARD_CHUNKS = 1


def whole_block(array):
    return pl.BlockSpec(array.shape, lambda step, rank: (0,) * array.ndim)


def mixer_forward(rank, proj, aux, segment_rows, taps, head_rows, gain, heads, dk, dv):
    length, width = proj.shape
    chunks = FORWARD_CHUNKS
    count = chunks * CHUNK
    steps = length // count
    conv_cols = heads * (2 * dk + dv)
    rows = lambda cols: pl.BlockSpec((count, cols), lambda step, rank: (step, 0))
    return pl.pallas_call(
        partial(forward_body, (heads, dk, dv, chunks)),
        grid_spec=pltpu.PrefetchScalarGridSpec(
            num_scalar_prefetch=1,
            grid=(steps,),
            in_specs=[
                rows(width),
                rows(LANES),
                pl.BlockSpec((chunks, 1, CHUNK), lambda step, rank: (step, 0, 0)),
                whole_block(taps),
                whole_block(head_rows),
                whole_block(gain),
            ],
            out_specs=[
                rows(heads * dv),
                rows(heads * dv),
                rows(heads * dv),
                pl.BlockSpec((chunks, dk, heads * dv), lambda step, rank: (step, 0, 0)),
                rows(heads * CHUNK),
            ],
            scratch_shapes=[
                pltpu.VMEM((8 + count, conv_cols), jnp.float32),
                pltpu.VMEM((heads, dk, dv), jnp.float32),
            ],
        ),
        out_shape=[
            jax.ShapeDtypeStruct((length, heads * dv), jnp.bfloat16),
            jax.ShapeDtypeStruct((length, heads * dv), jnp.float32),
            jax.ShapeDtypeStruct((length, heads * dv), jnp.float32),
            jax.ShapeDtypeStruct((length // CHUNK, dk, heads * dv), jnp.float32),
            jax.ShapeDtypeStruct((length, heads * CHUNK), jnp.float32),
        ],
        compiler_params=pltpu.CompilerParams(vmem_limit_bytes=48 * 2**20),
        cost_estimate=pl.CostEstimate(
            flops=80 * 10**9, bytes_accessed=length * width * 12, transcendentals=0
        ),
        name="mixer_forward",
    )(rank, proj, aux, segment_rows, taps, head_rows, gain)


def mixer_backward(
    rank, proj, aux, segment_rows, taps, head_rows, gain, saved, grad, heads, dk, dv
):
    length, width = proj.shape
    chunks = BACKWARD_CHUNKS
    count = chunks * CHUNK
    steps = length // count
    conv_cols = heads * (2 * dk + dv)
    out, fresh, states, inverses = saved
    place = lambda step: steps - 1 - step
    rows = lambda cols: pl.BlockSpec((count, cols), lambda step, rank: (place(step), 0))
    lags = taps.shape[0]
    before = pl.BlockSpec(
        (8, width), lambda step, rank: (jnp.maximum(place(step) * (count // 8) - 1, 0), 0)
    )
    whole = lambda shape: pl.BlockSpec(shape, lambda step, rank: (0, 0))
    return pl.pallas_call(
        partial(backward_body, (heads, dk, dv, chunks)),
        grid_spec=pltpu.PrefetchScalarGridSpec(
            num_scalar_prefetch=1,
            grid=(steps,),
            in_specs=[
                rows(width),
                before,
                rows(LANES),
                pl.BlockSpec((chunks, 1, CHUNK), lambda step, rank: (place(step), 0, 0)),
                whole_block(taps),
                whole_block(head_rows),
                whole_block(gain),
                rows(heads * dv),
                rows(heads * dv),
                pl.BlockSpec((chunks, dk, heads * dv), lambda step, rank: (place(step), 0, 0)),
                rows(heads * CHUNK),
                rows(heads * dv),
            ],
            out_specs=[
                rows(width),
                whole((8 * lags, conv_cols)),
                whole((8, dv)),
                whole((16, LANES)),
            ],
            scratch_shapes=[
                pltpu.VMEM((8 + count, conv_cols), jnp.float32),
                pltpu.VMEM((8 + count, conv_cols), jnp.float32),
                pltpu.VMEM((heads, dk, dv), jnp.float32),
            ],
        ),
        out_shape=[
            jax.ShapeDtypeStruct((length, width), jnp.bfloat16),
            jax.ShapeDtypeStruct((8 * lags, conv_cols), jnp.float32),
            jax.ShapeDtypeStruct((8, dv), jnp.float32),
            jax.ShapeDtypeStruct((16, LANES), jnp.float32),
        ],
        compiler_params=pltpu.CompilerParams(vmem_limit_bytes=48 * 2**20),
        cost_estimate=pl.CostEstimate(
            flops=160 * 10**9, bytes_accessed=length * width * 16, transcendentals=0
        ),
        name="mixer_backward",
    )(
        rank, proj, proj, aux, segment_rows, taps, head_rows, gain,
        out, fresh, states, inverses, grad,
    )


def segment_columns(segments):
    length = segments.shape[0]
    blocks = segments.reshape(-1, CHUNK)

    def earlier(lag):
        return jnp.concatenate([jnp.full((lag,), -1, jnp.int32), segments[:-lag]])

    def later(lag):
        return jnp.concatenate([segments[lag:], jnp.full((lag,), -1, jnp.int32)])

    same = [segments == earlier(lag) for lag in (1, 2, 3)]
    before = earlier(1).reshape(-1, CHUNK)[:, :1]
    same.append((blocks == before).reshape(length))
    same.append((blocks == blocks[:, -1:]).reshape(length))
    columns = [one.astype(jnp.float32) for one in same] + [segments.astype(jnp.float32)]
    columns += [(segments == later(lag)).astype(jnp.float32) for lag in (1, 2, 3)]
    table = jnp.stack(columns, axis=1)
    return jnp.pad(table, ((0, 0), (0, LANES - len(columns))))


def rms_parts(values):
    return lax.rsqrt(jnp.mean(values * values, axis=-1, keepdims=True) + TINY)


def rms_back(grad, gain, normed, scale):
    scaled = grad * gain
    return scale * (scaled - normed * jnp.mean(scaled * normed, axis=-1, keepdims=True))


def padded(array, width):
    return jnp.pad(array, ((0, 0), (0, width - array.shape[1])))


def product(left, right, left_dim, right_dim):
    return lax.dot_general(
        left, right, (((left_dim,), (right_dim,)), ((), ())), preferred_element_type=jnp.float32
    )


def up_to(size, unit):
    return -(-size // unit) * unit


def shards(
    layer_input,
    segments,
    norm_gain,
    w_query,
    w_key,
    w_value,
    w_outgate,
    w_beta,
    w_decay,
    conv_query,
    conv_key,
    conv_value,
    decay_log,
    decay_bias,
    out_gain,
    w_out,
    ffn_gain,
    w_gate,
    w_up,
    w_down,
    cotangent,
):
    tensor_rank = lax.axis_index("tensor")
    ranks = lax.axis_size("tensor")
    key_cols, value_cols, heads = w_query.shape[1], w_value.shape[1], w_beta.shape[1]
    dk, dv = key_cols // heads, value_cols // heads
    units = w_gate.shape[1]
    unit_cols = up_to(units, 256)
    conv_cols = 2 * key_cols + value_cols
    gate_at, small_at = conv_cols, conv_cols + value_cols

    joined = lax.all_gather(
        padded(
            jnp.concatenate([w_query, w_key, w_value, w_outgate, w_beta, w_decay], axis=1),
            small_at + LANES,
        ),
        "dp",
        axis=0,
        tiled=True,
    )
    rest = lax.all_gather(
        jnp.concatenate(
            [w_out.T, padded(w_gate, unit_cols), padded(w_up, unit_cols), padded(w_down.T, unit_cols)],
            axis=1,
        ),
        "dp",
        axis=0,
        tiled=True,
    )
    cut_out, cut_down = value_cols, value_cols + 2 * unit_cols
    out_full, pair_full, down_full = (
        rest[:, :cut_out],
        rest[:, cut_out:cut_down],
        rest[:, cut_down:],
    )

    residual = layer_input.astype(jnp.float32)
    first_scale = rms_parts(residual)
    first_normed = residual * first_scale
    mixer_rows = lax.all_gather(
        (first_normed * norm_gain).astype(jnp.bfloat16), "tensor", axis=0, tiled=True
    )
    projected = product(mixer_rows, joined, 1, 0)

    def local(array, width):
        return lax.dynamic_slice_in_dim(array, tensor_rank * width, width, array.ndim - 1)

    taps = jnp.concatenate(
        [local(conv_query, key_cols), local(conv_key, key_cols), local(conv_value, value_cols)],
        axis=1,
    )
    head_rows = jnp.pad(
        jnp.stack([local(decay_log, heads), local(decay_bias, heads)]),
        ((0, 6), (heads, LANES - 2 * heads)),
    )
    gain_row = out_gain[None, :]
    aux = segment_columns(segments)
    segment_rows = segments.astype(jnp.float32).reshape(-1, 1, CHUNK)
    rank = tensor_rank.astype(jnp.int32).reshape(1)
    gated, *saved = mixer_forward(
        rank, projected, aux, segment_rows, taps, head_rows, gain_row, heads, dk, dv
    )
    attended = lax.psum_scatter(
        product(gated, out_full, 1, 1).astype(jnp.bfloat16),
        "tensor",
        scatter_dimension=0,
        tiled=True,
    ).astype(jnp.float32)
    middle = residual + attended
    second_scale = rms_parts(middle)
    second_normed = middle * second_scale
    ffn_rows = lax.all_gather(
        (second_normed * ffn_gain).astype(jnp.bfloat16), "tensor", axis=0, tiled=True
    )
    cot_rows = lax.all_gather(cotangent, "tensor", axis=0, tiled=True)
    pair = product(ffn_rows, pair_full, 1, 0)
    gate_rows, up_rows = pair[:, :unit_cols], pair[:, unit_cols:]
    sig = jax.nn.sigmoid(gate_rows)
    hidden = (gate_rows * sig * up_rows).astype(jnp.bfloat16)
    grad_hidden = product(cot_rows, down_full, 1, 0)
    grad_pair = jnp.concatenate(
        [
            (grad_hidden * up_rows * sig * (1.0 + gate_rows * (1.0 - sig))).astype(jnp.bfloat16),
            (grad_hidden * gate_rows * sig).astype(jnp.bfloat16),
        ],
        axis=1,
    )
    grad_second = lax.psum_scatter(
        product(grad_pair, pair_full, 1, 1).astype(jnp.bfloat16),
        "tensor",
        scatter_dimension=0,
        tiled=True,
    ).astype(jnp.float32)
    grad_middle = cotangent.astype(jnp.float32) + rms_back(
        grad_second, ffn_gain, second_normed, second_scale
    )
    attn_rows = lax.all_gather(
        grad_middle.astype(jnp.bfloat16), "tensor", axis=0, tiled=True
    )
    ffn_out = lax.psum_scatter(
        product(hidden, down_full, 1, 1).astype(jnp.bfloat16),
        "tensor",
        scatter_dimension=0,
        tiled=True,
    ).astype(jnp.float32)
    layer_output = (middle + ffn_out).astype(jnp.bfloat16)
    grad_gated = product(attn_rows, out_full, 1, 0)
    grad_proj, dtaps, dgain, dhead = mixer_backward(
        rank, projected, aux, segment_rows, taps, head_rows, gain_row, saved, grad_gated, heads, dk, dv
    )
    grad_rest = jnp.concatenate(
        [
            product(attn_rows, gated, 0, 0),
            product(ffn_rows, grad_pair, 0, 0),
            product(cot_rows, hidden, 0, 0),
        ],
        axis=1,
    )
    grad_joined = product(mixer_rows, grad_proj, 0, 0)
    grad_first = lax.psum_scatter(
        product(grad_proj, joined, 1, 1).astype(jnp.bfloat16),
        "tensor",
        scatter_dimension=0,
        tiled=True,
    ).astype(jnp.float32)
    grad_input = grad_middle + rms_back(grad_first, norm_gain, first_normed, first_scale)

    grad_norm_gain = jnp.sum(joined.astype(jnp.float32) * grad_joined, axis=1) / norm_gain
    grad_ffn_gain = (
        jnp.sum(
            pair_full.astype(jnp.float32) * grad_rest[:, cut_out:cut_down], axis=1
        )
        / ffn_gain
    )
    summed_rest = lax.psum_scatter(
        grad_rest.astype(jnp.bfloat16), "dp", scatter_dimension=0, tiled=True
    ).astype(jnp.float32)
    summed_joined = lax.psum_scatter(
        grad_joined.astype(jnp.bfloat16), "dp", scatter_dimension=0, tiled=True
    ).astype(jnp.float32)

    lags = taps.shape[0]
    mine = jnp.concatenate(
        [
            jnp.sum(dtaps.reshape(lags, 8, conv_cols), axis=1).reshape(-1),
            jnp.sum(dhead[0:8], axis=0)[heads : 2 * heads],
            jnp.sum(dhead[8:16], axis=0)[heads : 2 * heads],
        ]
    )
    placed = jnp.where((jnp.arange(ranks) == tensor_rank)[:, None], mine[None, :], 0.0)
    vector = jnp.concatenate(
        [grad_norm_gain, grad_ffn_gain, jnp.sum(dgain, axis=0), placed.reshape(-1)]
    )
    small = lax.psum(vector, ("dp", "tensor"))
    width = norm_gain.shape[0]
    sections = small[2 * width + dv :].reshape(ranks, -1)
    taps_all = sections[:, : lags * conv_cols].reshape(ranks, lags, conv_cols).transpose(1, 0, 2)
    logs_all = sections[:, lags * conv_cols :]

    def columns(lo, hi):
        return summed_joined[:, lo:hi]

    return (
        layer_output,
        grad_input,
        small[:width],
        columns(0, key_cols),
        columns(key_cols, 2 * key_cols),
        columns(2 * key_cols, conv_cols),
        columns(gate_at, small_at),
        columns(small_at, small_at + heads),
        columns(small_at + heads, small_at + 2 * heads),
        taps_all[:, :, :key_cols].reshape(lags, -1),
        taps_all[:, :, key_cols : 2 * key_cols].reshape(lags, -1),
        taps_all[:, :, 2 * key_cols :].reshape(lags, -1),
        logs_all[:, :heads].reshape(-1),
        logs_all[:, heads:].reshape(-1),
        small[2 * width : 2 * width + dv],
        summed_rest[:, :cut_out].T,
        small[width : 2 * width],
        summed_rest[:, cut_out : cut_out + units],
        summed_rest[:, cut_out + unit_cols : cut_out + unit_cols + units],
        summed_rest[:, cut_down : cut_down + units].T,
    )


def solution(mesh):
    in_specs = (
        P(("dp", "tensor"), None),
        P("dp"),
        P(),
        P("dp", "tensor"),
        P("dp", "tensor"),
        P("dp", "tensor"),
        P("dp", "tensor"),
        P("dp", "tensor"),
        P("dp", "tensor"),
        P(),
        P(),
        P(),
        P(),
        P(),
        P(),
        P("tensor", "dp"),
        P(),
        P("dp", "tensor"),
        P("dp", "tensor"),
        P("tensor", "dp"),
        P(("dp", "tensor"), None),
    )
    out_specs = (
        P(("dp", "tensor"), None),
        P(("dp", "tensor"), None),
        P(),
        P("dp", "tensor"),
        P("dp", "tensor"),
        P("dp", "tensor"),
        P("dp", "tensor"),
        P("dp", "tensor"),
        P("dp", "tensor"),
        P(),
        P(),
        P(),
        P(),
        P(),
        P(),
        P("tensor", "dp"),
        P(),
        P("dp", "tensor"),
        P("dp", "tensor"),
        P("tensor", "dp"),
    )
    return jax.shard_map(shards, mesh=mesh, in_specs=in_specs, out_specs=out_specs, check_vma=False)
```

time: 2580 us -> 1130 us (0.44)
  waiting for transfers between devices: 1300 us -> 822 us
  other arithmetic: 481 us -> 24.2 us
  matrix products: 513 us -> 115 us
  local copies, waits for them, and re-layouts: 217 us -> 28.1 us
  Pallas kernels: 0 us -> 112 us
  blocking collectives: 39.5 us -> 0 us
    reduce_scatter x12 -> x6, waiting for transfers between devices: 790 us -> 407 us  [the longest x1 77.7 us: shards(): lax.psum_scatter(product(hidden, down_full, 1, 1).astype(jnp.bfloat16), '...]
    dot_general x214 -> x12, matrix products: 490 us -> 115 us  [product(): lax.dot_general(left, right, (((left_dim,), (right_dim,)), ((), ())), pre...]
    another operation x5 -> x2, other arithmetic: 320 us -> 0.17 us  [the longest x1 0.09 us: segment_columns(): table = jnp.stack(columns, axis=1)]
    pallas_call x0 -> x2, Pallas kernels: none -> 112 us  [the longest x1 66.9 us: mixer_backward(): pl.pallas_call(partial(backward_body, (heads, dk, dv, chunks)), grid_spec...]
    reduce_sum x34 -> x7, other arithmetic: 77.6 us -> 7.01 us  [the longest x2 3.79 us: rms_back(): jnp.mean(scaled * normed, axis=-1, keepdims=True)]
    unnamed x316 -> x98, local copies, waits for them, and re-layouts: 68.9 us -> 14.8 us
    psum x1, waiting for transfers between devices: 130 us -> 83.7 us  [shards(): small = lax.psum(vector, ('dp', 'tensor'))]
    all_gather x4 -> x0, blocking collectives: 39.5 us -> none  [the longest x1 11.8 us: shards(): lax.all_gather(w_query, 'dp', axis=0, tiled=True)]
  transfers between devices with their start and end apart: 25 -> 13, of which waited for: 22 -> 12; matrix products, arithmetic and copies ran while one was open for 26% -> 8% of each run, Pallas kernels for 0% -> 4%
where the time goes in v1:
time: 1130 us; the launch traced here: 1120 us
  waiting for transfers between devices  822 us (73%)
  matrix products  115 us (10%)
  Pallas kernels  112 us (10%)
  local copies, waits for them, and re-layouts  28.1 us (2%)
  other arithmetic  24.2 us (2%)
  between operations  14.9 us (1%)
    dot_general x12, matrix products, product(): lax.dot_general(left, right, (((left_dim,), (right_dim,)), ((), ())), pre...  115 us
    psum x1, waiting for transfers between devices, shards(): small = lax.psum(vector, ('dp', 'tensor'))  83.7 us
    all_gather x1, waiting for transfers between devices, shards(): lax.all_gather((first_normed * norm_gain).astype(jnp.bfloat16), 'tensor',...  82.9 us
    all_gather x1, waiting for transfers between devices, shards(): lax.all_gather((second_normed * ffn_gain).astype(jnp.bfloat16), 'tensor',...  80.3 us
    reduce_scatter x1, waiting for transfers between devices, shards(): lax.psum_scatter(product(hidden, down_full, 1, 1).astype(jnp.bfloat16), '...  77.7 us
    reduce_scatter x1, waiting for transfers between devices, shards(): lax.psum_scatter(product(gated, out_full, 1, 1).astype(jnp.bfloat16), 'te...  75.4 us
    reduce_scatter x1, waiting for transfers between devices, shards(): lax.psum_scatter(product(grad_pair, pair_full, 1, 1).astype(jnp.bfloat16)...  75.4 us
    reduce_scatter x1, waiting for transfers between devices, shards(): lax.psum_scatter(product(grad_proj, joined, 1, 1).astype(jnp.bfloat16), '...  73.6 us
  transfers between devices with their start and end apart: 13, of which 12 were waited for; matrix products, arithmetic and copies ran while one was open for 8% of the time, Pallas kernels for 4%

profile of v1, /device:TPU:0, one launch (start us, length us, event | category | flops | bytes accessed | tf_op | source)
XLA Modules:
  0.0 1117.3 jit_solution(12638916898362251596)
XLA Ops:
  8.9 1.2 concatenate.41
  11.0 1.5 fusion.19
  12.6 1.3 fusion.14
  14.5 0.9 fusion.34
  17.6 29.6 %all-gather.9.cloned.1.call-done = bf16[1024,1664]{1,0:T(8,128)(2,1)} async-done(((bf16[128,1664]{1,0:T(8,128)(2,1)}), bf16[1024,1664]{1,0:T(8,128)(2,1)}) %all-gather.9.cloned.1.call-update) | async-done | bytes 3407888 | tf_op jit(solution)/shard_map/all_gather | solution.py:594
  47.2 82.9 %all-gather.7.cloned.1.call-done = bf16[2048,1024]{1,0:T(8,128)(2,1)} async-done(((bf16[512,1024]{1,0:T(8,128)(2,1)}), bf16[2048,1024]{1,0:T(8,128)(2,1)}) %all-gather.7.cloned.1.call-update) | async-done | bytes 4194320 | tf_op jit(solution)/shard_map/all_gather | solution.py:622
  130.2 13.4 %fusion.60.proj_ref.before_ref = f32[2048,1664]{1,0:T(8,128)} fusion(bf16[2048,1024]{1,0:T(8,128)(2,1)} %all-gather.7.cloned.1.call-done, bf16[1024,1664]{1,0:T(8,128)(2,1)} %all-gather.9.cloned.1.call-done), kind=kOutput, calls=%fused_computation.125 | convolution fusion | flops 6979321856 | bytes 21233664 | tf_op jit(solution)/shard_map/dot_general | solution.py:553
  143.5 45.4 %mixer_forward.1 = (bf16[2048,512]{1,0:T(8,128)(2,1)S(1)}, f32[2048,512]{1,0:T(8,128)}, f32[2048,512]{1,0:T(8,128)}, f32[16,128,512]{2,1,0:T(8,128)}, f32[2048,256]{1,0:T(8,128)S(1)}) custom-call(s32[1]{0:T(128)} %bitcast.rank_ref, f32[2048,1664]{1,0:T(8,128)} %fusion.60.proj_ref.before_ref, f32[2048,128]{1,0:T(8,128)S(1)} %pad.27.aux_ref, ...), custom_call_target="tpu_custom_call" | custom-call | flops 80000000000 | bytes 40894464 | tf_op jit(solution)/shard_map/mixer_forward/pallas_call | solution.py:415
  189.0 1.3 copy-done.5
  190.3 6.4 convolution_convert_fusion
  196.7 75.4 %reduce-scatter.7.cloned.1.call-done = bf16[512,1024]{1,0:T(8,128)(2,1)} async-done(((bf16[2048,1024]{1,0:T(8,128)(2,1)}), bf16[512,1024]{1,0:T(8,128)(2,1)}) %reduce-scatter.7.cloned.1.call-update) | async-done | bytes 1048592 | tf_op jit(solution)/shard_map/reduce_scatter | solution.py:645
  272.2 1.6 multiply_reduce_fusion.3
  273.8 2.6 multiply_convert_fusion.1
  277.6 80.3 %all-gather.13.cloned.1.call-done = bf16[2048,1024]{1,0:T(8,128)(2,1)} async-done(((bf16[512,1024]{1,0:T(8,128)(2,1)}), bf16[2048,1024]{1,0:T(8,128)(2,1)}) %all-gather.13.cloned.1.call-update) | async-done | bytes 4194320 | tf_op jit(solution)/shard_map/all_gather | solution.py:654
  357.9 12.3 %fusion.12 = f32[2048,1536]{0,1:T(8,128)} fusion(bf16[2048,1024]{1,0:T(8,128)(2,1)} %all-gather.13.cloned.1.call-done, bf16[1024,2816]{1,0:T(8,128)(2,1)} %all-gather.11.cloned.1.call-done), kind=kOutput, calls=%fused_computation.26 | convolution fusion | flops 6442450944 | bytes 19922944 | tf_op jit(solution)/shard_map/dot_general | solution.py:553
  370.1 68.6 %all-gather.15.cloned.1.call-done = bf16[2048,1024]{1,0:T(8,128)(2,1)} async-done(((bf16[512,1024]{1,0:T(8,128)(2,1)}), bf16[2048,1024]{1,0:T(8,128)(2,1)}) %all-gather.15.cloned.1.call-update) | async-done | bytes 4194320 | tf_op jit(solution)/shard_map/all_gather | solution.py:657
  438.7 12.0 %fusion.2 = (bf16[2048,768]{0,1:T(8,128)(2,1)S(1)}, bf16[2048,768]{0,1:T(8,128)(2,1)S(1)}, bf16[2048,768]{0,1:T(8,128)(2,1)}) fusion(f32[2048,1536]{0,1:T(8,128)} %fusion.12, bf16[2048,1024]{1,0:T(8,128)(2,1)} %all-gather.15.cloned.1.call-done, bf16[1024,2816]{1,0:T(8,128)(2,1)} %all-gather.11.cloned.1.call-done), kind=kOutput, calls=%fused_computation.6 | convolution fusion | flops 3246391296 | bytes 27787264 | tf_op jit(solution)/shard_map/dot_general | solution.py:553
  450.8 1.7 copy-done.38
  452.4 1.0 copy-done.39
  453.4 10.2 fusion.7
  463.6 75.4 %reduce-scatter.11.cloned.1.call-done = bf16[512,1024]{1,0:T(8,128)(2,1)} async-done(((bf16[2048,1024]{1,0:T(8,128)(2,1)}), bf16[512,1024]{1,0:T(8,128)(2,1)}) %reduce-scatter.11.cloned.1.call-update) | async-done | bytes 1048592 | tf_op jit(solution)/shard_map/reduce_scatter | solution.py:670
  539.1 2.0 multiply_reduce_fusion.2
  541.1 1.8 fusion.48
  543.7 12.1 %fusion.50 = (bf16[1024,1536]{1,0:T(8,128)(2,1)}, f32[1024]{0:T(1024)S(1)}) fusion(bf16[1024,2816]{1,0:T(8,128)(2,1)} %all-gather.11.cloned.1.call-done, bf16[2048,1024]{1,0:T(8,128)(2,1)} %all-gather.13.cloned.1.call-done, bf16[2048,768]{0,1:T(8,128)(2,1)} %copy-done.39, bf16[2048,768]{0,1:T(8,128)(2,1)} %copy-done.38), kind=kOutput, calls=%fused_computation.115 | convolution fusion | flops 6461324288 | bytes 16781312 | tf_op jit(solution)/shard_map/dot_general | solution.py:553
  556.5 67.9 %all-gather.17.cloned.1.call-done = bf16[2048,1024]{1,0:T(8,128)(2,1)} async-done(((bf16[512,1024]{1,0:T(8,128)(2,1)}), bf16[2048,1024]{1,0:T(8,128)(2,1)}) %all-gather.17.cloned.1.call-update) | async-done | bytes 4194320 | tf_op jit(solution)/shard_map/all_gather | solution.py:679
  624.4 6.8 fusion.30.grad_ref
  631.2 66.9 %mixer_backward.1 = (bf16[2048,1664]{1,0:T(8,128)(2,1)}, f32[32,1024]{1,0:T(8,128)S(1)}, f32[8,256]{1,0:T(8,128)S(1)}, f32[16,128]{1,0:T(8,128)S(1)}) custom-call(s32[1]{0:T(128)} %bitcast.rank_ref, f32[2048,1664]{1,0:T(8,128)} %fusion.60.proj_ref.before_ref, f32[2048,1664]{1,0:T(8,128)} %fusion.60.proj_ref.before_ref, f32[2048,128]{1,0:T(8,128)S(1)} %pad.27.aux_ref, ...), custom_call_target="tpu_custom_call" | custom-call | flops 160000000000 | bytes 54525952 | tf_op jit(solution)/shard_map/mixer_backward/pallas_call | solution.py:471
  698.6 13.7 %fusion.49 = (bf16[1024,1664]{1,0:T(8,128)(2,1)}, f32[1024]{0:T(1024)S(1)}) fusion(bf16[1024,1664]{1,0:T(8,128)(2,1)} %all-gather.9.cloned.1.call-done, bf16[2048,1024]{1,0:T(8,128)(2,1)} %all-gather.7.cloned.1.call-done, bf16[2048,1664]{1,0:T(8,128)(2,1)} %get-tuple-element.34), kind=kOutput, calls=%fused_computation.114 | convolution fusion | flops 6986136576 | bytes 17829888 | tf_op jit(solution)/shard_map/dot_general | solution.py:553
  713.7 12.3 %convolution_convert_fusion.2 = bf16[2048,1024]{1,0:T(8,128)(2,1)} fusion(bf16[2048,1664]{1,0:T(8,128)(2,1)} %get-tuple-element.34, bf16[1024,1664]{1,0:T(8,128)(2,1)} %all-gather.9.cloned.1.call-done), kind=kOutput, calls=%fused_computation.18 | convolution fusion | flops 6981419008 | bytes 14417920 | tf_op jit(solution)/shard_map/dot_general | solution.py:553
  726.1 1.8 copy-done.37
  727.9 6.4 convolution_convert_fusion.1
  734.7 6.8 fusion.21
  741.5 2.4 convolution_convert_fusion.4
  743.9 2.8 pad_maximum_fusion.1
  746.8 83.7 %all-reduce.12.cloned.1.call-done = f32[18704]{0:T(1024)} async-done(((f32[18704]{0:T(1024)}), f32[18704]{0:T(1024)}) %all-reduce.12.cloned.1.call-update) | async-done | bytes 74832 | tf_op jit(solution)/shard_map/psum | solution.py:736
  834.7 1.2 slice.173
  836.0 1.3 fusion.55
  837.2 46.1 %reduce-scatter.15.cloned.1.call-done = bf16[128,1664]{1,0:T(8,128)(2,1)} async-done(((bf16[1024,1664]{1,0:T(8,128)(2,1)}), bf16[128,1664]{1,0:T(8,128)(2,1)}) %reduce-scatter.15.cloned.1.call-update) | async-done | bytes 426000 | tf_op jit(solution)/shard_map/reduce_scatter | solution.py:720
  883.3 0.9 fusion.52
  885.5 1.6 fusion.54
  887.1 1.8 fusion.53
  888.9 73.6 %reduce-scatter.13.cloned.1.call-done = bf16[512,1024]{1,0:T(8,128)(2,1)} async-done(((bf16[2048,1024]{1,0:T(8,128)(2,1)}), bf16[512,1024]{1,0:T(8,128)(2,1)}) %reduce-scatter.13.cloned.1.call-update) | async-done | bytes 1048592 | tf_op jit(solution)/shard_map/reduce_scatter | solution.py:702
  962.5 1.8 fusion.15
  964.3 77.7 %reduce-scatter.9.cloned.1.call-done = bf16[512,1024]{1,0:T(8,128)(2,1)} async-done(((bf16[2048,1024]{1,0:T(8,128)(2,1)}), bf16[512,1024]{1,0:T(8,128)(2,1)}) %reduce-scatter.9.cloned.1.call-update) | async-done | bytes 1048592 | tf_op jit(solution)/shard_map/reduce_scatter | solution.py:682
  1042.0 4.4 fusion.18
  1046.4 59.0 %reduce-scatter.17.cloned.1.call-done = bf16[128,2816]{1,0:T(8,128)(2,1)} async-done(((bf16[1024,2816]{1,0:T(8,128)(2,1)}), bf16[128,2816]{1,0:T(8,128)(2,1)}) %reduce-scatter.17.cloned.1.call-update) | async-done | bytes 720912 | tf_op jit(solution)/shard_map/reduce_scatter | solution.py:717
  1105.4 1.3 convert_element_type.111
  1106.7 0.9 copy.119
  (161 shorter events, 18.3 us)
Async XLA Ops:
  7.2 9.7 copy-start
  7.2 5.3 copy-start.7
  7.2 5.3 copy-start.24
  7.2 40.0 %all-gather.9.cloned.1.call-start = ((), (), s32[]{:S(2)}) async-start(), calls=%async_computation.7 | async-start | bytes 3833856 | tf_op jit(solution)/shard_map/all_gather | solution.py:594
  8.9 5.0 copy-start.18
  10.1 4.0 copy-start.19
  10.1 4.1 copy-start.20
  10.1 4.3 copy-start.21
  11.0 119.2 %all-gather.7.cloned.1.call-start = ((), (), s32[]{:S(2)}) async-start(), calls=%async_computation.6 | async-start | bytes 5242880 | tf_op jit(solution)/shard_map/all_gather | solution.py:622
  12.5 2.9 copy-start.28
  12.6 3.0 copy-start.17
  13.8 2.8 copy-start.34
  13.8 2.8 copy-start.35
  13.9 176.4 %all-gather.11.cloned.1.call-start = ((), (), s32[]{:S(2)}) async-start(), calls=%async_computation.8 | async-start | bytes 6488064 | tf_op jit(solution)/shard_map/all_gather | solution.py:603
  15.5 256.7 %reduce-scatter.7.cloned.1.call-start = ((), (), s32[]{:S(2)}) async-start(), calls=%async_computation.9 | async-start | bytes 5242880 | tf_op jit(solution)/shard_map/reduce_scatter | solution.py:645
  17.6 125.9 %copy-start.2 = (f32[256]{0:T(256)S(1)}, f32[256]{0:T(256)}, u32[]{:S(2)}) copy-start(f32[256]{0:T(256)} %param.35) | copy-start | bytes 3076
  190.3 6.4 copy-start.3
  196.7 75.5 %copy-start.8 = (bf16[512,1024]{1,0:T(8,128)(2,1)S(1)}, bf16[512,1024]{1,0:T(8,128)(2,1)}, u32[]{:S(2)}) copy-start(bf16[512,1024]{1,0:T(8,128)(2,1)} %param.21) | copy-start | bytes 3145732
  196.7 77.1 %copy-start.22 = (f32[1024]{0:T(1024)S(1)}, f32[1024]{0:T(1024)}, u32[]{:S(2)}) copy-start(f32[1024]{0:T(1024)} %param.37) | copy-start | bytes 12292
  196.7 161.2 %all-gather.13.cloned.1.call-start = ((), (), s32[]{:S(2)}) async-start(), calls=%async_computation.10 | async-start | bytes 5242880 | tf_op jit(solution)/shard_map/all_gather | solution.py:654
  273.8 267.3 %copy-start.26 = (f32[512]{0:T(512)}, f32[512]{0:T(512)S(1)}, u32[]{:S(2)}) copy-start(f32[512]{0:T(512)S(1)} %add_rsqrt_fusion) | copy-start | bytes 6148
  276.5 162.2 %all-gather.15.cloned.1.call-start = ((), (), s32[]{:S(2)}) async-start(), calls=%async_computation.12 | async-start | bytes 5242880 | tf_op jit(solution)/shard_map/all_gather | solution.py:657
  277.0 262.0 %reduce-scatter.11.cloned.1.call-start = ((), (), s32[]{:S(2)}) async-start(), calls=%async_computation.13 | async-start | bytes 5242880 | tf_op jit(solution)/shard_map/reduce_scatter | solution.py:670
  450.8 2.6 copy-start.39
  463.6 75.5 %copy-start.10 = (bf16[512,1024]{1,0:T(8,128)(2,1)S(1)}, bf16[512,1024]{1,0:T(8,128)(2,1)}, u32[]{:S(2)}) copy-start(bf16[512,1024]{1,0:T(8,128)(2,1)} %reduce-scatter.7.cloned.1.call-done) | copy-start | bytes 3145732
  463.6 160.8 %all-gather.17.cloned.1.call-start = ((), (), s32[]{:S(2)}) async-start(), calls=%async_computation.14 | async-start | bytes 5242880 | tf_op jit(solution)/shard_map/all_gather | solution.py:679
  539.0 2.1 copy-start.14
  543.0 287.6 %all-reduce.12.cloned.1.call-start = ((), (), s32[]{:S(2)}) async-start(), calls=%async_computation.16 | async-start | bytes 155648 | tf_op jit(solution)/shard_map/psum | solution.py:736
  556.5 74.7 %copy-start.6 = (f32[2048,256]{1,0:T(8,128)S(1)}, f32[2048,256]{1,0:T(8,128)}, u32[]{:S(2)}) copy-start(f32[2048,256]{1,0:T(8,128)} %copy-done.5) | copy-start | bytes 6291460
  631.2 67.2 %copy-start.33 = (pred[4]{0:T(512)(128)(4,1)S(1)}, pred[4]{0:T(512)(128)(4,1)}, u32[]{:S(2)}) copy-start(pred[4]{0:T(512)(128)(4,1)} %iota_compare_fusion.8) | copy-start | bytes 16
  698.6 13.8 %copy-start.25 = (f32[1024]{0:T(1024)S(1)}, f32[1024]{0:T(1024)}, u32[]{:S(2)}) copy-start(f32[1024]{0:T(1024)} %param.23) | copy-start | bytes 12292
  698.6 13.8 %copy-start.32 = (f32[1024]{0:T(1024)S(1)}, f32[1024]{0:T(1024)}, u32[]{:S(2)}) copy-start(f32[1024]{0:T(1024)} %div.27) | copy-start | bytes 12292
  713.0 170.3 %reduce-scatter.15.cloned.1.call-start = ((), (), s32[]{:S(2)}) async-start(), calls=%async_computation.17 | async-start | bytes 3833856 | tf_op jit(solution)/shard_map/reduce_scatter | solution.py:720
  713.6 248.9 %reduce-scatter.13.cloned.1.call-start = ((), (), s32[]{:S(2)}) async-start(), calls=%async_computation.15 | async-start | bytes 5242880 | tf_op jit(solution)/shard_map/reduce_scatter | solution.py:702
  726.0 316.0 %reduce-scatter.9.cloned.1.call-start = ((), (), s32[]{:S(2)}) async-start(), calls=%async_computation.11 | async-start | bytes 5242880 | tf_op jit(solution)/shard_map/reduce_scatter | solution.py:682
  734.3 7.2 copy-start.4
  734.3 371.0 %reduce-scatter.17.cloned.1.call-start = ((), (), s32[]{:S(2)}) async-start(), calls=%async_computation.18 | async-start | bytes 6488064 | tf_op jit(solution)/shard_map/reduce_scatter | solution.py:717
  734.6 6.9 copy-start.36
  741.5 2.4 copy-start.16
  746.8 215.8 %copy-start.9 = (bf16[512,1024]{1,0:T(8,128)(2,1)S(1)}, bf16[512,1024]{1,0:T(8,128)(2,1)}, u32[]{:S(2)}) copy-start(bf16[512,1024]{1,0:T(8,128)(2,1)} %param.21) | copy-start | bytes 3145732
  746.8 215.8 %copy-start.29 = (f32[512]{0:T(512)S(1)}, f32[512]{0:T(512)}, u32[]{:S(2)}) copy-start(f32[512]{0:T(512)} %copy-done.28) | copy-start | bytes 6148
  746.8 295.2 %copy-start.11 = (bf16[512,1024]{1,0:T(8,128)(2,1)S(1)}, bf16[512,1024]{1,0:T(8,128)(2,1)}, u32[]{:S(2)}) copy-start(bf16[512,1024]{1,0:T(8,128)(2,1)} %reduce-scatter.7.cloned.1.call-done) | copy-start | bytes 3145732
  746.8 295.2 %copy-start.13 = (bf16[512,1024]{1,0:T(8,128)(2,1)S(1)}, bf16[512,1024]{1,0:T(8,128)(2,1)}, u32[]{:S(2)}) copy-start(bf16[512,1024]{1,0:T(8,128)(2,1)} %reduce-scatter.11.cloned.1.call-done) | copy-start | bytes 3145732
  746.8 295.2 %copy-start.23 = (f32[1024]{0:T(1024)S(1)}, f32[1024]{0:T(1024)}, u32[]{:S(2)}) copy-start(f32[1024]{0:T(1024)} %param.37) | copy-start | bytes 12292
  746.8 295.2 %copy-start.27 = (f32[512]{0:T(512)S(1)}, f32[512]{0:T(512)}, u32[]{:S(2)}) copy-start(f32[512]{0:T(512)} %copy-done.26) | copy-start | bytes 6148
  746.8 295.2 %copy-start.31 = (f32[512]{0:T(512)S(1)}, f32[512]{0:T(512)}, u32[]{:S(2)}) copy-start(f32[512]{0:T(512)} %copy-done.30) | copy-start | bytes 6148
  1105.4 3.1 copy-start.15
  1105.4 5.0 copy-start.1
  (5 other events, 8.8 us)
Sparse Core Ops, SparseCore 0:
  11.1 36.1 all-gather.8
  49.4 80.7 all-gather.6
  132.1 41.8 all-gather.10
  196.8 75.2 reduce-scatter.6
  276.6 81.2 all-gather.12
  359.4 79.2 all-gather.14
  463.7 75.2 reduce-scatter.10
  543.1 81.2 all-gather.16
  713.1 117.3 all-reduce.11
  833.9 49.3 reduce-scatter.14
  885.7 76.7 reduce-scatter.12
  964.6 77.2 reduce-scatter.8
  1045.8 59.5 reduce-scatter.16

commit v2 on v1

--- a/solution.py
+++ b/solution.py
@@ -4,6 +4,7 @@
 import jax.numpy as jnp
 from jax import lax
 from jax.experimental import pallas as pl
+from jax.experimental.layout import Layout, with_layout_constraint
 from jax.experimental.pallas import tpu as pltpu
 from jax.sharding import PartitionSpec as P
 
@@ -397,7 +398,7 @@
     later_ref[count : count + 8, :] = later_ref[0:8, :]
 
 
-FORWARD_CHUNKS = 2
+FORWARD_CHUNKS = 4
 BACKWARD_CHUNKS = 1
 
 
@@ -405,20 +406,28 @@
     return pl.BlockSpec(array.shape, lambda step, rank: (0,) * array.ndim)
 
 
-def mixer_forward(rank, proj, aux, segment_rows, taps, head_rows, gain, heads, dk, dv):
+def turned_place(blocks, ranks):
+    return lambda place, rank: lax.rem(place - rank[0] * (blocks // ranks) + blocks, blocks)
+
+
+def mixer_forward(rank, proj, aux, segment_rows, taps, head_rows, gain, heads, dk, dv, ranks):
     length, width = proj.shape
     chunks = FORWARD_CHUNKS
     count = chunks * CHUNK
     steps = length // count
     conv_cols = heads * (2 * dk + dv)
+    turned = turned_place(steps, ranks)
     rows = lambda cols: pl.BlockSpec((count, cols), lambda step, rank: (step, 0))
+    turned_rows = lambda cols: pl.BlockSpec(
+        (count, cols), lambda step, rank: (turned(step, rank), 0)
+    )
     return pl.pallas_call(
         partial(forward_body, (heads, dk, dv, chunks)),
         grid_spec=pltpu.PrefetchScalarGridSpec(
             num_scalar_prefetch=1,
             grid=(steps,),
             in_specs=[
-                rows(width),
+                turned_rows(width),
                 rows(LANES),
                 pl.BlockSpec((chunks, 1, CHUNK), lambda step, rank: (step, 0, 0)),
                 whole_block(taps),
@@ -426,7 +435,7 @@
                 whole_block(gain),
             ],
             out_specs=[
-                rows(heads * dv),
+                turned_rows(heads * dv),
                 rows(heads * dv),
                 rows(heads * dv),
                 pl.BlockSpec((chunks, dk, heads * dv), lambda step, rank: (step, 0, 0)),
@@ -453,7 +462,7 @@
 
 
 def mixer_backward(
-    rank, proj, aux, segment_rows, taps, head_rows, gain, saved, grad, heads, dk, dv
+    rank, proj, aux, segment_rows, taps, head_rows, gain, saved, grad, heads, dk, dv, ranks
 ):
     length, width = proj.shape
     chunks = BACKWARD_CHUNKS
@@ -462,10 +471,19 @@
     conv_cols = heads * (2 * dk + dv)
     out, fresh, states, inverses = saved
     place = lambda step: steps - 1 - step
+    turned = turned_place(steps, ranks)
     rows = lambda cols: pl.BlockSpec((count, cols), lambda step, rank: (place(step), 0))
+    turned_rows = lambda cols: pl.BlockSpec(
+        (count, cols), lambda step, rank: (turned(place(step), rank), 0)
+    )
     lags = taps.shape[0]
+    turned_eights = turned_place(length // 8, ranks)
     before = pl.BlockSpec(
-        (8, width), lambda step, rank: (jnp.maximum(place(step) * (count // 8) - 1, 0), 0)
+        (8, width),
+        lambda step, rank: (
+            turned_eights(jnp.maximum(place(step) * (count // 8) - 1, 0), rank),
+            0,
+        ),
     )
     whole = lambda shape: pl.BlockSpec(shape, lambda step, rank: (0, 0))
     return pl.pallas_call(
@@ -474,7 +492,7 @@
             num_scalar_prefetch=1,
             grid=(steps,),
             in_specs=[
-                rows(width),
+                turned_rows(width),
                 before,
                 rows(LANES),
                 pl.BlockSpec((chunks, 1, CHUNK), lambda step, rank: (place(step), 0, 0)),
@@ -485,10 +503,10 @@
                 rows(heads * dv),
                 pl.BlockSpec((chunks, dk, heads * dv), lambda step, rank: (place(step), 0, 0)),
                 rows(heads * CHUNK),
-                rows(heads * dv),
+                turned_rows(heads * dv),
             ],
             out_specs=[
-                rows(width),
+                turned_rows(width),
                 whole((8 * lags, conv_cols)),
                 whole((8, dv)),
                 whole((16, LANES)),
@@ -536,8 +554,248 @@
     return jnp.pad(table, ((0, 0), (0, LANES - len(columns))))
 
 
-def rms_parts(values):
-    return lax.rsqrt(jnp.mean(values * values, axis=-1, keepdims=True) + TINY)
+UNIT_TILE = 256
+
+
+def ffn_body(
+    sizes,
+    rows_ref,
+    cot_ref,
+    gated_ref,
+    gain_ref,
+    *refs,
+):
+    ranks, tiles, spans = sizes
+    weight_refs = [refs[at * 4 : at * 4 + 4] for at in range(len(spans))]
+    refs = refs[4 * len(spans) :]
+    output_ref, dmiddle_ref, dgated_ref, dgain_ref = refs[:4]
+    grads_refs = refs[4:6]
+    ffn_steps(
+        ranks,
+        tiles,
+        spans,
+        rows_ref,
+        cot_ref,
+        gated_ref,
+        gain_ref,
+        weight_refs,
+        output_ref,
+        dmiddle_ref,
+        dgated_ref,
+        dgain_ref,
+        grads_refs,
+        *refs[6:],
+    )
+
+
+def ffn_steps(
+    ranks,
+    tiles,
+    spans,
+    rows_ref,
+    cot_ref,
+    gated_ref,
+    gain_ref,
+    weight_refs,
+    output_ref,
+    dmiddle_ref,
+    dgated_ref,
+    dgain_ref,
+    grads_refs,
+    middle_ref,
+    total_ref,
+    dsecond_ref,
+    second_ref,
+    second_turned_ref,
+    cot_turned_ref,
+    dattn_ref,
+    dattn_turned_ref,
+):
+    step = pl.program_id(0)
+    tokens, width = rows_ref.shape
+    begin, end = ranks, ranks + ranks * tiles
+    slabs = [slice(at, at + CHUNK) for at in range(0, tokens, CHUNK)]
+
+    def flat(ref):
+        return ref[...].reshape(width, ref.shape[-1])
+
+    @pl.when(step == 0)
+    def start():
+        middle_ref[...] = rows_ref[...].astype(jnp.float32)
+
+    def attend(w_out_ref):
+        middle_ref[...] += contract(gated_ref[...], flat(w_out_ref), (1, 1))
+
+    for (low, high), held in zip(spans, weight_refs):
+        pl.when(jnp.logical_and(step >= low, step < high))(partial(attend, held[0]))
+
+    @pl.when(step == begin)
+    def second_norm():
+        for slab in slabs:
+            middle = middle_ref[slab, :]
+            scale = lax.rsqrt(jnp.mean(middle * middle, axis=1, keepdims=True) + TINY)
+            second = middle * scale * gain_ref[...]
+            second_ref[slab, :] = second.astype(jnp.bfloat16)
+            second_turned_ref[:, slab] = jnp.transpose(second).astype(jnp.bfloat16)
+            cot_turned_ref[:, slab] = jnp.transpose(
+                cot_ref[slab, :].astype(jnp.float32)
+            ).astype(jnp.bfloat16)
+        total_ref[...] = jnp.zeros(total_ref.shape, jnp.float32)
+        dsecond_ref[...] = jnp.zeros(dsecond_ref.shape, jnp.float32)
+
+    def units(w_gate_ref, w_up_ref, w_down_ref, grads_ref):
+        w_gate, w_up, w_down = flat(w_gate_ref), flat(w_up_ref), flat(w_down_ref)
+        second = second_ref[...]
+        gate = contract(second, w_gate, (1, 0))
+        up = contract(second, w_up, (1, 0))
+        dhidden = contract(cot_ref[...], w_down, (1, 0))
+        sig = sigmoid(gate)
+        active = gate * sig
+        hidden = (active * up).astype(jnp.bfloat16)
+        dgate = (dhidden * up * (sig * (1.0 + gate * (1.0 - sig)))).astype(jnp.bfloat16)
+        dup = (dhidden * active).astype(jnp.bfloat16)
+        total_ref[...] += contract(hidden, w_down, (1, 1))
+        dsecond_ref[...] += contract(dgate, w_gate, (1, 1)) + contract(dup, w_up, (1, 1))
+        turned = second_turned_ref[...]
+        tile = gate.shape[1]
+        grads_ref[:, :tile] = contract(turned, dgate, (1, 0)).astype(jnp.bfloat16)
+        grads_ref[:, tile : 2 * tile] = contract(turned, dup, (1, 0)).astype(jnp.bfloat16)
+        grads_ref[:, 2 * tile :] = contract(cot_turned_ref[...], hidden, (1, 0)).astype(
+            jnp.bfloat16
+        )
+
+    for (low, high), held in zip(spans, weight_refs):
+        grads_ref = grads_refs[0 if low == 0 else 1]
+        pl.when(jnp.logical_and(step >= begin + low * tiles, step < begin + high * tiles))(
+            partial(units, *held[1:], grads_ref)
+        )
+
+    @pl.when(step == end)
+    def second_norm_back():
+        dgain_ref[...] = jnp.zeros(dgain_ref.shape, jnp.float32)
+        for slab in slabs:
+            middle = middle_ref[slab, :]
+            output_ref[slab, :] = (middle + total_ref[slab, :]).astype(jnp.bfloat16)
+            scale = lax.rsqrt(jnp.mean(middle * middle, axis=1, keepdims=True) + TINY)
+            normed = middle * scale
+            dsecond = dsecond_ref[slab, :]
+            dgain_ref[...] += jnp.sum((dsecond * normed).reshape(CHUNK // 8, 8, width), axis=0)
+            scaled = dsecond * gain_ref[...]
+            dmiddle = cot_ref[slab, :].astype(jnp.float32) + scale * (
+                scaled - normed * jnp.mean(scaled * normed, axis=1, keepdims=True)
+            )
+            dmiddle_ref[slab, :] = dmiddle
+            dattn_ref[slab, :] = dmiddle.astype(jnp.bfloat16)
+            dattn_turned_ref[:, slab] = jnp.transpose(dmiddle).astype(jnp.bfloat16)
+
+    def attend_back(w_out_ref):
+        dgated_ref[...] = contract(dattn_ref[...], flat(w_out_ref), (1, 0)).astype(
+            dgated_ref.dtype
+        )
+        cols = gated_ref.shape[1]
+        last_ref = grads_refs[-1]
+        last_ref[:, :cols] = contract(dattn_turned_ref[...], gated_ref[...], (1, 0)).astype(
+            jnp.bfloat16
+        )
+        last_ref[:, cols:] = jnp.zeros((last_ref.shape[0], last_ref.shape[1] - cols), jnp.bfloat16)
+
+    for (low, high), held in zip(spans, weight_refs):
+        pl.when(jnp.logical_and(step >= end + low, step < end + high))(
+            partial(attend_back, held[0])
+        )
+
+
+def ffn_block(rows, cot, gated, weights, spans, gain, value_cols, unit_cols):
+    tokens, width = rows.shape
+    ranks = spans[-1][1]
+    grad_spans = [(0, 1), (1, ranks)]
+    tiles = unit_cols // UNIT_TILE
+    begin, end = ranks, ranks + ranks * tiles
+    group = 3 * UNIT_TILE
+
+    def edge(step):
+        return jnp.where(step < end, jnp.minimum(step, ranks - 1), step - end)
+
+    def out_spec(array, low, high):
+        return pl.BlockSpec(
+            (array.shape[0], 1, array.shape[2], value_cols),
+            lambda step: (0, jnp.clip(edge(step) - low, 0, high - low - 1), 0, 0),
+        )
+
+    def tile_at(step, low, high):
+        return jnp.clip(step - begin - low * tiles, 0, (high - low) * tiles - 1)
+
+    def unit_spec(array, low, high, kind):
+        first = value_cols // UNIT_TILE + kind * tiles
+
+        def place(step):
+            tile = tile_at(step, low, high)
+            return (0, tile // tiles, 0, first + lax.rem(tile, tiles))
+
+        return pl.BlockSpec((array.shape[0], 1, array.shape[2], UNIT_TILE), place)
+
+    def grads_at(step, low, high):
+        place = tile_at(step, low, high)
+        return jnp.where(step < end, place, place + 1 + step - end) if high == ranks else place
+
+    whole = lambda shape: pl.BlockSpec(shape, lambda step: (0,) * len(shape))
+    bf, f32 = jnp.bfloat16, jnp.float32
+    weight_specs, weight_args = [], []
+    for array, (low, high) in zip(weights, spans):
+        weight_specs.append(out_spec(array, low, high))
+        weight_specs += [unit_spec(array, low, high, kind) for kind in range(3)]
+        weight_args += [array] * 4
+    late = lambda step: (0, jnp.maximum(step - end, 0))
+    return pl.pallas_call(
+        partial(ffn_body, (ranks, tiles, tuple(spans))),
+        grid=(end + ranks,),
+        in_specs=[
+            whole(rows.shape),
+            whole(cot.shape),
+            pl.BlockSpec((tokens, value_cols), lambda step: (0, edge(step))),
+            whole(gain.shape),
+            *weight_specs,
+        ],
+        out_specs=[
+            whole(rows.shape),
+            whole(rows.shape),
+            pl.BlockSpec((tokens, value_cols), late),
+            whole((8, width)),
+        ]
+        + [
+            pl.BlockSpec(
+                (width, group), lambda step, low=low, high=high: (0, grads_at(step, low, high))
+            )
+            for low, high in grad_spans
+        ],
+        scratch_shapes=[
+            pltpu.VMEM((tokens, width), f32),
+            pltpu.VMEM((tokens, width), f32),
+            pltpu.VMEM((tokens, width), f32),
+            pltpu.VMEM((tokens, width), bf),
+            pltpu.VMEM((width, tokens), bf),
+            pltpu.VMEM((width, tokens), bf),
+            pltpu.VMEM((tokens, width), bf),
+            pltpu.VMEM((width, tokens), bf),
+        ],
+        out_shape=[
+            jax.ShapeDtypeStruct(rows.shape, bf),
+            jax.ShapeDtypeStruct(rows.shape, f32),
+            jax.ShapeDtypeStruct((tokens, ranks * value_cols), bf),
+            jax.ShapeDtypeStruct((8, width), f32),
+        ]
+        + [
+            jax.ShapeDtypeStruct(
+                (width, ((high - low) * tiles + (ranks if high == ranks else 0)) * group), bf
+            )
+            for low, high in grad_spans
+        ],
+        compiler_params=pltpu.CompilerParams(vmem_limit_bytes=60 * 2**20),
+        cost_estimate=pl.CostEstimate(
+            flops=35 * 10**9, bytes_accessed=60 * 10**6, transcendentals=0
+        ),
+        name="ffn_block",
+    )(rows, cot, gated, gain, *weight_args)
 
 
 def rms_back(grad, gain, normed, scale):
@@ -557,6 +815,45 @@
 
 def up_to(size, unit):
     return -(-size // unit) * unit
+
+
+def fetched(block, ahead, ranks):
+    return lax.ppermute(block, "tensor", [((i + ahead) % ranks, i) for i in range(ranks)])
+
+
+def exchanged(blocks):
+    ranks = len(blocks)
+    result = [blocks[0]] + [None] * (ranks - 1)
+    for ahead in range(1, ranks):
+        result[ranks - ahead] = lax.ppermute(
+            blocks[ahead], "tensor", [(i, (i + ahead) % ranks) for i in range(ranks)]
+        )
+    return result
+
+
+def stacked_body(*refs):
+    for at, ref in enumerate(refs[1:-1]):
+        refs[-1][at] = ref[...]
+
+
+def stacked_after(blocks, earlier):
+    return pl.pallas_call(
+        stacked_body,
+        in_specs=[pl.BlockSpec(memory_space=pl.ANY)]
+        + [pl.BlockSpec(memory_space=pltpu.VMEM)] * len(blocks),
+        out_specs=pl.BlockSpec(memory_space=pltpu.VMEM),
+        out_shape=jax.ShapeDtypeStruct((len(blocks), *blocks[0].shape), blocks[0].dtype),
+        name="stacked_after",
+    )(earlier, *blocks)
+
+
+def summed_over(vector, axis):
+    size = lax.axis_size(axis)
+    apart = 1
+    while apart < size:
+        vector = vector + lax.ppermute(vector, axis, [(i, i ^ apart) for i in range(size)])
+        apart *= 2
+    return vector
 
 
 def shards(
@@ -587,7 +884,8 @@
     key_cols, value_cols, heads = w_query.shape[1], w_value.shape[1], w_beta.shape[1]
     dk, dv = key_cols // heads, value_cols // heads
     units = w_gate.shape[1]
-    unit_cols = up_to(units, 256)
+    unit_cols = up_to(units, UNIT_TILE)
+    tokens = layer_input.shape[0]
     conv_cols = 2 * key_cols + value_cols
     gate_at, small_at = conv_cols, conv_cols + value_cols
 
@@ -600,29 +898,24 @@
         axis=0,
         tiled=True,
     )
-    rest = lax.all_gather(
-        jnp.concatenate(
-            [w_out.T, padded(w_gate, unit_cols), padded(w_up, unit_cols), padded(w_down.T, unit_cols)],
-            axis=1,
-        ),
-        "dp",
-        axis=0,
-        tiled=True,
-    )
-    cut_out, cut_down = value_cols, value_cols + 2 * unit_cols
-    out_full, pair_full, down_full = (
-        rest[:, :cut_out],
-        rest[:, cut_out:cut_down],
-        rest[:, cut_down:],
-    )
+    rest_shard = jnp.concatenate(
+        [w_out.T, padded(w_gate, unit_cols), padded(w_up, unit_cols), padded(w_down.T, unit_cols)],
+        axis=1,
+    )
+    rest_shard = with_layout_constraint(rest_shard, Layout(major_to_minor=(0, 1)))
+
+    near_rest = lax.all_gather(rest_shard[None], "dp")
 
     residual = layer_input.astype(jnp.float32)
-    first_scale = rms_parts(residual)
+    first_scale = lax.rsqrt(jnp.mean(residual * residual, axis=-1, keepdims=True) + TINY)
     first_normed = residual * first_scale
-    mixer_rows = lax.all_gather(
-        (first_normed * norm_gain).astype(jnp.bfloat16), "tensor", axis=0, tiled=True
-    )
+    first = (first_normed * norm_gain).astype(jnp.bfloat16)
+    mixer_blocks = [first] + [fetched(first, ahead, ranks) for ahead in range(1, ranks)]
+    mixer_rows = jnp.concatenate(mixer_blocks, axis=0)
     projected = product(mixer_rows, joined, 1, 0)
+
+    rest_shard, _ = lax.optimization_barrier((rest_shard, mixer_blocks))
+    far = [fetched(rest_shard, ahead, ranks) for ahead in range(1, ranks)]
 
     def local(array, width):
         return lax.dynamic_slice_in_dim(array, tensor_rank * width, width, array.ndim - 1)
@@ -639,87 +932,82 @@
     aux = segment_columns(segments)
     segment_rows = segments.astype(jnp.float32).reshape(-1, 1, CHUNK)
     rank = tensor_rank.astype(jnp.int32).reshape(1)
+    ahead, projected = lax.optimization_barrier((far[0], projected))
+    next_rest = lax.all_gather(ahead[None], "dp")
     gated, *saved = mixer_forward(
-        rank, projected, aux, segment_rows, taps, head_rows, gain_row, heads, dk, dv
-    )
-    attended = lax.psum_scatter(
-        product(gated, out_full, 1, 1).astype(jnp.bfloat16),
-        "tensor",
-        scatter_dimension=0,
-        tiled=True,
-    ).astype(jnp.float32)
-    middle = residual + attended
-    second_scale = rms_parts(middle)
-    second_normed = middle * second_scale
-    ffn_rows = lax.all_gather(
-        (second_normed * ffn_gain).astype(jnp.bfloat16), "tensor", axis=0, tiled=True
-    )
-    cot_rows = lax.all_gather(cotangent, "tensor", axis=0, tiled=True)
-    pair = product(ffn_rows, pair_full, 1, 0)
-    gate_rows, up_rows = pair[:, :unit_cols], pair[:, unit_cols:]
-    sig = jax.nn.sigmoid(gate_rows)
-    hidden = (gate_rows * sig * up_rows).astype(jnp.bfloat16)
-    grad_hidden = product(cot_rows, down_full, 1, 0)
-    grad_pair = jnp.concatenate(
-        [
-            (grad_hidden * up_rows * sig * (1.0 + gate_rows * (1.0 - sig))).astype(jnp.bfloat16),
-            (grad_hidden * gate_rows * sig).astype(jnp.bfloat16),
-        ],
-        axis=1,
-    )
-    grad_second = lax.psum_scatter(
-        product(grad_pair, pair_full, 1, 1).astype(jnp.bfloat16),
-        "tensor",
-        scatter_dimension=0,
-        tiled=True,
-    ).astype(jnp.float32)
-    grad_middle = cotangent.astype(jnp.float32) + rms_back(
-        grad_second, ffn_gain, second_normed, second_scale
-    )
-    attn_rows = lax.all_gather(
-        grad_middle.astype(jnp.bfloat16), "tensor", axis=0, tiled=True
-    )
-    ffn_out = lax.psum_scatter(
-        product(hidden, down_full, 1, 1).astype(jnp.bfloat16),
-        "tensor",
-        scatter_dimension=0,
-        tiled=True,
-    ).astype(jnp.float32)
-    layer_output = (middle + ffn_out).astype(jnp.bfloat16)
-    grad_gated = product(attn_rows, out_full, 1, 0)
+        rank, projected, aux, segment_rows, taps, head_rows, gain_row, heads, dk, dv, ranks
+    )
+
+    def token_blocks(array):
+        return [array[at * tokens : (at + 1) * tokens] for at in range(ranks)]
+
+    far_rest = lax.all_gather(stacked_after(far[1:], gated), "dp")
+    gated_rows = jnp.concatenate(exchanged(token_blocks(gated)), axis=1)
+    spans = [(0, 1), (1, 2), (2, ranks)]
+    layer_output, grad_middle, grad_gated, dffn, near_grads, far_grads = ffn_block(
+        layer_input,
+        cotangent,
+        gated_rows,
+        [near_rest, next_rest, far_rest],
+        spans,
+        ffn_gain[None, :],
+        value_cols,
+        unit_cols,
+    )
+
+    def scattered(array):
+        return lax.psum_scatter(array, "dp", scatter_dimension=0, tiled=True)
+
+    summed_far = scattered(far_grads)
+    grad_gated_rows = jnp.concatenate(
+        exchanged(
+            [grad_gated[:, at * value_cols : (at + 1) * value_cols] for at in range(ranks)]
+        ),
+        axis=0,
+    )
     grad_proj, dtaps, dgain, dhead = mixer_backward(
-        rank, projected, aux, segment_rows, taps, head_rows, gain_row, saved, grad_gated, heads, dk, dv
-    )
-    grad_rest = jnp.concatenate(
-        [
-            product(attn_rows, gated, 0, 0),
-            product(ffn_rows, grad_pair, 0, 0),
-            product(cot_rows, hidden, 0, 0),
-        ],
-        axis=1,
-    )
+        rank,
+        projected,
+        aux,
+        segment_rows,
+        taps,
+        head_rows,
+        gain_row,
+        saved,
+        grad_gated_rows,
+        heads,
+        dk,
+        dv,
+        ranks,
+    )
+    back_first = [
+        product(block, joined, 1, 1).astype(jnp.bfloat16) for block in token_blocks(grad_proj)
+    ]
+    grad_proj, _ = lax.optimization_barrier((grad_proj, back_first))
     grad_joined = product(mixer_rows, grad_proj, 0, 0)
-    grad_first = lax.psum_scatter(
-        product(grad_proj, joined, 1, 1).astype(jnp.bfloat16),
-        "tensor",
-        scatter_dimension=0,
-        tiled=True,
-    ).astype(jnp.float32)
-    grad_input = grad_middle + rms_back(grad_first, norm_gain, first_normed, first_scale)
-
+    received_first = exchanged(back_first)
     grad_norm_gain = jnp.sum(joined.astype(jnp.float32) * grad_joined, axis=1) / norm_gain
-    grad_ffn_gain = (
-        jnp.sum(
-            pair_full.astype(jnp.float32) * grad_rest[:, cut_out:cut_down], axis=1
+
+    group = 3 * UNIT_TILE
+    tiles = unit_cols // UNIT_TILE
+    span_cols = tiles * group
+    grad_joined_low = grad_joined.astype(jnp.bfloat16)
+    near_grads, summed_far = lax.optimization_barrier(
+        (jnp.concatenate([near_grads, grad_joined_low], axis=1), summed_far)
+    )
+    summed_near = scattered(near_grads)
+    summed_joined = summed_near[:, span_cols:].astype(jnp.float32)
+    out_at = (ranks - 1) * span_cols
+    outs_for = [
+        summed_far[:, out_at + at * group : out_at + at * group + value_cols]
+        for at in range(ranks)
+    ]
+    rest_sends = [outs_for[0]] + [
+        jnp.concatenate(
+            [summed_far[:, at * span_cols : (at + 1) * span_cols], outs_for[at + 1]], axis=1
         )
-        / ffn_gain
-    )
-    summed_rest = lax.psum_scatter(
-        grad_rest.astype(jnp.bfloat16), "dp", scatter_dimension=0, tiled=True
-    ).astype(jnp.float32)
-    summed_joined = lax.psum_scatter(
-        grad_joined.astype(jnp.bfloat16), "dp", scatter_dimension=0, tiled=True
-    ).astype(jnp.float32)
+        for at in range(ranks - 1)
+    ]
 
     lags = taps.shape[0]
     mine = jnp.concatenate(
@@ -731,9 +1019,31 @@
     )
     placed = jnp.where((jnp.arange(ranks) == tensor_rank)[:, None], mine[None, :], 0.0)
     vector = jnp.concatenate(
-        [grad_norm_gain, grad_ffn_gain, jnp.sum(dgain, axis=0), placed.reshape(-1)]
-    )
-    small = lax.psum(vector, ("dp", "tensor"))
+        [grad_norm_gain, jnp.sum(dffn, axis=0), jnp.sum(dgain, axis=0), placed.reshape(-1)]
+    )
+    received_first, rest_sends, vector = lax.optimization_barrier(
+        (received_first, rest_sends, vector)
+    )
+    small = summed_over(summed_over(vector, "dp"), "tensor")
+    received_rest = exchanged(rest_sends)
+    owned = summed_near[:, :span_cols].astype(jnp.float32) + sum(
+        part[:, :span_cols].astype(jnp.float32) for part in received_rest[1:]
+    )
+    owned_out = received_rest[0].astype(jnp.float32) + sum(
+        part[:, span_cols:].astype(jnp.float32) for part in received_rest[1:]
+    )
+    by_kind = [
+        jnp.concatenate(
+            [
+                owned[:, tile * group + kind * UNIT_TILE : tile * group + (kind + 1) * UNIT_TILE]
+                for tile in range(tiles)
+            ],
+            axis=1,
+        )[:, :units]
+        for kind in range(3)
+    ]
+    grad_first = sum(part.astype(jnp.float32) for part in received_first)
+    grad_input = grad_middle + rms_back(grad_first, norm_gain, first_normed, first_scale)
     width = norm_gain.shape[0]
     sections = small[2 * width + dv :].reshape(ranks, -1)
     taps_all = sections[:, : lags * conv_cols].reshape(ranks, lags, conv_cols).transpose(1, 0, 2)
@@ -758,11 +1068,11 @@
         logs_all[:, :heads].reshape(-1),
         logs_all[:, heads:].reshape(-1),
         small[2 * width : 2 * width + dv],
-        summed_rest[:, :cut_out].T,
+        owned_out.T,
         small[width : 2 * width],
-        summed_rest[:, cut_out : cut_out + units],
-        summed_rest[:, cut_out + unit_cols : cut_out + unit_cols + units],
-        summed_rest[:, cut_down : cut_down + units].T,
+        by_kind[0],
+        by_kind[1],
+        by_kind[2].T,
     )
 
 

time: 1130 us -> 649 us (0.57)
  waiting for transfers between devices: 822 us -> 328 us
  matrix products: 115 us -> 37.4 us
  Pallas kernels: 112 us -> 166 us
  starting transfers between devices: 1.42 us -> 40.4 us
    reduce_scatter x6 -> x2, waiting for transfers between devices: 407 us -> 0.01 us  [scattered(): return lax.psum_scatter(array, 'dp', scatter_dimension=0, tiled=True)]
    ppermute x0 -> x23, waiting for transfers between devices: none -> 309 us  [the longest x12 158 us: exchanged(): lax.ppermute(blocks[ahead], 'tensor', [(i, (i + ahead) % ranks) for i in...]
    all_gather x5 -> x3, waiting for transfers between devices: 300 us -> 18.8 us  [the longest x1 18.8 us: shards(): far_rest = lax.all_gather(stacked_after(far[1:], gated), 'dp')]
    psum x1 -> x0, waiting for transfers between devices: 83.7 us -> none  [shards(): small = lax.psum(vector, ('dp', 'tensor'))]
    dot_general x12 -> x6, matrix products: 115 us -> 37.4 us  [product(): lax.dot_general(left, right, (((left_dim,), (right_dim,)), ((), ())), pre...]
    pallas_call x0 -> x2, Pallas kernels: none -> 62.4 us  [the longest x1 59.7 us: ffn_block(): pl.pallas_call(partial(ffn_body, (ranks, tiles, tuple(spans))), grid=(end...]
    ppermute x0 -> x23, starting transfers between devices: none -> 40.2 us  [the longest x12 25.5 us: exchanged(): lax.ppermute(blocks[ahead], 'tensor', [(i, (i + ahead) % ranks) for i in...]
    all_gather x1, waiting for transfers between devices: 29.6 us -> 0.01 us  [shards(): lax.all_gather(padded(jnp.concatenate([w_query, w_key, w_value, w_outgate...]
  transfers between devices with their start and end apart: 13 -> 29, of which waited for: 12 -> 16; matrix products, arithmetic and copies ran while one was open for 8% -> 11% of each run, Pallas kernels for 4% -> 17%
where the time goes in v2:
time: 649 us; the launch traced here: 643 us
  waiting for transfers between devices  328 us (51%)
  Pallas kernels  166 us (26%)
  starting transfers between devices  40.4 us (6%)
  matrix products  37.4 us (6%)
  local copies, waits for them, and re-layouts  32.4 us (5%)
  other arithmetic  23.4 us (4%)
  between operations  14.9 us (2%)
    ppermute x12, waiting for transfers between devices, exchanged(): lax.ppermute(blocks[ahead], 'tensor', [(i, (i + ahead) % ranks) for i in...  158 us
    ppermute x6, waiting for transfers between devices, fetched(): lax.ppermute(block, 'tensor', [((i + ahead) % ranks, i) for i in range(ra...  96.5 us
    pallas_call x1, Pallas kernels, mixer_backward(): pl.pallas_call(partial(backward_body, (heads, dk, dv, chunks)), grid_spec...  67.1 us
    pallas_call x1, Pallas kernels, ffn_block(): pl.pallas_call(partial(ffn_body, (ranks, tiles, tuple(spans))), grid=(end...  59.7 us
    ppermute x5, waiting for transfers between devices, summed_over(): lax.ppermute(vector, axis, [(i, i ^ apart) for i in range(size)])  55.1 us
    dot_general x6, matrix products, product(): lax.dot_general(left, right, (((left_dim,), (right_dim,)), ((), ())), pre...  37.4 us
    pallas_call x1, Pallas kernels, mixer_forward(): pl.pallas_call(partial(forward_body, (heads, dk, dv, chunks)), grid_spec=...  36.9 us
    ppermute x12, starting transfers between devices, exchanged(): lax.ppermute(blocks[ahead], 'tensor', [(i, (i + ahead) % ranks) for i in...  25.5 us
  transfers between devices with their start and end apart: 29, of which 16 were waited for; matrix products, arithmetic and copies ran while one was open for 11% of the time, Pallas kernels for 17%

profile of v2, /device:TPU:0, one launch (start us, length us, event | category | flops | bytes accessed | tf_op | source)
XLA Modules:
  0.0 643.3 jit_solution(9080970184857322800)
XLA Ops:
  13.8 5.1 collective-permute-start
  20.0 22.6 %collective-permute-done = bf16[512,1024]{1,0:T(8,128)(2,1)S(1)} collective-permute-done((bf16[512,1024]{1,0:T(8,128)(2,1)S(1)}, bf16[512,1024]{1,0:T(8,128)(2,1)S(1)}, u32[]{:S(2)}, u32[]{:S(2)}) %collective-permute-start) | collective-permute-done | bytes 1048608 | tf_op jit(solution)/shard_map/ppermute | solution.py:821
  42.5 66.1 %collective-permute-done.1 = bf16[512,1024]{1,0:T(8,128)(2,1)S(1)} collective-permute-done((bf16[512,1024]{1,0:T(8,128)(2,1)S(1)}, bf16[512,1024]{1,0:T(8,128)(2,1)S(1)}, u32[]{:S(2)}, u32[]{:S(2)}) %collective-permute-start.1) | collective-permute-done | bytes 1048608 | tf_op jit(solution)/shard_map/ppermute | solution.py:821
  110.7 14.7 %fusion.38.proj_ref.before_ref = f32[2048,1664]{1,0:T(8,128)} fusion(bf16[1024,1664]{1,0:T(8,128)(2,1)} %all-gather.8.cloned.1.call-done, bf16[512,1024]{1,0:T(8,128)(2,1)} %copy-done.35, bf16[512,1024]{1,0:T(8,128)(2,1)} %copy-done.33, bf16[512,1024]{1,0:T(8,128)(2,1)} %copy-done.31, bf16[512,1024]{1,0:T(8,128)(2,1)S(1)} %fusion.3), kind=kOutput, calls=%fused_computation.47 | convolution fusion | flops 6996099072 | bytes 21233664 | tf_op jit(solution)/shard_map/dot_general | solution.py:811
  125.4 2.3 collective-permute-done.3
  130.7 2.1 collective-permute-start.7
  133.6 36.9 %mixer_forward.1 = (bf16[2048,512]{1,0:T(8,128)(2,1)S(1)}, f32[2048,512]{1,0:T(8,128)}, f32[2048,512]{1,0:T(8,128)}, f32[16,128,512]{2,1,0:T(8,128)}, f32[2048,256]{1,0:T(8,128)S(1)}) custom-call(s32[1]{0:T(128)} %bitcast.rank_ref, f32[2048,1664]{1,0:T(8,128)} %fusion.38.proj_ref.before_ref, f32[2048,128]{1,0:T(8,128)S(1)} %pad.30.aux_ref, ...), custom_call_target="tpu_custom_call" | custom-call | flops 80000000000 | bytes 40894464 | tf_op jit(solution)/shard_map/mixer_forward/pallas_call | solution.py:424
  170.5 1.3 copy-done.2
  171.9 1.3 copy-done.5
  173.2 5.5 collective-permute-done.7.refs_1_
  180.4 2.8 stacked_after.1
  184.2 1.9 collective-permute-start.6
  186.1 11.5 %collective-permute-done.4 = bf16[512,512]{1,0:T(8,128)(2,1)S(1)} collective-permute-done((bf16[512,512]{1,0:T(8,128)(2,1)S(1)}, bf16[512,512]{1,0:T(8,128)(2,1)S(1)}, u32[]{:S(2)}, u32[]{:S(2)}) %collective-permute-start.4) | collective-permute-done | bytes 524320 | tf_op jit(solution)/shard_map/ppermute | solution.py:828
  197.6 31.3 %collective-permute-done.5 = bf16[512,512]{1,0:T(8,128)(2,1)S(1)} collective-permute-done((bf16[512,512]{1,0:T(8,128)(2,1)S(1)}, bf16[512,512]{1,0:T(8,128)(2,1)S(1)}, u32[]{:S(2)}, u32[]{:S(2)}) %collective-permute-start.5) | collective-permute-done | bytes 524320 | tf_op jit(solution)/shard_map/ppermute | solution.py:828
  228.9 1.6 pad_maximum_fusion.2.gated_ref
  230.6 18.8 %all-gather.14.cloned.1.call-done = bf16[16,128,2816]{2,1,0:T(8,128)(2,1)} async-done(((bf16[2,128,2816]{2,1,0:T(8,128)(2,1)}), bf16[16,128,2816]{2,1,0:T(8,128)(2,1)}) %all-gather.14.cloned.1.call-update) | async-done | bytes 11534352 | tf_op jit(solution)/shard_map/all_gather | solution.py:944
  249.3 59.7 %ffn_block.1 = (bf16[512,1024]{1,0:T(8,128)(2,1)}, f32[512,1024]{1,0:T(8,128)}, bf16[512,2048]{1,0:T(8,128)(2,1)}, f32[8,1024]{1,0:T(8,128)}, bf16[1024,2304]{1,0:T(8,128)(2,1)}, /*index=5*/bf16[1024,9984]{1,0:T(8,128)(2,1)}) custom-call(bf16[512,1024]{1,0:T(8,128)(2,1)} %rows_ref.1, bf16[512,1024]{1,0:T(8,128)(2,1)} %cot_ref.1, ...), custom_call_target="tpu_custom_call" | custom-call | flops 35000000512 | bytes 60000000 | tf_op jit(solution)/shard_map/ffn_block/pallas_call | solution.py:749
  309.1 1.5 copy-done.10
  310.8 2.5 collective-permute-start.10
  313.3 1.5 collective-permute-start.11
  314.8 2.3 collective-permute-start.9
  317.1 31.9 %collective-permute-done.10 = bf16[512,512]{1,0:T(8,128)(2,1)S(1)} collective-permute-done((bf16[512,512]{1,0:T(8,128)(2,1)S(1)}, bf16[512,512]{1,0:T(8,128)(2,1)S(1)}, u32[]{:S(2)}, u32[]{:S(2)}) %collective-permute-start.10) | collective-permute-done | bytes 524320 | tf_op jit(solution)/shard_map/ppermute | solution.py:828
  349.9 1.4 copy-done.6
  351.3 67.1 %mixer_backward.1 = (bf16[2048,1664]{1,0:T(8,128)(2,1)}, f32[32,1024]{1,0:T(8,128)S(1)}, f32[8,256]{1,0:T(8,128)S(1)}, f32[16,128]{1,0:T(8,128)S(1)}) custom-call(s32[1]{0:T(128)} %bitcast.rank_ref, f32[2048,1664]{1,0:T(8,128)} %fusion.38.proj_ref.before_ref, f32[2048,1664]{1,0:T(8,128)} %fusion.38.proj_ref.before_ref, f32[2048,128]{1,0:T(8,128)S(1)} %pad.30.aux_ref, ...), custom_call_target="tpu_custom_call" | custom-call | flops 160000000000 | bytes 54525952 | tf_op jit(solution)/shard_map/mixer_backward/pallas_call | solution.py:489
  418.4 4.7 fusion.20
  423.1 3.1 fusion.23
  426.2 3.1 fusion.26
  429.3 2.1 fusion.17
  431.5 9.7 %multiply_reduce_fusion = (f32[1024]{0:T(1024)S(1)}, bf16[1024,1664]{1,0:T(8,128)(2,1)}) fusion(bf16[1024,1664]{1,0:T(8,128)(2,1)S(1)} %copy-done.30, bf16[2048,1664]{1,0:T(8,128)(2,1)S(1)} %copy-done.37, bf16[512,1024]{1,0:T(8,128)(2,1)S(1)} %copy-done.36, bf16[512,1024]{1,0:T(8,128)(2,1)S(1)} %copy-done.34, bf16[512,1024]{1,0:T(8,128)(2,1)S(1)} %copy-done.32, ...), kind=kOutput, calls=%fused_computation.1 | convolution fusion | flops 7002913792 | bytes 17829888 | tf_op jit(solution)/shard_map/dot_general | solution.py:811
  441.2 7.2 %pad_maximum_fusion = bf16[1024,3968]{1,0:T(8,128)(2,1)} fusion(bf16[1024,1664]{1,0:T(8,128)(2,1)} %get-tuple-element.163, bf16[1024,2304]{1,0:T(8,128)(2,1)} %get-tuple-element.62), kind=kLoop, calls=%fused_computation | loop fusion | flops 16252928 | bytes 16252928 | tf_op jit(solution)/shard_map/concatenate | solution.py:996
  449.2 2.5 collective-permute-start.12
  451.6 10.1 %collective-permute-start.13 = (bf16[512,1024]{1,0:T(8,128)(2,1)}, bf16[512,1024]{1,0:T(8,128)(2,1)S(1)}, u32[]{:S(2)}, u32[]{:S(2)}) collective-permute-start(bf16[512,1024]{1,0:T(8,128)(2,1)} %fusion.23), channel_id=1, source_target_pairs={{0,2},{1,3},{2,0},{3,1},{4,6},{5,7},{6,4},{7,5},{8,10},{9,11},{10,... | collective-permute-start | bytes 3145736 | tf_op jit(solution)/shard_map/ppermute | solution.py:828
  461.7 1.9 collective-permute-start.14
  464.2 1.2 fusion.53
  465.4 2.0 fusion.52
  470.1 13.4 %collective-permute-done.12 = bf16[512,1024]{1,0:T(8,128)(2,1)S(1)} collective-permute-done((bf16[512,1024]{1,0:T(8,128)(2,1)}, bf16[512,1024]{1,0:T(8,128)(2,1)S(1)}, u32[]{:S(2)}, u32[]{:S(2)}) %collective-permute-start.12) | collective-permute-done | bytes 1048608 | tf_op jit(solution)/shard_map/ppermute | solution.py:828
  483.5 69.0 %collective-permute-done.13 = bf16[512,1024]{1,0:T(8,128)(2,1)S(1)} collective-permute-done((bf16[512,1024]{1,0:T(8,128)(2,1)}, bf16[512,1024]{1,0:T(8,128)(2,1)S(1)}, u32[]{:S(2)}, u32[]{:S(2)}) %collective-permute-start.13) | collective-permute-done | bytes 1048608 | tf_op jit(solution)/shard_map/ppermute | solution.py:828
  552.5 1.3 collective-permute-done.15
  553.8 1.6 collective-permute-start.16
  555.3 2.0 collective-permute-start.22
  558.3 1.2 collective-permute-start.17
  559.5 2.1 fusion.4
  561.6 1.2 collective-permute-done.17
  563.4 40.5 %collective-permute-done.18 = f32[18704]{0:T(1024)S(1)} collective-permute-done((f32[18704]{0:T(1024)S(1)}, f32[18704]{0:T(1024)S(1)}, u32[]{:S(2)}, u32[]{:S(2)}) %collective-permute-start.18) | collective-permute-done | bytes 74848 | tf_op jit(solution)/shard_map/ppermute | solution.py:854
  603.9 2.3 collective-permute-start.19
  606.3 3.5 fusion.7
  609.8 11.3 %collective-permute-done.19 = f32[18704]{0:T(1024)S(1)} collective-permute-done((f32[18704]{0:T(1024)S(1)}, f32[18704]{0:T(1024)S(1)}, u32[]{:S(2)}, u32[]{:S(2)}) %collective-permute-start.19) | collective-permute-done | bytes 74848 | tf_op jit(solution)/shard_map/ppermute | solution.py:854
  630.3 1.7 add_add_fusion
  (189 shorter events, 35.9 us)
Async XLA Ops:
  7.2 122.8 %copy-start = (f32[4,2048]{1,0:T(4,128)S(1)}, f32[4,2048]{1,0:T(4,128)}, u32[]{:S(2)}) copy-start(f32[4,2048]{1,0:T(4,128)} %param.32) | copy-start | bytes 98308
  7.2 3.8 copy-start.19
  7.2 3.9 copy-start.20
  7.2 4.1 copy-start.21
  7.2 4.3 copy-start.22
  7.2 103.4 %all-gather.8.cloned.1.call-start = ((), (), s32[]{:S(2)}) async-start(), calls=%async_computation.2 | async-start | bytes 3833856 | tf_op jit(solution)/shard_map/all_gather | solution.py:892
  11.0 219.6 %all-gather.10.cloned.1.call-start = ((), (), s32[]{:S(2)}) async-start(), calls=%async_computation.5 | async-start | bytes 6488064 | tf_op jit(solution)/shard_map/all_gather | solution.py:907
  12.5 98.1 %copy-start.9 = (bf16[128,2816]{1,0:T(8,128)(2,1)S(1)}, bf16[128,2816]{1,0:T(8,128)(2,1)}, u32[]{:S(2)}) copy-start(bf16[128,2816]{1,0:T(8,128)(2,1)} %fusion.35) | copy-start | bytes 2162692
  12.6 218.0 %all-gather.12.cloned.1.call-start = ((), (), s32[]{:S(2)}) async-start(), calls=%async_computation.6 | async-start | bytes 6488064 | tf_op jit(solution)/shard_map/all_gather | solution.py:936
  13.8 111.6 %copy-start.12 = (bf16[512,1024]{1,0:T(8,128)(2,1)}, bf16[512,1024]{1,0:T(8,128)(2,1)S(1)}, u32[]{:S(2)}) copy-start(bf16[512,1024]{1,0:T(8,128)(2,1)S(1)} %fusion.3) | copy-start | bytes 3145732
  13.8 114.8 %copy-start.18 = (s32[2048]{0:T(1024)S(1)}, s32[2048]{0:T(1024)}, u32[]{:S(2)}) copy-start(s32[2048]{0:T(1024)} %param.22) | copy-start | bytes 24580
  13.8 28.7 %collective-permute-start = (bf16[512,1024]{1,0:T(8,128)(2,1)S(1)}, bf16[512,1024]{1,0:T(8,128)(2,1)S(1)}, u32[]{:S(2)}, u32[]{:S(2)}) collective-permute-start(bf16[512,1024]{1,0:T(8,128)(2,1)S(1)} %fusion.3), channel_id=1, source_target_pairs={{1,0},{2,1},{3,2},{0,3},{5,4},{6,5},{7,6},{4,7},{9,8},{10,9},{11,1... | collective-permute-start | bytes 3145736 | tf_op jit(solution)/shard_map/ppermute | solution.py:821
  18.9 89.7 %collective-permute-start.1 = (bf16[512,1024]{1,0:T(8,128)(2,1)S(1)}, bf16[512,1024]{1,0:T(8,128)(2,1)S(1)}, u32[]{:S(2)}, u32[]{:S(2)}) collective-permute-start(bf16[512,1024]{1,0:T(8,128)(2,1)S(1)} %fusion.3), channel_id=1, source_target_pairs={{2,0},{3,1},{0,2},{1,3},{6,4},{7,5},{4,6},{5,7},{10,8},{11,9},{8,1... | collective-permute-start | bytes 3145736 | tf_op jit(solution)/shard_map/ppermute | solution.py:821
  18.9 89.7 %collective-permute-start.2 = (bf16[512,1024]{1,0:T(8,128)(2,1)S(1)}, bf16[512,1024]{1,0:T(8,128)(2,1)S(1)}, u32[]{:S(2)}, u32[]{:S(2)}) collective-permute-start(bf16[512,1024]{1,0:T(8,128)(2,1)S(1)} %fusion.3), channel_id=1, source_target_pairs={{3,0},{0,1},{1,2},{2,3},{7,4},{4,5},{5,6},{6,7},{11,8},{8,9},{9,10... | collective-permute-start | bytes 3145736 | tf_op jit(solution)/shard_map/ppermute | solution.py:821
  42.5 66.1 %copy-start.31 = (bf16[512,1024]{1,0:T(8,128)(2,1)}, bf16[512,1024]{1,0:T(8,128)(2,1)S(1)}, u32[]{:S(2)}) copy-start(bf16[512,1024]{1,0:T(8,128)(2,1)S(1)} %collective-permute-done) | copy-start | bytes 3145732
  110.7 17.0 %collective-permute-start.3 = (bf16[128,2816]{1,0:T(8,128)(2,1)S(1)}, bf16[128,2816]{1,0:T(8,128)(2,1)S(1)}, u32[]{:S(2)}, u32[]{:S(2)}) collective-permute-start(bf16[128,2816]{1,0:T(8,128)(2,1)S(1)} %copy-done.9), channel_id=1, source_target_pairs={{1,0},{2,1},{3,2},{0,3},{5,4},{6,5},{7,6},{4,7},{9,8},{10,9},{11,1... | collective-permute-start | bytes 2162696 | tf_op jit(solution)/shard_map/ppermute | solution.py:821
  128.6 5.0 copy-start.4
  128.6 120.7 %all-gather.14.cloned.1.call-start = ((), (), s32[]{:S(2)}) async-start(), calls=%async_computation.7 | async-start | bytes 12976128 | tf_op jit(solution)/shard_map/all_gather | solution.py:944
  130.7 47.9 %collective-permute-start.7 = (bf16[128,2816]{1,0:T(8,128)(2,1)S(1)}, bf16[128,2816]{1,0:T(8,128)(2,1)S(1)}, u32[]{:S(2)}, u32[]{:S(2)}) collective-permute-start(bf16[128,2816]{1,0:T(8,128)(2,1)S(1)} %copy-done.9), channel_id=1, source_target_pairs={{2,0},{3,1},{0,2},{1,3},{6,4},{7,5},{4,6},{5,7},{10,8},{11,9},{8,1... | collective-permute-start | bytes 2162696 | tf_op jit(solution)/shard_map/ppermute | solution.py:821
  132.9 45.8 %collective-permute-start.8 = (bf16[128,2816]{1,0:T(8,128)(2,1)S(1)}, bf16[128,2816]{1,0:T(8,128)(2,1)S(1)}, u32[]{:S(2)}, u32[]{:S(2)}) collective-permute-start(bf16[128,2816]{1,0:T(8,128)(2,1)S(1)} %copy-done.9), channel_id=1, source_target_pairs={{3,0},{0,1},{1,2},{2,3},{7,4},{4,5},{5,6},{6,7},{11,8},{8,9},{9,10... | collective-permute-start | bytes 2162696 | tf_op jit(solution)/shard_map/ppermute | solution.py:821
  180.4 2.8 copy-start.3
  183.2 265.2 %reduce-scatter.3.cloned.1.call-start = ((), (), s32[]{:S(2)}) async-start(), calls=%async_computation.3 | async-start | bytes 23003136 | tf_op jit(solution)/shard_map/reduce_scatter | solution.py:959
  183.4 14.2 %collective-permute-start.4 = (bf16[512,512]{1,0:T(8,128)(2,1)S(1)}, bf16[512,512]{1,0:T(8,128)(2,1)S(1)}, u32[]{:S(2)}, u32[]{:S(2)}) collective-permute-start(bf16[512,512]{1,0:T(8,128)(2,1)S(1)} %get-tuple-element.178), channel_id=1, source_target_pairs={{0,3},{1,0},{2,1},{3,2},{4,7},{5,4},{6,5},{7,6},{8,11},{9,8},{10,9... | collective-permute-start | bytes 1572872 | tf_op jit(solution)/shard_map/ppermute | solution.py:828
  183.5 45.4 %collective-permute-start.5 = (bf16[512,512]{1,0:T(8,128)(2,1)S(1)}, bf16[512,512]{1,0:T(8,128)(2,1)S(1)}, u32[]{:S(2)}, u32[]{:S(2)}) collective-permute-start(bf16[512,512]{1,0:T(8,128)(2,1)S(1)} %get-tuple-element.177), channel_id=1, source_target_pairs={{0,2},{1,3},{2,0},{3,1},{4,6},{5,7},{6,4},{7,5},{8,10},{9,11},{10,... | collective-permute-start | bytes 1572872 | tf_op jit(solution)/shard_map/ppermute | solution.py:828
  184.2 44.8 %collective-permute-start.6 = (bf16[512,512]{1,0:T(8,128)(2,1)S(1)}, bf16[512,512]{1,0:T(8,128)(2,1)S(1)}, u32[]{:S(2)}, u32[]{:S(2)}) collective-permute-start(bf16[512,512]{1,0:T(8,128)(2,1)S(1)} %get-tuple-element.176), channel_id=1, source_target_pairs={{0,1},{1,2},{2,3},{3,0},{4,5},{5,6},{6,7},{7,4},{8,9},{9,10},{10,1... | collective-permute-start | bytes 1572872 | tf_op jit(solution)/shard_map/ppermute | solution.py:828
  309.0 318.4 %reduce-scatter.5.cloned.1.call-start = ((), (), s32[]{:S(2)}) async-start(), calls=%async_computation.4 | async-start | bytes 9142272 | tf_op jit(solution)/shard_map/reduce_scatter | solution.py:959
  310.8 38.2 %collective-permute-start.10 = (bf16[512,512]{1,0:T(8,128)(2,1)S(1)}, bf16[512,512]{1,0:T(8,128)(2,1)S(1)}, u32[]{:S(2)}, u32[]{:S(2)}) collective-permute-start(bf16[512,512]{1,0:T(8,128)(2,1)S(1)} %get-tuple-element.173), channel_id=1, source_target_pairs={{0,2},{1,3},{2,0},{3,1},{4,6},{5,7},{6,4},{7,5},{8,10},{9,11},{10,... | collective-permute-start | bytes 1572872 | tf_op jit(solution)/shard_map/ppermute | solution.py:828
  313.3 35.8 %collective-permute-start.11 = (bf16[512,512]{1,0:T(8,128)(2,1)S(1)}, bf16[512,512]{1,0:T(8,128)(2,1)S(1)}, u32[]{:S(2)}, u32[]{:S(2)}) collective-permute-start(bf16[512,512]{1,0:T(8,128)(2,1)S(1)} %get-tuple-element.172), channel_id=1, source_target_pairs={{0,1},{1,2},{2,3},{3,0},{4,5},{5,6},{6,7},{7,4},{8,9},{9,10},{10,1... | collective-permute-start | bytes 1572872 | tf_op jit(solution)/shard_map/ppermute | solution.py:828
  314.8 35.0 %collective-permute-start.9 = (bf16[512,512]{1,0:T(8,128)(2,1)S(1)}, bf16[512,512]{1,0:T(8,128)(2,1)S(1)}, u32[]{:S(2)}, u32[]{:S(2)}) collective-permute-start(bf16[512,512]{1,0:T(8,128)(2,1)S(1)} %get-tuple-element.174), channel_id=1, source_target_pairs={{0,3},{1,0},{2,1},{3,2},{4,7},{5,4},{6,5},{7,6},{8,11},{9,8},{10,9... | collective-permute-start | bytes 1572872 | tf_op jit(solution)/shard_map/ppermute | solution.py:828
  351.3 67.1 %copy-start.30 = (bf16[1024,1664]{1,0:T(8,128)(2,1)S(1)}, bf16[1024,1664]{1,0:T(8,128)(2,1)}, u32[]{:S(2)}) copy-start(bf16[1024,1664]{1,0:T(8,128)(2,1)} %all-gather.8.cloned.1.call-done) | copy-start | bytes 10223620
  418.4 4.7 copy-start.37
  448.4 15.7 %copy-start.24 = (f32[1024]{0:T(1024)S(1)}, f32[1024]{0:T(1024)}, u32[]{:S(2)}) copy-start(f32[1024]{0:T(1024)} %param.23) | copy-start | bytes 12292
  449.2 34.3 %collective-permute-start.12 = (bf16[512,1024]{1,0:T(8,128)(2,1)}, bf16[512,1024]{1,0:T(8,128)(2,1)S(1)}, u32[]{:S(2)}, u32[]{:S(2)}) collective-permute-start(bf16[512,1024]{1,0:T(8,128)(2,1)} %fusion.20), channel_id=1, source_target_pairs={{0,3},{1,0},{2,1},{3,2},{4,7},{5,4},{6,5},{7,6},{8,11},{9,8},{10,9... | collective-permute-start | bytes 3145736 | tf_op jit(solution)/shard_map/ppermute | solution.py:828
  451.6 100.8 %collective-permute-start.13 = (bf16[512,1024]{1,0:T(8,128)(2,1)}, bf16[512,1024]{1,0:T(8,128)(2,1)S(1)}, u32[]{:S(2)}, u32[]{:S(2)}) collective-permute-start(bf16[512,1024]{1,0:T(8,128)(2,1)} %fusion.23), channel_id=1, source_target_pairs={{0,2},{1,3},{2,0},{3,1},{4,6},{5,7},{6,4},{7,5},{8,10},{9,11},{10,... | collective-permute-start | bytes 3145736 | tf_op jit(solution)/shard_map/ppermute | solution.py:828
  461.7 90.8 %collective-permute-start.14 = (bf16[512,1024]{1,0:T(8,128)(2,1)}, bf16[512,1024]{1,0:T(8,128)(2,1)}, u32[]{:S(2)}, u32[]{:S(2)}) collective-permute-start(bf16[512,1024]{1,0:T(8,128)(2,1)} %fusion.26), channel_id=1, source_target_pairs={{0,1},{1,2},{2,3},{3,0},{4,5},{5,6},{6,7},{7,4},{8,9},{9,10},{10,1... | collective-permute-start | bytes 3145736 | tf_op jit(solution)/shard_map/ppermute | solution.py:828
  467.4 92.1 %copy-start.8 = (bf16[512,1024]{1,0:T(8,128)(2,1)S(1)}, bf16[512,1024]{1,0:T(8,128)(2,1)}, u32[]{:S(2)}) copy-start(bf16[512,1024]{1,0:T(8,128)(2,1)} %rows_ref.1) | copy-start | bytes 3145732
  467.4 92.1 %copy-start.27 = (f32[512]{0:T(512)S(1)}, f32[512]{0:T(512)}, u32[]{:S(2)}) copy-start(f32[512]{0:T(512)} %copy-done.26) | copy-start | bytes 6148
  552.5 1.3 collective-permute-start.15
  553.8 4.5 collective-permute-start.16
  555.3 70.2 %collective-permute-start.20 = (bf16[128,2816]{1,0:T(8,128)(2,1)}, bf16[128,2816]{1,0:T(8,128)(2,1)}, u32[]{:S(2)}, u32[]{:S(2)}) collective-permute-start(bf16[128,2816]{1,0:T(8,128)(2,1)} %pad_maximum_fusion.6), channel_id=1, source_target_pairs={{0,3},{1,0},{2,1},{3,2},{4,7},{5,4},{6,5},{7,6},{8,11},{9,8},{10,9... | collective-permute-start | bytes 2162696 | tf_op jit(solution)/shard_map/ppermute | solution.py:828
  555.3 70.2 %collective-permute-start.21 = (bf16[128,2816]{1,0:T(8,128)(2,1)}, bf16[128,2816]{1,0:T(8,128)(2,1)}, u32[]{:S(2)}, u32[]{:S(2)}) collective-permute-start(bf16[128,2816]{1,0:T(8,128)(2,1)} %pad_maximum_fusion.5), channel_id=1, source_target_pairs={{0,2},{1,3},{2,0},{3,1},{4,6},{5,7},{6,4},{7,5},{8,10},{9,11},{10,... | collective-permute-start | bytes 2162696 | tf_op jit(solution)/shard_map/ppermute | solution.py:828
  555.3 70.2 %collective-permute-start.22 = (bf16[128,2816]{1,0:T(8,128)(2,1)}, bf16[128,2816]{1,0:T(8,128)(2,1)}, u32[]{:S(2)}, u32[]{:S(2)}) collective-permute-start(bf16[128,2816]{1,0:T(8,128)(2,1)} %pad_maximum_fusion.4), channel_id=1, source_target_pairs={{0,1},{1,2},{2,3},{3,0},{4,5},{5,6},{6,7},{7,4},{8,9},{9,10},{10,1... | collective-permute-start | bytes 2162696 | tf_op jit(solution)/shard_map/ppermute | solution.py:828
  558.3 48.0 %copy-start.11 = (f32[512,1024]{1,0:T(8,128)S(1)}, f32[512,1024]{1,0:T(8,128)}, u32[]{:S(2)}) copy-start(f32[512,1024]{1,0:T(8,128)} %get-tuple-element.55) | copy-start | bytes 6291460
  558.3 4.5 collective-permute-start.17
  562.8 41.2 %collective-permute-start.18 = (f32[18704]{0:T(1024)S(1)}, f32[18704]{0:T(1024)S(1)}, u32[]{:S(2)}, u32[]{:S(2)}) collective-permute-start(f32[18704]{0:T(1024)S(1)} %add.102), channel_id=1, source_target_pairs={{0,1},{1,0},{2,3},{3,2},{4,5},{5,4},{6,7},{7,6},{8,9},{9,8},{10,11... | collective-permute-start | bytes 224456 | tf_op jit(solution)/shard_map/ppermute | solution.py:854
  603.9 17.1 %collective-permute-start.19 = (f32[18704]{0:T(1024)S(1)}, f32[18704]{0:T(1024)S(1)}, u32[]{:S(2)}, u32[]{:S(2)}) collective-permute-start(f32[18704]{0:T(1024)S(1)} %add.103), channel_id=1, source_target_pairs={{0,2},{1,3},{2,0},{3,1},{4,6},{5,7},{6,4},{7,5},{8,10},{9,11},{10,... | collective-permute-start | bytes 224456 | tf_op jit(solution)/shard_map/ppermute | solution.py:854
  627.4 2.8 copy-start.14
  632.1 4.1 copy-start.1
  (19 other events, 26.9 us)
Sparse Core Ops, SparseCore 0:
  11.1 36.1 all-gather.7
  49.7 43.3 all-gather.9
  128.7 43.0 all-gather.11
  183.3 65.9 all-gather.13
  309.2 133.1 reduce-scatter.2
  448.6 79.0 reduce-scatter.4

commit v3 on v2

--- a/solution.py
+++ b/solution.py
@@ -207,6 +207,7 @@
 
 def backward_body(
     sizes,
+    held,
     rank_ref,
     proj_ref,
     before_ref,
@@ -220,15 +221,13 @@
     state_ref,
     inverse_ref,
     grad_ref,
-    dproj_ref,
-    dtaps_ref,
-    dgain_ref,
-    dhead_ref,
-    window_ref,
-    later_ref,
-    carried_ref,
+    later_in_ref,
+    carried_in_ref,
+    *refs,
 ):
-    heads, dk, dv, chunks = sizes
+    dproj_ref, dtaps_ref, dgain_ref, dhead_ref, later_out_ref, carried_ref = refs[held : held + 6]
+    window_ref, later_ref = refs[held + 6 :]
+    heads, dk, dv, chunks, top = sizes
     count = chunks * CHUNK
     keys, conv_cols = heads * dk, heads * (2 * dk + dv)
     gate_at, small_at = conv_cols, conv_cols + heads * dv
@@ -236,14 +235,14 @@
 
     @pl.when(pl.program_id(0) == 0)
     def start():
-        later_ref[count : count + 8, :] = jnp.zeros((8, conv_cols), jnp.float32)
-        carried_ref[...] = jnp.zeros(carried_ref.shape, jnp.float32)
+        later_ref[count : count + 8, :] = later_in_ref[...]
+        carried_ref[...] = carried_in_ref[...]
         dtaps_ref[...] = jnp.zeros(dtaps_ref.shape, jnp.float32)
         dgain_ref[...] = jnp.zeros(dgain_ref.shape, jnp.float32)
         dhead_ref[...] = jnp.zeros(dhead_ref.shape, jnp.float32)
 
     aux = aux_ref[...]
-    first = pl.program_id(0) == pl.num_programs(0) - 1
+    first = pl.program_id(0) == top
     window_ref[0:8, :] = jnp.where(first, 0.0, before_ref[:, :conv_cols])
     window_ref[8 : 8 + count, :] = proj_ref[:, :conv_cols]
     beta_all, decay_all, slope_all = head_scalars(
@@ -396,6 +395,7 @@
             )
         dproj_ref[:, lo:hi] = total.astype(jnp.bfloat16)
     later_ref[count : count + 8, :] = later_ref[0:8, :]
+    later_out_ref[...] = later_ref[0:8, :]
 
 
 FORWARD_CHUNKS = 4
@@ -462,15 +462,33 @@
 
 
 def mixer_backward(
-    rank, proj, aux, segment_rows, taps, head_rows, gain, saved, grad, heads, dk, dv, ranks
+    rank,
+    proj,
+    aux,
+    segment_rows,
+    taps,
+    head_rows,
+    gain,
+    saved,
+    grad,
+    heads,
+    dk,
+    dv,
+    ranks,
+    high,
+    low,
+    later,
+    carried,
+    dproj,
 ):
+    held = [] if dproj is None else [dproj]
     length, width = proj.shape
     chunks = BACKWARD_CHUNKS
     count = chunks * CHUNK
     steps = length // count
     conv_cols = heads * (2 * dk + dv)
     out, fresh, states, inverses = saved
-    place = lambda step: steps - 1 - step
+    place = lambda step: high - step
     turned = turned_place(steps, ranks)
     rows = lambda cols: pl.BlockSpec((count, cols), lambda step, rank: (place(step), 0))
     turned_rows = lambda cols: pl.BlockSpec(
@@ -487,10 +505,10 @@
     )
     whole = lambda shape: pl.BlockSpec(shape, lambda step, rank: (0, 0))
     return pl.pallas_call(
-        partial(backward_body, (heads, dk, dv, chunks)),
+        partial(backward_body, (heads, dk, dv, chunks, high), len(held)),
         grid_spec=pltpu.PrefetchScalarGridSpec(
             num_scalar_prefetch=1,
-            grid=(steps,),
+            grid=(high - low + 1,),
             in_specs=[
                 turned_rows(width),
                 before,
@@ -504,17 +522,21 @@
                 pl.BlockSpec((chunks, dk, heads * dv), lambda step, rank: (place(step), 0, 0)),
                 rows(heads * CHUNK),
                 turned_rows(heads * dv),
-            ],
+                whole_block(later),
+                whole_block(carried),
+            ]
+            + [pl.BlockSpec(memory_space=pl.ANY)] * len(held),
             out_specs=[
                 turned_rows(width),
                 whole((8 * lags, conv_cols)),
                 whole((8, dv)),
                 whole((16, LANES)),
+                whole(later.shape),
+                pl.BlockSpec(carried.shape, lambda step, rank: (0, 0, 0)),
             ],
             scratch_shapes=[
                 pltpu.VMEM((8 + count, conv_cols), jnp.float32),
                 pltpu.VMEM((8 + count, conv_cols), jnp.float32),
-                pltpu.VMEM((heads, dk, dv), jnp.float32),
             ],
         ),
         out_shape=[
@@ -522,7 +544,10 @@
             jax.ShapeDtypeStruct((8 * lags, conv_cols), jnp.float32),
             jax.ShapeDtypeStruct((8, dv), jnp.float32),
             jax.ShapeDtypeStruct((16, LANES), jnp.float32),
+            jax.ShapeDtypeStruct(later.shape, jnp.float32),
+            jax.ShapeDtypeStruct(carried.shape, jnp.float32),
         ],
+        input_output_aliases={15: 0} if held else {},
         compiler_params=pltpu.CompilerParams(vmem_limit_bytes=48 * 2**20),
         cost_estimate=pl.CostEstimate(
             flops=160 * 10**9, bytes_accessed=length * width * 16, transcendentals=0
@@ -530,7 +555,7 @@
         name="mixer_backward",
     )(
         rank, proj, proj, aux, segment_rows, taps, head_rows, gain,
-        out, fresh, states, inverses, grad,
+        out, fresh, states, inverses, grad, later, carried, *held,
     )
 
 
@@ -665,7 +690,7 @@
         )
 
     for (low, high), held in zip(spans, weight_refs):
-        grads_ref = grads_refs[0 if low == 0 else 1]
+        grads_ref = grads_refs[0 if low >= 2 else 1]
         pl.when(jnp.logical_and(step >= begin + low * tiles, step < begin + high * tiles))(
             partial(units, *held[1:], grads_ref)
         )
@@ -708,7 +733,7 @@
 def ffn_block(rows, cot, gated, weights, spans, gain, value_cols, unit_cols):
     tokens, width = rows.shape
     ranks = spans[-1][1]
-    grad_spans = [(0, 1), (1, ranks)]
+    grad_spans = [(2, ranks), (0, 2)]
     tiles = unit_cols // UNIT_TILE
     begin, end = ranks, ranks + ranks * tiles
     group = 3 * UNIT_TILE
@@ -736,7 +761,7 @@
 
     def grads_at(step, low, high):
         place = tile_at(step, low, high)
-        return jnp.where(step < end, place, place + 1 + step - end) if high == ranks else place
+        return jnp.where(step < end, place, place + 1 + step - end) if low == 0 else place
 
     whole = lambda shape: pl.BlockSpec(shape, lambda step: (0,) * len(shape))
     bf, f32 = jnp.bfloat16, jnp.float32
@@ -786,7 +811,7 @@
         ]
         + [
             jax.ShapeDtypeStruct(
-                (width, ((high - low) * tiles + (ranks if high == ranks else 0)) * group), bf
+                (width, ((high - low) * tiles + (ranks if low == 0 else 0)) * group), bf
             )
             for low, high in grad_spans
         ],
@@ -825,10 +850,27 @@
     ranks = len(blocks)
     result = [blocks[0]] + [None] * (ranks - 1)
     for ahead in range(1, ranks):
+        if blocks[ahead] is None:
+            continue
         result[ranks - ahead] = lax.ppermute(
             blocks[ahead], "tensor", [(i, (i + ahead) % ranks) for i in range(ranks)]
         )
     return result
+
+
+def nothing_body(*refs):
+    pass
+
+
+def after(value, *earlier):
+    return pl.pallas_call(
+        nothing_body,
+        in_specs=[pl.BlockSpec(memory_space=pl.ANY)] * (1 + len(earlier)),
+        out_specs=pl.BlockSpec(memory_space=pl.ANY),
+        out_shape=jax.ShapeDtypeStruct(value.shape, value.dtype),
+        input_output_aliases={0: 0},
+        name="after",
+    )(value, *earlier)
 
 
 def stacked_body(*refs):
@@ -944,7 +986,7 @@
     far_rest = lax.all_gather(stacked_after(far[1:], gated), "dp")
     gated_rows = jnp.concatenate(exchanged(token_blocks(gated)), axis=1)
     spans = [(0, 1), (1, 2), (2, ranks)]
-    layer_output, grad_middle, grad_gated, dffn, near_grads, far_grads = ffn_block(
+    layer_output, grad_middle, grad_gated, dffn, far_grads, near_grads = ffn_block(
         layer_input,
         cotangent,
         gated_rows,
@@ -959,27 +1001,49 @@
         return lax.psum_scatter(array, "dp", scatter_dimension=0, tiled=True)
 
     summed_far = scattered(far_grads)
+    span_cols = unit_cols // UNIT_TILE * 3 * UNIT_TILE
+    received_far = exchanged(
+        [None, None]
+        + [summed_far[:, at * span_cols : (at + 1) * span_cols] for at in range(ranks - 2)]
+    )
     grad_gated_rows = jnp.concatenate(
         exchanged(
             [grad_gated[:, at * value_cols : (at + 1) * value_cols] for at in range(ranks)]
         ),
         axis=0,
     )
-    grad_proj, dtaps, dgain, dhead = mixer_backward(
-        rank,
-        projected,
-        aux,
-        segment_rows,
-        taps,
-        head_rows,
-        gain_row,
-        saved,
-        grad_gated_rows,
-        heads,
-        dk,
-        dv,
-        ranks,
-    )
+    blocks = segments.shape[0] // (BACKWARD_CHUNKS * CHUNK)
+    cut = blocks * 3 // 8
+    later = jnp.zeros((8, conv_cols), jnp.float32)
+    carried = jnp.zeros((heads, dk, dv), jnp.float32)
+    grad_proj = None
+    small_grads = []
+    for high, low in ((blocks - 1, cut), (cut - 1, 0)):
+        if low == 0:
+            summed_near = scattered(after(near_grads, summed_far, later))
+            later = after(later, summed_far)
+        grad_proj, dtaps, dgain, dhead, later, carried = mixer_backward(
+            rank,
+            projected,
+            aux,
+            segment_rows,
+            taps,
+            head_rows,
+            gain_row,
+            saved,
+            grad_gated_rows,
+            heads,
+            dk,
+            dv,
+            ranks,
+            high,
+            low,
+            later,
+            carried,
+            grad_proj,
+        )
+        small_grads.append((dtaps, dgain, dhead))
+    dtaps, dgain, dhead = (sum(parts) for parts in zip(*small_grads))
     back_first = [
         product(block, joined, 1, 1).astype(jnp.bfloat16) for block in token_blocks(grad_proj)
     ]
@@ -990,23 +1054,21 @@
 
     group = 3 * UNIT_TILE
     tiles = unit_cols // UNIT_TILE
-    span_cols = tiles * group
     grad_joined_low = grad_joined.astype(jnp.bfloat16)
-    near_grads, summed_far = lax.optimization_barrier(
-        (jnp.concatenate([near_grads, grad_joined_low], axis=1), summed_far)
-    )
-    summed_near = scattered(near_grads)
-    summed_joined = summed_near[:, span_cols:].astype(jnp.float32)
-    out_at = (ranks - 1) * span_cols
-    outs_for = [
-        summed_far[:, out_at + at * group : out_at + at * group + value_cols]
-        for at in range(ranks)
-    ]
-    rest_sends = [outs_for[0]] + [
+    summed_joined = scattered(grad_joined_low).astype(jnp.float32)
+    out_at = 2 * span_cols
+    near_sends = [
+        summed_near[:, out_at : out_at + value_cols],
         jnp.concatenate(
-            [summed_far[:, at * span_cols : (at + 1) * span_cols], outs_for[at + 1]], axis=1
-        )
-        for at in range(ranks - 1)
+            [
+                summed_near[:, span_cols:out_at],
+                summed_near[:, out_at + group : out_at + group + value_cols],
+            ],
+            axis=1,
+        ),
+    ] + [
+        summed_near[:, out_at + at * group : out_at + at * group + value_cols]
+        for at in range(2, ranks)
     ]
 
     lags = taps.shape[0]
@@ -1021,16 +1083,18 @@
     vector = jnp.concatenate(
         [grad_norm_gain, jnp.sum(dffn, axis=0), jnp.sum(dgain, axis=0), placed.reshape(-1)]
     )
-    received_first, rest_sends, vector = lax.optimization_barrier(
-        (received_first, rest_sends, vector)
-    )
-    small = summed_over(summed_over(vector, "dp"), "tensor")
-    received_rest = exchanged(rest_sends)
-    owned = summed_near[:, :span_cols].astype(jnp.float32) + sum(
-        part[:, :span_cols].astype(jnp.float32) for part in received_rest[1:]
-    )
-    owned_out = received_rest[0].astype(jnp.float32) + sum(
-        part[:, span_cols:].astype(jnp.float32) for part in received_rest[1:]
+    vector = after(vector, *received_first[1:])
+    vector = summed_over(vector, "dp")
+    small = vector + sum(fetched(vector, ahead, ranks) for ahead in range(1, ranks))
+    received_near = exchanged(near_sends)
+    owned = sum(
+        part.astype(jnp.float32)
+        for part in [summed_near[:, :span_cols], received_near[ranks - 1][:, :span_cols]]
+        + [part for part in received_far if part is not None]
+    )
+    owned_out = sum(
+        part.astype(jnp.float32)
+        for part in received_near[: ranks - 1] + [received_near[ranks - 1][:, span_cols:]]
     )
     by_kind = [
         jnp.concatenate(
@@ -1042,6 +1106,7 @@
         )[:, :units]
         for kind in range(3)
     ]
+    received_first[1] = after(received_first[1], grad_joined_low)
     grad_first = sum(part.astype(jnp.float32) for part in received_first)
     grad_input = grad_middle + rms_back(grad_first, norm_gain, first_normed, first_scale)
     width = norm_gain.shape[0]

time: 649 us -> 634 us (0.977)
  waiting for transfers between devices: 328 us -> 300 us
  local copies, waits for them, and re-layouts: 32.4 us -> 41.3 us
    ppermute x5 -> x3, waiting for transfers between devices: 55.1 us -> 8.19 us  [summed_over(): lax.ppermute(vector, axis, [(i, i ^ apart) for i in range(size)])]
    ppermute x6 -> x9, waiting for transfers between devices: 96.5 us -> 120 us  [fetched(): lax.ppermute(block, 'tensor', [((i + ahead) % ranks, i) for i in range(ra...]
    concatenate x4 -> x1, other arithmetic: 9.93 us -> 0.92 us  [shards(): jnp.concatenate([summed_near[:, span_cols:out_at], summed_near[:, out_at...]
    ppermute x12 -> x14, waiting for transfers between devices: 158 us -> 153 us  [exchanged(): lax.ppermute(blocks[ahead], 'tensor', [(i, (i + ahead) % ranks) for i in...]
    ppermute x6 -> x9, starting transfers between devices: 9.01 us -> 13.5 us  [fetched(): lax.ppermute(block, 'tensor', [((i + ahead) % ranks, i) for i in range(ra...]
    ppermute x12 -> x14, starting transfers between devices: 25.5 us -> 29.9 us  [exchanged(): lax.ppermute(blocks[ahead], 'tensor', [(i, (i + ahead) % ranks) for i in...]
    unnamed x94 -> x128, local copies, waits for them, and re-layouts: 20.6 us -> 23.8 us
    pallas_call x1 -> x6, Pallas kernels: 67.1 us -> 69.4 us  [the longest x2 69.4 us: mixer_backward(): pl.pallas_call(partial(backward_body, (heads, dk, dv, chunks, high), len(...]
  transfers between devices with their start and end apart: 29 -> 33, of which waited for: 16 -> 17; matrix products, arithmetic and copies ran while one was open for 11% -> 12% of each run, Pallas kernels for 17% -> 17%
where the time goes in v3:
time: 634 us; the launch traced here: 627 us
  waiting for transfers between devices  300 us (47%)
  Pallas kernels  169 us (27%)
  starting transfers between devices  46.1 us (7%)
  local copies, waits for them, and re-layouts  41.3 us (7%)
  matrix products  38.7 us (6%)
  other arithmetic  17.2 us (3%)
  between operations  14.9 us (2%)
    ppermute x14, waiting for transfers between devices, exchanged(): lax.ppermute(blocks[ahead], 'tensor', [(i, (i + ahead) % ranks) for i in...  153 us
    ppermute x9, waiting for transfers between devices, fetched(): lax.ppermute(block, 'tensor', [((i + ahead) % ranks, i) for i in range(ra...  120 us
    pallas_call x2, Pallas kernels, mixer_backward(): pl.pallas_call(partial(backward_body, (heads, dk, dv, chunks, high), len(...  69.4 us
    pallas_call x1, Pallas kernels, ffn_block(): pl.pallas_call(partial(ffn_body, (ranks, tiles, tuple(spans))), grid=(end...  59.7 us
    dot_general x6, matrix products, product(): lax.dot_general(left, right, (((left_dim,), (right_dim,)), ((), ())), pre...  38.7 us
    pallas_call x1, Pallas kernels, mixer_forward(): pl.pallas_call(partial(forward_body, (heads, dk, dv, chunks)), grid_spec=...  37 us
    ppermute x14, starting transfers between devices, exchanged(): lax.ppermute(blocks[ahead], 'tensor', [(i, (i + ahead) % ranks) for i in...  29.9 us
    unnamed x128, local copies, waits for them, and re-layouts  23.8 us
  transfers between devices with their start and end apart: 33, of which 17 were waited for; matrix products, arithmetic and copies ran while one was open for 12% of the time, Pallas kernels for 17%

profile of v3, /device:TPU:0, one launch (start us, length us, event | category | flops | bytes accessed | tf_op | source)
XLA Modules:
  0.0 626.7 jit_solution(14045344609896921327)
XLA Ops:
  13.3 5.1 collective-permute-start
  19.4 22.6 %collective-permute-done = bf16[512,1024]{1,0:T(8,128)(2,1)S(1)} collective-permute-done((bf16[512,1024]{1,0:T(8,128)(2,1)S(1)}, bf16[512,1024]{1,0:T(8,128)(2,1)S(1)}, u32[]{:S(2)}, u32[]{:S(2)}) %collective-permute-start) | collective-permute-done | bytes 1048608 | tf_op jit(solution)/shard_map/ppermute | solution.py:846
  42.0 66.1 %collective-permute-done.1 = bf16[512,1024]{1,0:T(8,128)(2,1)S(1)} collective-permute-done((bf16[512,1024]{1,0:T(8,128)(2,1)S(1)}, bf16[512,1024]{1,0:T(8,128)(2,1)S(1)}, u32[]{:S(2)}, u32[]{:S(2)}) %collective-permute-start.1) | collective-permute-done | bytes 1048608 | tf_op jit(solution)/shard_map/ppermute | solution.py:846
  110.1 14.9 %fusion.38.proj_ref.before_ref = f32[2048,1664]{1,0:T(8,128)} fusion(bf16[1024,1664]{1,0:T(8,128)(2,1)} %all-gather.8.cloned.1.call-done, bf16[512,1024]{1,0:T(8,128)(2,1)} %copy-done.52, bf16[512,1024]{1,0:T(8,128)(2,1)} %copy-done.50, bf16[512,1024]{1,0:T(8,128)(2,1)} %copy-done.48, bf16[512,1024]{1,0:T(8,128)(2,1)S(1)} %fusion.3), kind=kOutput, calls=%fused_computation.44 | convolution fusion | flops 6996099072 | bytes 21233664 | tf_op jit(solution)/shard_map/dot_general | solution.py:836
  124.9 2.1 collective-permute-done.3
  130.2 2.2 collective-permute-start.7
  133.3 37.0 %mixer_forward.1 = (bf16[2048,512]{1,0:T(8,128)(2,1)S(1)}, f32[2048,512]{1,0:T(8,128)}, f32[2048,512]{1,0:T(8,128)}, f32[16,128,512]{2,1,0:T(8,128)}, f32[2048,256]{1,0:T(8,128)S(1)}) custom-call(s32[1]{0:T(128)} %bitcast.rank_ref, f32[2048,1664]{1,0:T(8,128)} %fusion.38.proj_ref.before_ref, f32[2048,128]{1,0:T(8,128)S(1)} %pad.30.aux_ref, ...), custom_call_target="tpu_custom_call" | custom-call | flops 80000000000 | bytes 40894464 | tf_op jit(solution)/shard_map/mixer_forward/pallas_call | solution.py:424
  173.0 5.1 collective-permute-done.7.refs_1_
  179.8 2.8 stacked_after.1
  183.6 1.9 collective-permute-start.6
  185.5 11.5 %collective-permute-done.4 = bf16[512,512]{1,0:T(8,128)(2,1)S(1)} collective-permute-done((bf16[512,512]{1,0:T(8,128)(2,1)S(1)}, bf16[512,512]{1,0:T(8,128)(2,1)S(1)}, u32[]{:S(2)}, u32[]{:S(2)}) %collective-permute-start.4) | collective-permute-done | bytes 524320 | tf_op jit(solution)/shard_map/ppermute | solution.py:855
  197.0 31.3 %collective-permute-done.5 = bf16[512,512]{1,0:T(8,128)(2,1)S(1)} collective-permute-done((bf16[512,512]{1,0:T(8,128)(2,1)S(1)}, bf16[512,512]{1,0:T(8,128)(2,1)S(1)}, u32[]{:S(2)}, u32[]{:S(2)}) %collective-permute-start.5) | collective-permute-done | bytes 524320 | tf_op jit(solution)/shard_map/ppermute | solution.py:855
  228.4 1.6 pad_maximum_fusion.1.gated_ref
  230.0 18.8 %all-gather.14.cloned.1.call-done = bf16[16,128,2816]{2,1,0:T(8,128)(2,1)} async-done(((bf16[2,128,2816]{2,1,0:T(8,128)(2,1)}), bf16[16,128,2816]{2,1,0:T(8,128)(2,1)}) %all-gather.14.cloned.1.call-update) | async-done | bytes 11534352 | tf_op jit(solution)/shard_map/all_gather | solution.py:986
  248.8 59.7 %ffn_block.1 = (bf16[512,1024]{1,0:T(8,128)(2,1)}, f32[512,1024]{1,0:T(8,128)}, bf16[512,2048]{1,0:T(8,128)(2,1)}, f32[8,1024]{1,0:T(8,128)}, bf16[1024,4608]{1,0:T(8,128)(2,1)}, /*index=5*/bf16[1024,7680]{1,0:T(8,128)(2,1)}) custom-call(bf16[512,1024]{1,0:T(8,128)(2,1)} %rows_ref.1, bf16[512,1024]{1,0:T(8,128)(2,1)} %cot_ref.1, ...), custom_call_target="tpu_custom_call" | custom-call | flops 35000000512 | bytes 60000000 | tf_op jit(solution)/shard_map/ffn_block/pallas_call | solution.py:774
  308.4 2.7 fusion.52
  311.1 2.4 collective-permute-start.10
  313.5 1.5 collective-permute-start.11
  315.0 2.3 collective-permute-start.9
  317.4 32.1 %collective-permute-done.10 = bf16[512,512]{1,0:T(8,128)(2,1)S(1)} collective-permute-done((bf16[512,512]{1,0:T(8,128)(2,1)}, bf16[512,512]{1,0:T(8,128)(2,1)S(1)}, u32[]{:S(2)}, u32[]{:S(2)}) %collective-permute-start.10) | collective-permute-done | bytes 524320 | tf_op jit(solution)/shard_map/ppermute | solution.py:855
  350.5 1.9 pad_maximum_fusion.2.grad_ref
  352.9 42.9 %mixer_backward.2 = (bf16[2048,1664]{1,0:T(8,128)(2,1)}, f32[32,1024]{1,0:T(8,128)S(1)}, f32[8,256]{1,0:T(8,128)S(1)}, f32[16,128]{1,0:T(8,128)S(1)}, f32[8,1024]{1,0:T(8,128)S(1)}, /*index=5*/f32[2,128,256]{2,1,0:T(8,128)S(1)}) custom-call(s32[1]{0:T(128)} %bitcast.rank_ref, f32[2048,1664]{1,0:T(8,128)} %fusion.38.proj_ref.before_ref, ...), custom_call_target="tpu_custom_call" | custom-call | flops 160000000000 | bytes 54525952 | tf_op jit(solution)/shard_map/mixer_backward/pallas_call | solution.py:507
  399.2 1.6 copy-done.9
  401.8 26.4 %mixer_backward.3 = (bf16[2048,1664]{1,0:T(8,128)(2,1)}, f32[32,1024]{1,0:T(8,128)S(1)}, f32[8,256]{1,0:T(8,128)S(1)}, f32[16,128]{1,0:T(8,128)S(1)}, f32[8,1024]{1,0:T(8,128)}, /*index=5*/f32[2,128,256]{2,1,0:T(8,128)}) custom-call(s32[1]{0:T(128)} %bitcast.rank_ref, f32[2048,1664]{1,0:T(8,128)} %fusion.38.proj_ref.before_ref, ...), custom_call_target="tpu_custom_call", output_to_operand_aliasing={{0}: (15, {})} | custom-call | flops 160000000000 | bytes 54525952 | tf_op jit(solution)/shard_map/mixer_backward/pallas_call | solution.py:507
  428.2 4.8 fusion.20
  433.0 2.1 collective-permute-start.12
  435.1 3.1 fusion.26
  438.2 11.5 %collective-permute-start.13 = (bf16[512,1024]{1,0:T(8,128)(2,1)}, bf16[512,1024]{1,0:T(8,128)(2,1)S(1)}, u32[]{:S(2)}, u32[]{:S(2)}) collective-permute-start(bf16[512,1024]{1,0:T(8,128)(2,1)} %fusion.26), channel_id=1, source_target_pairs={{0,2},{1,3},{2,0},{3,1},{4,6},{5,7},{6,4},{7,5},{8,10},{9,11},{10,... | collective-permute-start | bytes 3145736 | tf_op jit(solution)/shard_map/ppermute | solution.py:855
  449.7 3.1 fusion.23
  452.8 2.1 collective-permute-start.14
  454.9 3.1 fusion.17
  458.0 9.8 %multiply_reduce_fusion = (f32[1024]{0:T(1024)S(1)}, bf16[1024,1664]{1,0:T(8,128)(2,1)}) fusion(bf16[1024,1664]{1,0:T(8,128)(2,1)S(1)} %copy-done.47, bf16[2048,1664]{1,0:T(8,128)(2,1)S(1)} %copy-done.54, bf16[512,1024]{1,0:T(8,128)(2,1)S(1)} %copy-done.53, bf16[512,1024]{1,0:T(8,128)(2,1)S(1)} %copy-done.51, bf16[512,1024]{1,0:T(8,128)(2,1)S(1)} %copy-done.49, ...), kind=kOutput, calls=%fused_computation | convolution fusion | flops 7002913792 | bytes 17829888 | tf_op jit(solution)/shard_map/dot_general | solution.py:836
  469.2 68.4 %collective-permute-done.13.refs_2_ = bf16[512,1024]{1,0:T(8,128)(2,1)S(1)} collective-permute-done((bf16[512,1024]{1,0:T(8,128)(2,1)}, bf16[512,1024]{1,0:T(8,128)(2,1)S(1)}, u32[]{:S(2)}, u32[]{:S(2)}) %collective-permute-start.13) | collective-permute-done | bytes 1048608 | tf_op jit(solution)/shard_map/ppermute | solution.py:855
  540.7 1.5 collective-permute-start.16
  542.3 2.5 fusion.4
  544.8 2.5 collective-permute-done.16
  548.2 5.5 collective-permute-done.17
  553.7 3.3 collective-permute-start.18
  557.9 3.6 fusion.7
  561.4 6.7 %collective-permute-done.18 = f32[18704]{0:T(1024)S(1)} collective-permute-done((f32[18704]{0:T(1024)S(1)}, f32[18704]{0:T(1024)S(1)}, u32[]{:S(2)}, u32[]{:S(2)}) %collective-permute-start.18) | collective-permute-done | bytes 74848 | tf_op jit(solution)/shard_map/ppermute | solution.py:846
  568.1 17.5 %collective-permute-done.19 = f32[18704]{0:T(1024)S(1)} collective-permute-done((f32[18704]{0:T(1024)S(1)}, f32[18704]{0:T(1024)S(1)}, u32[]{:S(2)}, u32[]{:S(2)}) %collective-permute-start.19) | collective-permute-done | bytes 74848 | tf_op jit(solution)/shard_map/ppermute | solution.py:846
  586.4 1.9 fusion.54
  596.5 1.6 fusion.59
  598.1 1.8 fusion.58
  599.9 2.4 collective-permute-start.21
  603.8 6.5 %collective-permute-done.23 = bf16[128,2816]{1,0:T(8,128)(2,1)S(1)} collective-permute-done((bf16[128,2816]{1,0:T(8,128)(2,1)}, bf16[128,2816]{1,0:T(8,128)(2,1)S(1)}, u32[]{:S(2)}, u32[]{:S(2)}) %collective-permute-start.23) | collective-permute-done | bytes 720928 | tf_op jit(solution)/shard_map/ppermute | solution.py:855
  610.3 1.8 convert_add_fusion
  615.7 2.1 collective-permute-done.22
  (237 shorter events, 46.3 us)
Async XLA Ops:
  7.2 122.3 %copy-start = (f32[4,2048]{1,0:T(4,128)S(1)}, f32[4,2048]{1,0:T(4,128)}, u32[]{:S(2)}) copy-start(f32[4,2048]{1,0:T(4,128)} %param.32) | copy-start | bytes 98308
  7.2 102.8 %all-gather.8.cloned.1.call-start = ((), (), s32[]{:S(2)}) async-start(), calls=%async_computation.3 | async-start | bytes 3833856 | tf_op jit(solution)/shard_map/all_gather | solution.py:934
  11.0 219.0 %all-gather.10.cloned.1.call-start = ((), (), s32[]{:S(2)}) async-start(), calls=%async_computation.7 | async-start | bytes 6488064 | tf_op jit(solution)/shard_map/all_gather | solution.py:949
  12.5 97.5 %copy-start.20 = (bf16[128,2816]{1,0:T(8,128)(2,1)S(1)}, bf16[128,2816]{1,0:T(8,128)(2,1)}, u32[]{:S(2)}) copy-start(bf16[128,2816]{1,0:T(8,128)(2,1)} %fusion.35) | copy-start | bytes 2162692
  12.6 217.4 %all-gather.12.cloned.1.call-start = ((), (), s32[]{:S(2)}) async-start(), calls=%async_computation.8 | async-start | bytes 6488064 | tf_op jit(solution)/shard_map/all_gather | solution.py:978
  12.9 95.2 %copy-start.41 = (f32[512]{0:T(512)}, f32[512]{0:T(512)S(1)}, u32[]{:S(2)}) copy-start(f32[512]{0:T(512)S(1)} %add_rsqrt_fusion) | copy-start | bytes 6148
  13.2 111.7 %copy-start.23 = (bf16[512,1024]{1,0:T(8,128)(2,1)}, bf16[512,1024]{1,0:T(8,128)(2,1)S(1)}, u32[]{:S(2)}) copy-start(bf16[512,1024]{1,0:T(8,128)(2,1)S(1)} %fusion.3) | copy-start | bytes 3145732
  13.3 114.8 %copy-start.30 = (s32[2048]{0:T(1024)S(1)}, s32[2048]{0:T(1024)}, u32[]{:S(2)}) copy-start(s32[2048]{0:T(1024)} %param.22) | copy-start | bytes 24580
  13.3 28.7 %collective-permute-start = (bf16[512,1024]{1,0:T(8,128)(2,1)S(1)}, bf16[512,1024]{1,0:T(8,128)(2,1)S(1)}, u32[]{:S(2)}, u32[]{:S(2)}) collective-permute-start(bf16[512,1024]{1,0:T(8,128)(2,1)S(1)} %fusion.3), channel_id=1, source_target_pairs={{1,0},{2,1},{3,2},{0,3},{5,4},{6,5},{7,6},{4,7},{9,8},{10,9},{11,1... | collective-permute-start | bytes 3145736 | tf_op jit(solution)/shard_map/ppermute | solution.py:846
  18.4 89.7 %collective-permute-start.1 = (bf16[512,1024]{1,0:T(8,128)(2,1)S(1)}, bf16[512,1024]{1,0:T(8,128)(2,1)S(1)}, u32[]{:S(2)}, u32[]{:S(2)}) collective-permute-start(bf16[512,1024]{1,0:T(8,128)(2,1)S(1)} %fusion.3), channel_id=1, source_target_pairs={{2,0},{3,1},{0,2},{1,3},{6,4},{7,5},{4,6},{5,7},{10,8},{11,9},{8,1... | collective-permute-start | bytes 3145736 | tf_op jit(solution)/shard_map/ppermute | solution.py:846
  18.4 89.7 %collective-permute-start.2 = (bf16[512,1024]{1,0:T(8,128)(2,1)S(1)}, bf16[512,1024]{1,0:T(8,128)(2,1)S(1)}, u32[]{:S(2)}, u32[]{:S(2)}) collective-permute-start(bf16[512,1024]{1,0:T(8,128)(2,1)S(1)} %fusion.3), channel_id=1, source_target_pairs={{3,0},{0,1},{1,2},{2,3},{7,4},{4,5},{5,6},{6,7},{11,8},{8,9},{9,10... | collective-permute-start | bytes 3145736 | tf_op jit(solution)/shard_map/ppermute | solution.py:846
  42.0 66.1 %copy-start.48 = (bf16[512,1024]{1,0:T(8,128)(2,1)}, bf16[512,1024]{1,0:T(8,128)(2,1)S(1)}, u32[]{:S(2)}) copy-start(bf16[512,1024]{1,0:T(8,128)(2,1)S(1)} %collective-permute-done) | copy-start | bytes 3145732
  110.1 17.0 %collective-permute-start.3 = (bf16[128,2816]{1,0:T(8,128)(2,1)S(1)}, bf16[128,2816]{1,0:T(8,128)(2,1)S(1)}, u32[]{:S(2)}, u32[]{:S(2)}) collective-permute-start(bf16[128,2816]{1,0:T(8,128)(2,1)S(1)} %copy-done.20), channel_id=1, source_target_pairs={{1,0},{2,1},{3,2},{0,3},{5,4},{6,5},{7,6},{4,7},{9,8},{10,9},{11,1... | collective-permute-start | bytes 2162696 | tf_op jit(solution)/shard_map/ppermute | solution.py:846
  128.0 120.7 %all-gather.14.cloned.1.call-start = ((), (), s32[]{:S(2)}) async-start(), calls=%async_computation.9 | async-start | bytes 12976128 | tf_op jit(solution)/shard_map/all_gather | solution.py:986
  130.2 47.9 %collective-permute-start.7 = (bf16[128,2816]{1,0:T(8,128)(2,1)S(1)}, bf16[128,2816]{1,0:T(8,128)(2,1)S(1)}, u32[]{:S(2)}, u32[]{:S(2)}) collective-permute-start(bf16[128,2816]{1,0:T(8,128)(2,1)S(1)} %copy-done.20), channel_id=1, source_target_pairs={{2,0},{3,1},{0,2},{1,3},{6,4},{7,5},{4,6},{5,7},{10,8},{11,9},{8,1... | collective-permute-start | bytes 2162696 | tf_op jit(solution)/shard_map/ppermute | solution.py:846
  132.3 45.8 %collective-permute-start.8 = (bf16[128,2816]{1,0:T(8,128)(2,1)S(1)}, bf16[128,2816]{1,0:T(8,128)(2,1)S(1)}, u32[]{:S(2)}, u32[]{:S(2)}) collective-permute-start(bf16[128,2816]{1,0:T(8,128)(2,1)S(1)} %copy-done.20), channel_id=1, source_target_pairs={{3,0},{0,1},{1,2},{2,3},{7,4},{4,5},{5,6},{6,7},{11,8},{8,9},{9,10... | collective-permute-start | bytes 2162696 | tf_op jit(solution)/shard_map/ppermute | solution.py:846
  182.7 214.5 %reduce-scatter.4.cloned.1.call-start = ((), (), s32[]{:S(2)}) async-start(), calls=%async_computation.4 | async-start | bytes 10616832 | tf_op jit(solution)/shard_map/reduce_scatter | solution.py:1001
  182.9 14.2 %collective-permute-start.4 = (bf16[512,512]{1,0:T(8,128)(2,1)S(1)}, bf16[512,512]{1,0:T(8,128)(2,1)S(1)}, u32[]{:S(2)}, u32[]{:S(2)}) collective-permute-start(bf16[512,512]{1,0:T(8,128)(2,1)S(1)} %get-tuple-element.161), channel_id=1, source_target_pairs={{0,3},{1,0},{2,1},{3,2},{4,7},{5,4},{6,5},{7,6},{8,11},{9,8},{10,9... | collective-permute-start | bytes 1572872 | tf_op jit(solution)/shard_map/ppermute | solution.py:855
  182.9 45.4 %collective-permute-start.5 = (bf16[512,512]{1,0:T(8,128)(2,1)S(1)}, bf16[512,512]{1,0:T(8,128)(2,1)S(1)}, u32[]{:S(2)}, u32[]{:S(2)}) collective-permute-start(bf16[512,512]{1,0:T(8,128)(2,1)S(1)} %get-tuple-element.160), channel_id=1, source_target_pairs={{0,2},{1,3},{2,0},{3,1},{4,6},{5,7},{6,4},{7,5},{8,10},{9,11},{10,... | collective-permute-start | bytes 1572872 | tf_op jit(solution)/shard_map/ppermute | solution.py:855
  183.6 44.8 %collective-permute-start.6 = (bf16[512,512]{1,0:T(8,128)(2,1)S(1)}, bf16[512,512]{1,0:T(8,128)(2,1)S(1)}, u32[]{:S(2)}, u32[]{:S(2)}) collective-permute-start(bf16[512,512]{1,0:T(8,128)(2,1)S(1)} %get-tuple-element.159), channel_id=1, source_target_pairs={{0,1},{1,2},{2,3},{3,0},{4,5},{5,6},{6,7},{7,4},{8,9},{9,10},{10,1... | collective-permute-start | bytes 1572872 | tf_op jit(solution)/shard_map/ppermute | solution.py:855
  311.1 38.4 %collective-permute-start.10 = (bf16[512,512]{1,0:T(8,128)(2,1)}, bf16[512,512]{1,0:T(8,128)(2,1)S(1)}, u32[]{:S(2)}, u32[]{:S(2)}) collective-permute-start(bf16[512,512]{1,0:T(8,128)(2,1)} %get-tuple-element.156), channel_id=1, source_target_pairs={{0,2},{1,3},{2,0},{3,1},{4,6},{5,7},{6,4},{7,5},{8,10},{9,11},{10,... | collective-permute-start | bytes 1572872 | tf_op jit(solution)/shard_map/ppermute | solution.py:855
  313.5 36.0 %collective-permute-start.11 = (bf16[512,512]{1,0:T(8,128)(2,1)S(1)}, bf16[512,512]{1,0:T(8,128)(2,1)S(1)}, u32[]{:S(2)}, u32[]{:S(2)}) collective-permute-start(bf16[512,512]{1,0:T(8,128)(2,1)S(1)} %get-tuple-element.155), channel_id=1, source_target_pairs={{0,1},{1,2},{2,3},{3,0},{4,5},{5,6},{6,7},{7,4},{8,9},{9,10},{10,1... | collective-permute-start | bytes 1572872 | tf_op jit(solution)/shard_map/ppermute | solution.py:855
  315.0 35.1 %collective-permute-start.9 = (bf16[512,512]{1,0:T(8,128)(2,1)S(1)}, bf16[512,512]{1,0:T(8,128)(2,1)}, u32[]{:S(2)}, u32[]{:S(2)}) collective-permute-start(bf16[512,512]{1,0:T(8,128)(2,1)S(1)} %get-tuple-element.157), channel_id=1, source_target_pairs={{0,3},{1,0},{2,1},{3,2},{4,7},{5,4},{6,5},{7,6},{8,11},{9,8},{10,9... | collective-permute-start | bytes 1572872 | tf_op jit(solution)/shard_map/ppermute | solution.py:855
  317.4 269.0 %reduce-scatter.8.cloned.1.call-start = ((), (), s32[]{:S(2)}) async-start(), calls=%async_computation.6 | async-start | bytes 17694720 | tf_op jit(solution)/shard_map/reduce_scatter | solution.py:1001
  397.1 197.2 %reduce-scatter.6.cloned.1.call-start = ((), (), s32[]{:S(2)}) async-start(), calls=%async_computation.5 | async-start | bytes 3833856 | tf_op jit(solution)/shard_map/reduce_scatter | solution.py:1001
  401.8 26.4 %copy-start.47 = (bf16[1024,1664]{1,0:T(8,128)(2,1)S(1)}, bf16[1024,1664]{1,0:T(8,128)(2,1)}, u32[]{:S(2)}) copy-start(bf16[1024,1664]{1,0:T(8,128)(2,1)} %all-gather.8.cloned.1.call-done) | copy-start | bytes 10223620
  428.2 6.9 %copy-start.54 = (bf16[2048,1664]{1,0:T(8,128)(2,1)S(1)}, bf16[2048,1664]{1,0:T(8,128)(2,1)}, u32[]{:S(2)}) copy-start(bf16[2048,1664]{1,0:T(8,128)(2,1)} %get-tuple-element.61) | copy-start | bytes 20447236
  433.0 36.2 %collective-permute-start.12 = (bf16[512,1024]{1,0:T(8,128)(2,1)}, bf16[512,1024]{1,0:T(8,128)(2,1)S(1)}, u32[]{:S(2)}, u32[]{:S(2)}) collective-permute-start(bf16[512,1024]{1,0:T(8,128)(2,1)} %fusion.20), channel_id=1, source_target_pairs={{0,3},{1,0},{2,1},{3,2},{4,7},{5,4},{6,5},{7,6},{8,11},{9,8},{10,9... | collective-permute-start | bytes 3145736 | tf_op jit(solution)/shard_map/ppermute | solution.py:855
  438.2 99.5 %collective-permute-start.13 = (bf16[512,1024]{1,0:T(8,128)(2,1)}, bf16[512,1024]{1,0:T(8,128)(2,1)S(1)}, u32[]{:S(2)}, u32[]{:S(2)}) collective-permute-start(bf16[512,1024]{1,0:T(8,128)(2,1)} %fusion.26), channel_id=1, source_target_pairs={{0,2},{1,3},{2,0},{3,1},{4,6},{5,7},{6,4},{7,5},{8,10},{9,11},{10,... | collective-permute-start | bytes 3145736 | tf_op jit(solution)/shard_map/ppermute | solution.py:855
  452.8 84.9 %collective-permute-start.14 = (bf16[512,1024]{1,0:T(8,128)(2,1)}, bf16[512,1024]{1,0:T(8,128)(2,1)}, u32[]{:S(2)}, u32[]{:S(2)}) collective-permute-start(bf16[512,1024]{1,0:T(8,128)(2,1)} %fusion.23), channel_id=1, source_target_pairs={{0,1},{1,2},{2,3},{3,0},{4,5},{5,6},{6,7},{7,4},{8,9},{9,10},{10,1... | collective-permute-start | bytes 3145736 | tf_op jit(solution)/shard_map/ppermute | solution.py:855
  457.9 9.8 %copy-start.39 = (f32[1024]{0:T(1024)S(1)}, f32[1024]{0:T(1024)}, u32[]{:S(2)}) copy-start(f32[1024]{0:T(1024)} %param.23) | copy-start | bytes 12292
  468.0 70.7 %copy-start.16 = (bf16[128,4608]{1,0:T(8,128)(2,1)S(1)}, bf16[128,4608]{1,0:T(8,128)(2,1)}, u32[]{:S(2)}) copy-start(bf16[128,4608]{1,0:T(8,128)(2,1)} %reduce-scatter.4.cloned.1.call-done.refs_1_) | copy-start | bytes 3538948
  469.2 68.4 %copy-start.14 = (bf16[512,1024]{1,0:T(8,128)(2,1)}, bf16[512,1024]{1,0:T(8,128)(2,1)S(1)}, u32[]{:S(2)}) copy-start(bf16[512,1024]{1,0:T(8,128)(2,1)S(1)} %collective-permute-done.12.refs_0_.refs_1_) | copy-start | bytes 3145732
  538.7 1.5 collective-permute-start.15
  539.8 64.0 %collective-permute-start.24 = (bf16[128,2304]{1,0:T(8,128)(2,1)}, bf16[128,2304]{1,0:T(8,128)(2,1)}, u32[]{:S(2)}, u32[]{:S(2)}) collective-permute-start(bf16[128,2304]{1,0:T(8,128)(2,1)} %get-tuple-element.174), channel_id=1, source_target_pairs={{0,3},{1,0},{2,1},{3,2},{4,7},{5,4},{6,5},{7,6},{8,11},{9,8},{10,9... | collective-permute-start | bytes 1769480 | tf_op jit(solution)/shard_map/ppermute | solution.py:855
  539.8 64.0 %collective-permute-start.25 = (bf16[128,2304]{1,0:T(8,128)(2,1)}, bf16[128,2304]{1,0:T(8,128)(2,1)}, u32[]{:S(2)}, u32[]{:S(2)}) collective-permute-start(bf16[128,2304]{1,0:T(8,128)(2,1)} %get-tuple-element.175), channel_id=1, source_target_pairs={{0,2},{1,3},{2,0},{3,1},{4,6},{5,7},{6,4},{7,5},{8,10},{9,11},{10,... | collective-permute-start | bytes 1769480 | tf_op jit(solution)/shard_map/ppermute | solution.py:855
  540.7 17.2 %copy-start.15 = (bf16[512,1024]{1,0:T(8,128)(2,1)S(1)}, bf16[512,1024]{1,0:T(8,128)(2,1)}, u32[]{:S(2)}) copy-start(bf16[512,1024]{1,0:T(8,128)(2,1)} %after.5) | copy-start | bytes 3145732
  540.7 17.1 %copy-start.22 = (f32[512,1024]{1,0:T(8,128)S(1)}, f32[512,1024]{1,0:T(8,128)}, u32[]{:S(2)}) copy-start(f32[512,1024]{1,0:T(8,128)} %get-tuple-element.50) | copy-start | bytes 6291460
  540.7 6.5 %collective-permute-start.16 = (f32[18704]{0:T(1024)S(1)}, f32[18704]{0:T(1024)S(1)}, u32[]{:S(2)}, u32[]{:S(2)}) collective-permute-start(f32[18704]{0:T(1024)S(1)} %add.117), channel_id=1, source_target_pairs={{0,8},{4,12},{8,0},{12,4},{16,24},{20,28},{24,16},{28,20},{1,9},{5... | collective-permute-start | bytes 224456 | tf_op jit(solution)/shard_map/ppermute | solution.py:896
  547.3 6.4 %collective-permute-start.17 = (f32[18704]{0:T(1024)S(1)}, f32[18704]{0:T(1024)S(1)}, u32[]{:S(2)}, u32[]{:S(2)}) collective-permute-start(f32[18704]{0:T(1024)S(1)} %add.118), channel_id=1, source_target_pairs={{0,16},{4,20},{8,24},{12,28},{16,0},{20,4},{24,8},{28,12},{1,17},{... | collective-permute-start | bytes 224456 | tf_op jit(solution)/shard_map/ppermute | solution.py:896
  553.7 14.4 %collective-permute-start.18 = (f32[18704]{0:T(1024)S(1)}, f32[18704]{0:T(1024)S(1)}, u32[]{:S(2)}, u32[]{:S(2)}) collective-permute-start(f32[18704]{0:T(1024)S(1)} %add.119), channel_id=1, source_target_pairs={{1,0},{2,1},{3,2},{0,3},{5,4},{6,5},{7,6},{4,7},{9,8},{10,9},{11,1... | collective-permute-start | bytes 224456 | tf_op jit(solution)/shard_map/ppermute | solution.py:846
  557.0 28.6 %collective-permute-start.19 = (f32[18704]{0:T(1024)S(1)}, f32[18704]{0:T(1024)S(1)}, u32[]{:S(2)}, u32[]{:S(2)}) collective-permute-start(f32[18704]{0:T(1024)S(1)} %add.119), channel_id=1, source_target_pairs={{2,0},{3,1},{0,2},{1,3},{6,4},{7,5},{4,6},{5,7},{10,8},{11,9},{8,1... | collective-permute-start | bytes 224456 | tf_op jit(solution)/shard_map/ppermute | solution.py:846
  557.0 28.6 %collective-permute-start.20 = (f32[18704]{0:T(1024)S(1)}, f32[18704]{0:T(1024)S(1)}, u32[]{:S(2)}, u32[]{:S(2)}) collective-permute-start(f32[18704]{0:T(1024)S(1)} %add.119), channel_id=1, source_target_pairs={{3,0},{0,1},{1,2},{2,3},{7,4},{4,5},{5,6},{6,7},{11,8},{8,9},{9,10... | collective-permute-start | bytes 224456 | tf_op jit(solution)/shard_map/ppermute | solution.py:846
  586.4 23.9 %copy-start.21 = (bf16[128,7680]{1,0:T(8,128)(2,1)S(1)}, bf16[128,7680]{1,0:T(8,128)(2,1)}, u32[]{:S(2)}) copy-start(bf16[128,7680]{1,0:T(8,128)(2,1)} %reduce-scatter.8.cloned.1.call-done) | copy-start | bytes 5898244
  589.3 21.1 %collective-permute-start.23 = (bf16[128,2816]{1,0:T(8,128)(2,1)}, bf16[128,2816]{1,0:T(8,128)(2,1)S(1)}, u32[]{:S(2)}, u32[]{:S(2)}) collective-permute-start(bf16[128,2816]{1,0:T(8,128)(2,1)} %pad_maximum_fusion.3), channel_id=1, source_target_pairs={{0,1},{1,2},{2,3},{3,0},{4,5},{5,6},{6,7},{7,4},{8,9},{9,10},{10,1... | collective-permute-start | bytes 2162696 | tf_op jit(solution)/shard_map/ppermute | solution.py:855
  599.9 15.8 %collective-permute-start.21 = (bf16[128,512]{1,0:T(8,128)(2,1)}, bf16[128,512]{1,0:T(8,128)(2,1)}, u32[]{:S(2)}, u32[]{:S(2)}) collective-permute-start(bf16[128,512]{1,0:T(8,128)(2,1)} %get-tuple-element.164), channel_id=1, source_target_pairs={{0,3},{1,0},{2,1},{3,2},{4,7},{5,4},{6,5},{7,6},{8,11},{9,8},{10,9... | collective-permute-start | bytes 393224 | tf_op jit(solution)/shard_map/ppermute | solution.py:855
  602.4 15.4 %collective-permute-start.22 = (bf16[128,512]{1,0:T(8,128)(2,1)}, bf16[128,512]{1,0:T(8,128)(2,1)}, u32[]{:S(2)}, u32[]{:S(2)}) collective-permute-start(bf16[128,512]{1,0:T(8,128)(2,1)} %get-tuple-element.163), channel_id=1, source_target_pairs={{0,2},{1,3},{2,0},{3,1},{4,6},{5,7},{6,4},{7,5},{8,10},{9,11},{10,... | collective-permute-start | bytes 393224 | tf_op jit(solution)/shard_map/ppermute | solution.py:855
  612.9 6.8 %copy-start.1 = (f32[4,2048]{1,0:T(4,128)S(1)}, f32[4,2048]{1,0:T(4,128)}, u32[]{:S(2)}) copy-start(f32[4,2048]{1,0:T(4,128)} %param.32) | copy-start | bytes 98308
  (41 other events, 87.2 us)
Sparse Core Ops, SparseCore 0:
  11.1 36.1 all-gather.7
  49.7 43.3 all-gather.9
  128.1 43.0 all-gather.11
  182.8 65.9 all-gather.13
  317.5 73.7 reduce-scatter.3
  397.3 118.3 reduce-scatter.7
  519.1 49.1 reduce-scatter.5
